TPU v7x, 32 devices: a whole 2x2x4 slice. The times are simulated.
32 devices in a mesh: dp: 8 (over z, x), blk: 4 (over y, core).
Axes of the slice: x: 2, y: 2, z: 4, core: 2. Of those that a mesh axis runs over, the one named last changes fastest.
Arguments:
- block_input: bfloat16 [2, 8, 1024, 960], P(None, 'dp', 'blk'), may hold values from -6 to 6
- cotangent: bfloat16 [2, 8, 1024, 960], P(None, 'dp', 'blk'), may hold values from -6 to 6
- seq_lengths: int32 [2, 8], P(None, 'dp'), may hold values from 512 to 1024, as said below
- routes_two: int32 [2, 8, 256], P(None, 'dp'), may hold values from 0 to 1023, as said below
- routes_three: int32 [2, 8, 128], P(None, 'dp'), may hold values from 0 to 1023, as said below
- query_weight: bfloat16 [960, 960], P('dp'), may hold values from -0.1875 to 0.1875
- key_weight: bfloat16 [960, 320], P('dp'), may hold values from -0.1875 to 0.1875
- value_weight: bfloat16 [960, 320], P('dp'), may hold values from -0.1875 to 0.1875
- output_weight: bfloat16 [960, 960], P('dp'), may hold values from -1.5 to 1.5
- gate_weight: bfloat16 [960, 2560], P('dp'), may hold values from -0.1875 to 0.1875
- up_weight: bfloat16 [960, 2560], P('dp'), may hold values from -0.1875 to 0.1875
- down_weight: bfloat16 [2560, 960], P('dp'), may hold values from -0.125 to 0.125
- first_gain: bfloat16 [960], P('dp'), may hold values from 0.099609375 to 1.8984375
- second_gain: bfloat16 [960], P('dp'), may hold values from 0.099609375 to 1.8984375
- router_weight: bfloat16 [960, 3], P('dp'), may hold values from -0.125 to 0.125
Outputs:
- block_output: bfloat16 [2, 8, 1024, 960], P(None, 'dp', 'blk')
- input_grad: float32 [2, 8, 1024, 960], P(None, 'dp', 'blk')
- grad_query: float32 [960, 960], P('dp')
- grad_key: float32 [960, 320], P('dp')
- grad_value: float32 [960, 320], P('dp')
- grad_output: float32 [960, 960], P('dp')
- grad_gate: float32 [960, 2560], P('dp')
- grad_up: float32 [960, 2560], P('dp')
- grad_down: float32 [2560, 960], P('dp')
- grad_first: float32 [960], P('dp')
- grad_second: float32 [960], P('dp')
- grad_router: float32 [960, 3], P('dp')
Inputs may be any that keep to these rules, and one draw needn't show every extreme that they name: `seq_lengths`: in each micro-batch, each group of 1 sequence holds one sequence (drawn from the seed) longer than 768; some sequence has length exactly 1024. `routes_two`: for each sequence: 256 distinct positions below its length, in increasing order; at most 128 of them lie in any aligned block of 256 positions, and some block of every sequence holds exactly 128. `routes_three`: for each sequence: 128 distinct positions taken from its routes_two, in increasing order; at most 64 of them lie in any aligned block of 256 positions, and some block of every sequence holds exactly 64.
All inputs are finite; a program needn't handle non-finite values.
Results may differ from a plain program's by a relative error of at most 0.033.
Values may be sent and summed in bfloat16 or wider, within the bound.
A program may use at most 192 MiB of HBM per device.

v0:
```python
import math

import jax
import jax.numpy as jnp
from jax import lax
from jax.sharding import PartitionSpec as P

HEADS = 15
KV_HEADS = 5
HEAD_DIM = 64
RECUR = 3


eps = 1e-05
rope_base = 10000.0
masked_fill = -1e30


def as_sent(shard):

    def short(part):
        return part.astype(jnp.bfloat16) if part.dtype == jnp.float32 else part

    return jax.tree.map(short, shard)


def rotate(values, cosine, sine_part):
    half_dim = values.shape[-1] // 2
    turned = jnp.concatenate([-values[..., half_dim:], values[..., :half_dim]], axis=-1)
    return values * cosine + turned * sine_part


def rotate_back(gradient, cosine, sine_part):
    half_dim = gradient.shape[-1] // 2
    scaled = gradient * sine_part
    turned = jnp.concatenate([scaled[..., half_dim:], -scaled[..., :half_dim]], axis=-1)
    return gradient * cosine + turned


def angles(positions):
    frequency = rope_base ** (-(jnp.arange(HEAD_DIM // 2, dtype=jnp.float32) * 2.0) / HEAD_DIM)
    frequency = jnp.concatenate([frequency, frequency])
    phases = positions.astype(jnp.float32)[..., None] * frequency
    return (jnp.cos(phases)[..., None, :], jnp.sin(phases)[..., None, :])


def routed_slots(routes, blocks, block_len, slot_count):
    total_routes = routes.shape[1]
    block_starts = jnp.arange(blocks, dtype=jnp.int32) * block_len
    before = jnp.sum((routes[:, None, :] < block_starts[None, :, None]).astype(jnp.int32), axis=2)
    first_pick = jnp.minimum(before, total_routes - slot_count)
    pick_index = first_pick[:, :, None] + jnp.arange(slot_count, dtype=jnp.int32)[None, None, :]
    found_places = jnp.take_along_axis(
        routes, pick_index.reshape(routes.shape[0], blocks * slot_count), axis=1
    )
    found_places = found_places.reshape(routes.shape[0], blocks, slot_count)
    inside = (found_places >= block_starts[None, :, None]) & (
        found_places < block_starts[None, :, None] + block_len
    )
    return jnp.where(inside, found_places, -1).reshape(routes.shape[0], blocks * slot_count)


def pick_rows(block_vals, index_vals):
    return block_vals[index_vals]


def place_rows(block_vals, index_vals, new_vals):
    return block_vals.at[index_vals].set(new_vals, mode="drop")


def attention_mask(query_places, key_places):
    key_side = key_places[:, None, None, None, :]
    return (key_side >= 0) & (key_side <= query_places[:, None, None, :, None])


def block_forward(tokens, positions, all_slots, gathered, recursion):
    (
        query_projection,
        key_projection,
        value_projection,
        output_projection,
        gate_projection,
        up_projection,
        down_projection,
        gain_one,
        gain_two,
        router_matrix,
    ) = gathered
    seq_count, slot_count, model_width = tokens.shape
    groups = HEADS // KV_HEADS
    attn_scale = 1.0 / math.sqrt(HEAD_DIM)
    first_scale = lax.rsqrt(jnp.mean(tokens * tokens, axis=-1, keepdims=True) + eps)
    normalized_input = (tokens * first_scale * gain_one.astype(jnp.float32)).astype(jnp.bfloat16)
    cosine, sine_part = angles(positions)
    query_unrotated = jnp.dot(
        normalized_input, query_projection, preferred_element_type=jnp.float32
    )
    queries = rotate(
        query_unrotated.reshape(seq_count, slot_count, HEADS, HEAD_DIM), cosine, sine_part
    )
    queries = queries.astype(jnp.bfloat16).reshape(
        seq_count, slot_count, KV_HEADS, groups, HEAD_DIM
    )
    key_unrotated = jnp.dot(normalized_input, key_projection, preferred_element_type=jnp.float32)
    keyset = rotate(
        key_unrotated.reshape(seq_count, slot_count, KV_HEADS, HEAD_DIM), cosine, sine_part
    )
    keyset = keyset.astype(jnp.bfloat16).reshape(seq_count, slot_count, KV_HEADS * HEAD_DIM)
    value_collection = jnp.dot(
        normalized_input, value_projection, preferred_element_type=jnp.float32
    ).astype(jnp.bfloat16)
    key_all, value_all = (
        lax.all_gather(keyset, "blk", axis=1, tiled=True),
        lax.all_gather(value_collection, "blk", axis=1, tiled=True),
    )
    key_all = key_all.reshape(seq_count, -1, KV_HEADS, HEAD_DIM)
    value_all = value_all.reshape(seq_count, -1, KV_HEADS, HEAD_DIM)
    allowed = attention_mask(positions, all_slots)
    scores = (
        jnp.einsum("sqgcd,skgd->sgcqk", queries, key_all, preferred_element_type=jnp.float32)
        * attn_scale
    )
    scores = jnp.where(allowed, scores, masked_fill)
    row_max = jnp.max(scores, axis=-1)
    raised = jnp.where(allowed, jnp.exp(scores - row_max[..., None]), 0.0)
    total = jnp.sum(raised, axis=-1)
    safe_sum = jnp.where(total > 0, total, 1.0)
    chances = (raised / safe_sum[..., None]).astype(jnp.bfloat16)
    attended = jnp.einsum(
        "sgcqk,skgd->sqgcd", chances, value_all, preferred_element_type=jnp.float32
    )
    attended = attended.reshape(seq_count, slot_count, HEADS * HEAD_DIM)
    summary = row_max + jnp.log(safe_sum)
    attention_reduced = attended.astype(jnp.bfloat16)
    branch_result = jnp.dot(
        attention_reduced, output_projection, preferred_element_type=jnp.float32
    )
    middle = tokens + branch_result
    second_scale = lax.rsqrt(jnp.mean(middle * middle, axis=-1, keepdims=True) + eps)
    normalized_second = (middle * second_scale * gain_two.astype(jnp.float32)).astype(jnp.bfloat16)
    gate_preactivation = jnp.dot(
        normalized_second, gate_projection, preferred_element_type=jnp.float32
    )
    up_preactivation = jnp.dot(normalized_second, up_projection, preferred_element_type=jnp.float32)
    hidden_activation = (jax.nn.silu(gate_preactivation) * up_preactivation).astype(jnp.bfloat16)
    feedforward_output = jnp.dot(
        hidden_activation, down_projection, preferred_element_type=jnp.float32
    )
    router_gate = jax.nn.sigmoid(
        jnp.sum(tokens * router_matrix[:, recursion].astype(jnp.float32), axis=-1)
    )
    result = tokens + router_gate[..., None] * (branch_result + feedforward_output)
    stored = (
        tokens,
        positions,
        cosine,
        sine_part,
        first_scale,
        normalized_input,
        queries,
        keyset,
        value_collection,
        attention_reduced,
        summary,
        branch_result,
        middle,
        second_scale,
        normalized_second,
        gate_preactivation,
        up_preactivation,
        hidden_activation,
        feedforward_output,
        router_gate,
    )
    return (result, stored)


def block_backward(incoming, stored, gathered, recursion, all_slots):
    (
        query_projection,
        key_projection,
        value_projection,
        output_projection,
        gate_projection,
        up_projection,
        down_projection,
        gain_one,
        gain_two,
        router_matrix,
    ) = gathered
    (
        tokens,
        positions,
        cosine,
        sine_part,
        first_scale,
        normalized_input,
        queries,
        keyset,
        value_collection,
        attention_reduced,
        summary,
        branch_result,
        middle,
        second_scale,
        normalized_second,
        gate_preactivation,
        up_preactivation,
        hidden_activation,
        feedforward_output,
        router_gate,
    ) = stored
    seq_count, slot_count, model_width = tokens.shape
    groups = HEADS // KV_HEADS
    attn_scale = 1.0 / math.sqrt(HEAD_DIM)
    router_column = router_matrix[:, recursion].astype(jnp.float32)
    branches = branch_result + feedforward_output
    gate_grad = jnp.sum(incoming * branches, axis=-1)
    logit_grad = gate_grad * router_gate * (1.0 - router_gate)
    token_grad = incoming + logit_grad[..., None] * router_column
    router_grad = jnp.einsum("sr,srd->d", logit_grad, tokens, precision=lax.Precision.HIGHEST)
    scaled_grad = router_gate[..., None] * incoming
    feed_grad = scaled_grad.astype(jnp.bfloat16)
    grad_down = jnp.einsum(
        "srf,srd->fd", hidden_activation, feed_grad, preferred_element_type=jnp.float32
    )
    hidden_grad = jnp.einsum(
        "srd,fd->srf", feed_grad, down_projection, preferred_element_type=jnp.float32
    )
    gate_sigmoid = jax.nn.sigmoid(gate_preactivation)
    up_grad = (hidden_grad * gate_preactivation * gate_sigmoid).astype(jnp.bfloat16)
    gate_pre_grad = (
        hidden_grad
        * up_preactivation
        * gate_sigmoid
        * (1.0 + gate_preactivation * (1.0 - gate_sigmoid))
    ).astype(jnp.bfloat16)
    grad_gate = jnp.einsum(
        "srd,srf->df", normalized_second, gate_pre_grad, preferred_element_type=jnp.float32
    )
    grad_up = jnp.einsum(
        "srd,srf->df", normalized_second, up_grad, preferred_element_type=jnp.float32
    )
    normed_two_grad = jnp.einsum(
        "srf,df->srd", gate_pre_grad, gate_projection, preferred_element_type=jnp.float32
    ) + jnp.einsum("srf,df->srd", up_grad, up_projection, preferred_element_type=jnp.float32)
    grad_second = jnp.sum(normed_two_grad * middle * second_scale, axis=(0, 1))
    shaped = normed_two_grad * gain_two.astype(jnp.float32)
    middle_grad = second_scale * shaped - second_scale**3 * middle * jnp.mean(
        shaped * middle, axis=-1, keepdims=True
    )
    token_grad = token_grad + middle_grad
    branch_grad = (scaled_grad + middle_grad).astype(jnp.bfloat16)
    grad_output = jnp.einsum(
        "srq,srd->qd", attention_reduced, branch_grad, preferred_element_type=jnp.float32
    )
    attn_grad = jnp.einsum(
        "srd,qd->srq", branch_grad, output_projection, preferred_element_type=jnp.float32
    )
    attn_grad = attn_grad.astype(jnp.bfloat16).reshape(
        seq_count, slot_count, KV_HEADS, groups, HEAD_DIM
    )
    key_all, value_all = (
        lax.all_gather(as_sent(keyset), "blk", axis=1, tiled=True).astype(keyset.dtype),
        lax.all_gather(as_sent(value_collection), "blk", axis=1, tiled=True).astype(
            value_collection.dtype
        ),
    )
    key_all = key_all.reshape(seq_count, -1, KV_HEADS, HEAD_DIM)
    value_all = value_all.reshape(seq_count, -1, KV_HEADS, HEAD_DIM)
    allowed = attention_mask(positions, all_slots)
    scores = (
        jnp.einsum("sqgcd,skgd->sgcqk", queries, key_all, preferred_element_type=jnp.float32)
        * attn_scale
    )
    chances = jnp.where(allowed, jnp.exp(scores - summary[..., None]), 0.0)
    chance_grad = jnp.einsum(
        "sqgcd,skgd->sgcqk", attn_grad, value_all, preferred_element_type=jnp.float32
    )
    row_dots = jnp.sum(chances * chance_grad, axis=-1)
    score_grad = (chances * (chance_grad - row_dots[..., None])).astype(jnp.bfloat16)
    query_grad = (
        jnp.einsum("sgcqk,skgd->sqgcd", score_grad, key_all, preferred_element_type=jnp.float32)
        * attn_scale
    )
    key_grad_all = (
        jnp.einsum("sgcqk,sqgcd->skgd", score_grad, queries, preferred_element_type=jnp.float32)
        * attn_scale
    )
    value_grad_all = jnp.einsum(
        "sgcqk,sqgcd->skgd",
        chances.astype(jnp.bfloat16),
        attn_grad,
        preferred_element_type=jnp.float32,
    )
    key_grad, value_grad = (
        lax.psum_scatter(
            key_grad_all.reshape(seq_count, -1, KV_HEADS * HEAD_DIM).astype(jnp.bfloat16),
            "blk",
            scatter_dimension=1,
            tiled=True,
        ).astype(jnp.float32),
        lax.psum_scatter(
            value_grad_all.reshape(seq_count, -1, KV_HEADS * HEAD_DIM).astype(jnp.bfloat16),
            "blk",
            scatter_dimension=1,
            tiled=True,
        ).astype(jnp.float32),
    )
    query_raw_grad = rotate_back(
        query_grad.reshape(seq_count, slot_count, HEADS, HEAD_DIM), cosine, sine_part
    )
    query_raw_grad = query_raw_grad.astype(jnp.bfloat16).reshape(
        seq_count, slot_count, HEADS * HEAD_DIM
    )
    key_raw_grad = rotate_back(
        key_grad.reshape(seq_count, slot_count, KV_HEADS, HEAD_DIM), cosine, sine_part
    )
    key_raw_grad = key_raw_grad.astype(jnp.bfloat16).reshape(
        seq_count, slot_count, KV_HEADS * HEAD_DIM
    )
    value_low = value_grad.astype(jnp.bfloat16)
    grad_query = jnp.einsum(
        "srd,srq->dq", normalized_input, query_raw_grad, preferred_element_type=jnp.float32
    )
    grad_key = jnp.einsum(
        "srd,srk->dk", normalized_input, key_raw_grad, preferred_element_type=jnp.float32
    )
    grad_value = jnp.einsum(
        "srd,srk->dk", normalized_input, value_low, preferred_element_type=jnp.float32
    )
    normed_grad = (
        jnp.einsum(
            "srq,dq->srd", query_raw_grad, query_projection, preferred_element_type=jnp.float32
        )
        + jnp.einsum(
            "srk,dk->srd", key_raw_grad, key_projection, preferred_element_type=jnp.float32
        )
        + jnp.einsum("srk,dk->srd", value_low, value_projection, preferred_element_type=jnp.float32)
    )
    grad_first = jnp.sum(normed_grad * tokens * first_scale, axis=(0, 1))
    shaped_one = normed_grad * gain_one.astype(jnp.float32)
    token_grad = (
        token_grad
        + first_scale * shaped_one
        - first_scale**3 * tokens * jnp.mean(shaped_one * tokens, axis=-1, keepdims=True)
    )
    matrices = (
        grad_query,
        grad_key,
        grad_value,
        grad_output,
        grad_gate,
        grad_up,
        grad_down,
        grad_first,
        grad_second,
    )
    return (token_grad, matrices, router_grad)


def per_device(
    block_input,
    cotangent,
    seq_lengths,
    routes_two,
    routes_three,
    query_weight,
    key_weight,
    value_weight,
    output_weight,
    gate_weight,
    up_weight,
    down_weight,
    first_gain,
    second_gain,
    router_weight,
):
    micro_count, seq_count, block_len, model_width = block_input.shape
    blocks = lax.axis_size("blk")
    device = lax.axis_index("blk")
    capacity = (block_len, block_len // 2, block_len // 4)
    all_places = jnp.arange(block_len * blocks, dtype=jnp.int32)
    shard_weights = (
        query_weight,
        key_weight,
        value_weight,
        output_weight,
        gate_weight,
        up_weight,
        down_weight,
        first_gain,
        second_gain,
        router_weight,
    )

    def one_micro(collected, inputs):
        micro_input, micro_cotangent, lengths_now, routes_now_two, routes_now_three = inputs
        gathered = (
            lax.all_gather(query_weight, "dp", axis=0, tiled=True),
            lax.all_gather(key_weight, "dp", axis=0, tiled=True),
            lax.all_gather(value_weight, "dp", axis=0, tiled=True),
            lax.all_gather(output_weight, "dp", axis=0, tiled=True),
            lax.all_gather(gate_weight, "dp", axis=0, tiled=True),
            lax.all_gather(up_weight, "dp", axis=0, tiled=True),
            lax.all_gather(down_weight, "dp", axis=0, tiled=True),
            lax.all_gather(first_gain, "dp", axis=0, tiled=True),
            lax.all_gather(second_gain, "dp", axis=0, tiled=True),
            lax.all_gather(router_weight, "dp", axis=0, tiled=True),
        )
        slot_sets = (
            jnp.where(all_places[None, :] < lengths_now[:, None], all_places[None, :], -1),
            routed_slots(routes_now_two, blocks, block_len, capacity[1]),
            routed_slots(routes_now_three, blocks, block_len, capacity[2]),
        )
        current = micro_input.astype(jnp.float32)
        records = []
        for recursion in range(RECUR):
            slot_count = capacity[recursion]
            own_slots = lax.dynamic_slice_in_dim(
                slot_sets[recursion], device * slot_count, slot_count, 1
            )
            present = own_slots >= 0
            local_index = jnp.where(present, own_slots - device * block_len, 0)
            if recursion == 0:
                tokens = current
            else:
                tokens = jax.vmap(pick_rows)(current, local_index)
            result, stored = block_forward(
                tokens, own_slots, slot_sets[recursion], gathered, recursion
            )
            target = jnp.where(present, local_index, block_len)
            current = jax.vmap(place_rows)(current, target, result)
            records.append((stored, local_index, target, present))
        upstream = micro_cotangent.astype(jnp.float32)
        matrix_sums = None
        router_columns = [None] * RECUR
        for recursion in range(RECUR - 1, -1, -1):
            stored, local_index, target, present = records[recursion]
            incoming = jnp.where(
                present[..., None], jax.vmap(pick_rows)(upstream, local_index), 0.0
            )
            token_grad, matrices, router_grad = block_backward(
                incoming, stored, gathered, recursion, slot_sets[recursion]
            )
            upstream = jax.vmap(place_rows)(upstream, target, token_grad)
            router_columns[recursion] = router_grad
            if matrix_sums is None:
                matrix_sums = matrices
            else:
                matrix_sums = tuple(
                    (earlier + latest for earlier, latest in zip(matrix_sums, matrices))
                )
        full_grads = matrix_sums + (jnp.stack(router_columns, axis=1),)
        shares = (
            lax.psum_scatter(
                full_grads[0].astype(jnp.bfloat16), "dp", scatter_dimension=0, tiled=True
            ).astype(jnp.float32),
            lax.psum_scatter(
                full_grads[1].astype(jnp.bfloat16), "dp", scatter_dimension=0, tiled=True
            ).astype(jnp.float32),
            lax.psum_scatter(
                full_grads[2].astype(jnp.bfloat16), "dp", scatter_dimension=0, tiled=True
            ).astype(jnp.float32),
            lax.psum_scatter(
                full_grads[3].astype(jnp.bfloat16), "dp", scatter_dimension=0, tiled=True
            ).astype(jnp.float32),
            lax.psum_scatter(
                full_grads[4].astype(jnp.bfloat16), "dp", scatter_dimension=0, tiled=True
            ).astype(jnp.float32),
            lax.psum_scatter(
                full_grads[5].astype(jnp.bfloat16), "dp", scatter_dimension=0, tiled=True
            ).astype(jnp.float32),
            lax.psum_scatter(
                full_grads[6].astype(jnp.bfloat16), "dp", scatter_dimension=0, tiled=True
            ).astype(jnp.float32),
            lax.psum_scatter(
                full_grads[7].astype(jnp.bfloat16), "dp", scatter_dimension=0, tiled=True
            ).astype(jnp.float32),
            lax.psum_scatter(
                full_grads[8].astype(jnp.bfloat16), "dp", scatter_dimension=0, tiled=True
            ).astype(jnp.float32),
            lax.psum_scatter(
                full_grads[9].astype(jnp.bfloat16), "dp", scatter_dimension=0, tiled=True
            ).astype(jnp.float32),
        )
        collected = tuple((earlier + latest for earlier, latest in zip(collected, shares)))
        return (collected, (current.astype(jnp.bfloat16), upstream))

    start_grads = tuple((jnp.zeros(matrix.shape, jnp.float32) for matrix in shard_weights))
    collected, (outputs, input_grads) = lax.scan(
        one_micro, start_grads, (block_input, cotangent, seq_lengths, routes_two, routes_three)
    )
    collected = (
        lax.psum(collected[0].astype(jnp.bfloat16), "blk").astype(jnp.float32),
        lax.psum(collected[1].astype(jnp.bfloat16), "blk").astype(jnp.float32),
        lax.psum(collected[2].astype(jnp.bfloat16), "blk").astype(jnp.float32),
        lax.psum(collected[3].astype(jnp.bfloat16), "blk").astype(jnp.float32),
        lax.psum(collected[4].astype(jnp.bfloat16), "blk").astype(jnp.float32),
        lax.psum(collected[5].astype(jnp.bfloat16), "blk").astype(jnp.float32),
        lax.psum(collected[6].astype(jnp.bfloat16), "blk").astype(jnp.float32),
        lax.psum(collected[7].astype(jnp.bfloat16), "blk").astype(jnp.float32),
        lax.psum(collected[8].astype(jnp.bfloat16), "blk").astype(jnp.float32),
        lax.psum(collected[9].astype(jnp.bfloat16), "blk").astype(jnp.float32),
    )
    return (
        outputs,
        input_grads,
        collected[0],
        collected[1],
        collected[2],
        collected[3],
        collected[4],
        collected[5],
        collected[6],
        collected[7],
        collected[8],
        collected[9],
    )


def solution(mesh):
    in_specs = (
        P(None, "dp", "blk", None),
        P(None, "dp", "blk", None),
        P(None, "dp"),
        P(None, "dp", None),
        P(None, "dp", None),
        P("dp", None),
        P("dp", None),
        P("dp", None),
        P("dp", None),
        P("dp", None),
        P("dp", None),
        P("dp", None),
        P("dp"),
        P("dp"),
        P("dp", None),
    )
    out_specs = (
        P(None, "dp", "blk", None),
        P(None, "dp", "blk", None),
        P("dp", None),
        P("dp", None),
        P("dp", None),
        P("dp", None),
        P("dp", None),
        P("dp", None),
        P("dp", None),
        P("dp"),
        P("dp"),
        P("dp", None),
    )
    return jax.shard_map(
        per_device, mesh=mesh, in_specs=in_specs, out_specs=out_specs, check_vma=False
    )
```

profile of v0, /device:TPU:0, one launch (start us, length us, event | category | flops | bytes accessed | tf_op | source)
XLA Modules:
  0.0 2563.5 jit_solution(9383139565556632671)
XLA Ops:
  8.1 2471.1 %while.36 = (s32[]{:T(128)}, f32[120,960]{1,0:T(8,128)}, f32[120,320]{0,1:T(8,128)}, f32[120,320]{0,1:T(8,128)}, f32[120,960]{1,0:T(8,128)}, /*index=5*/f32[120,...) while((s32[]{:T(128)}, f32[120,960]{1,0:T(8,128)}, ...), condition=%wide.region_58.59_spmd.clone.clone, body=%wide.region_0.58_spmd.clone.clone.sunk | while | flops 30645301248 | bytes 1381716480 | solution.py:491
  24.6 22.3 all-gather.28
  49.6 17.5 all-reduce.17
  67.1 32.7 %all-gather.27 = bf16[8,120,320]{1,2,0:T(8,128)(2,1)S(1)} all-gather(bf16[1,120,320]{1,2,0:T(8,128)(2,1)S(1)} %bitcast.1553), channel_id=1, replica_groups=mesh['dp'=8,'blk'=4] {'dp'}, dimensions={0}, use_global_device_ids=true | all-gather | bytes 691200 | tf_op jit(solution)/shard_map/while/body/eval_jaxpr/all_gather | solution.py:401
  110.1 33.2 %all-gather.30 = bf16[8,120,320]{1,2,0:T(8,128)(2,1)S(1)} all-gather(bf16[1,120,320]{1,2,0:T(8,128)(2,1)S(1)} %bitcast.1552), channel_id=1, replica_groups=mesh['dp'=8,'blk'=4] {'dp'}, dimensions={0}, use_global_device_ids=true | all-gather | bytes 691200 | tf_op jit(solution)/shard_map/while/body/eval_jaxpr/all_gather | solution.py:402
  215.9 68.2 %all-gather.48.cloned.1.call-done = bf16[960,2560]{1,0:T(8,128)(2,1)} async-done(((bf16[120,2560]{1,0:T(8,128)(2,1)}), bf16[960,2560]{1,0:T(8,128)(2,1)}) %all-gather.48.cloned.1.call-update) | async-done | bytes 4915216 | tf_op jit(solution)/shard_map/while/body/eval_jaxpr/all_gather | solution.py:405
  291.2 79.7 %all-gather.50.cloned.1.call-done = bf16[2560,960]{1,0:T(8,128)(2,1)} async-done(((bf16[320,960]{1,0:T(8,128)(2,1)}), bf16[2560,960]{1,0:T(8,128)(2,1)}) %all-gather.50.cloned.1.call-update) | async-done | bytes 4915216 | tf_op jit(solution)/shard_map/while/body/eval_jaxpr/all_gather | solution.py:406
  510.2 21.3 reduce-scatter.31.cloned.1.call-done
  590.2 15.3 reduce-scatter.35.cloned.1.call-done
  684.9 20.4 reduce-scatter.43.cloned.1.call-done
  776.4 37.7 %all-reduce.19 = (bf16[960]{0:T(1024)(128)(2,1)S(1)}, bf16[960]{0:T(1024)(128)(2,1)S(1)}, bf16[960,3]{0,1:T(4,128)(2,1)S(1)}) all-reduce(bf16[960]{0:T(1024)(128)(2,1)S(1)} %add_convert_fusion.27, bf16[960]{0:T(1024)(128)(2,1)S(1)} %copy-done.172, ...), channel_id=21, replica_groups=mesh['dp'=8,'blk'=4] {'dp'}, use_global_device_ids=true, to_apply=%region_48.48.clone | all-reduce | flops 4800 | bytes 19200 | tf_op jit(solution)/shard_map/while
  817.1 45.8 %reduce-scatter.45.cloned.1.call-done = bf16[120,960]{1,0:T(8,128)(2,1)} async-done(((bf16[960,960]{1,0:T(8,128)(2,1)}), bf16[120,960]{1,0:T(8,128)(2,1)}) %reduce-scatter.45.cloned.1.call-update) | async-done | bytes 230416 | tf_op jit(solution)/shard_map/while/body/eval_jaxpr/reduce_scatter | solution.py:465
  864.7 67.7 %reduce-scatter.39.cloned.1.call-done = bf16[120,960]{1,0:T(8,128)(2,1)} async-done(((bf16[960,960]{1,0:T(8,128)(2,1)}), bf16[120,960]{1,0:T(8,128)(2,1)}) %reduce-scatter.39.cloned.1.call-update) | async-done | bytes 230416 | tf_op jit(solution)/shard_map/while/body/eval_jaxpr/reduce_scatter | solution.py:456
  933.5 103.8 %reduce-scatter.51.cloned.1.call-done = bf16[320,960]{1,0:T(8,128)(2,1)} async-done(((bf16[2560,960]{1,0:T(8,128)(2,1)}), bf16[320,960]{1,0:T(8,128)(2,1)}) %reduce-scatter.51.cloned.1.call-update) | async-done | bytes 614416 | tf_op jit(solution)/shard_map/while/body/eval_jaxpr/reduce_scatter | solution.py:474
  1038.8 100.3 %reduce-scatter.49.cloned.1.call-done = bf16[120,2560]{1,0:T(8,128)(2,1)} async-done(((bf16[960,2560]{1,0:T(8,128)(2,1)}), bf16[120,2560]{1,0:T(8,128)(2,1)}) %reduce-scatter.49.cloned.1.call-update) | async-done | bytes 614416 | tf_op jit(solution)/shard_map/while/body/eval_jaxpr/reduce_scatter | solution.py:471
  1141.4 100.1 %reduce-scatter.47.cloned.1.call-done = bf16[120,2560]{1,0:T(8,128)(2,1)} async-done(((bf16[960,2560]{1,0:T(8,128)(2,1)}), bf16[120,2560]{1,0:T(8,128)(2,1)}) %reduce-scatter.47.cloned.1.call-update) | async-done | bytes 614416 | tf_op jit(solution)/shard_map/while/body/eval_jaxpr/reduce_scatter | solution.py:468
  1260.4 19.3 all-gather.28
  1282.5 17.4 all-reduce.17
  1300.0 32.4 %all-gather.27 = bf16[8,120,320]{1,2,0:T(8,128)(2,1)S(1)} all-gather(bf16[1,120,320]{1,2,0:T(8,128)(2,1)S(1)} %bitcast.1553), channel_id=1, replica_groups=mesh['dp'=8,'blk'=4] {'dp'}, dimensions={0}, use_global_device_ids=true | all-gather | bytes 691200 | tf_op jit(solution)/shard_map/while/body/eval_jaxpr/all_gather | solution.py:401
  1342.9 33.3 %all-gather.30 = bf16[8,120,320]{1,2,0:T(8,128)(2,1)S(1)} all-gather(bf16[1,120,320]{1,2,0:T(8,128)(2,1)S(1)} %bitcast.1552), channel_id=1, replica_groups=mesh['dp'=8,'blk'=4] {'dp'}, dimensions={0}, use_global_device_ids=true | all-gather | bytes 691200 | tf_op jit(solution)/shard_map/while/body/eval_jaxpr/all_gather | solution.py:402
  1448.1 68.6 %all-gather.48.cloned.1.call-done = bf16[960,2560]{1,0:T(8,128)(2,1)} async-done(((bf16[120,2560]{1,0:T(8,128)(2,1)}), bf16[960,2560]{1,0:T(8,128)(2,1)}) %all-gather.48.cloned.1.call-update) | async-done | bytes 4915216 | tf_op jit(solution)/shard_map/while/body/eval_jaxpr/all_gather | solution.py:405
  1523.8 79.8 %all-gather.50.cloned.1.call-done = bf16[2560,960]{1,0:T(8,128)(2,1)} async-done(((bf16[320,960]{1,0:T(8,128)(2,1)}), bf16[2560,960]{1,0:T(8,128)(2,1)}) %all-gather.50.cloned.1.call-update) | async-done | bytes 4915216 | tf_op jit(solution)/shard_map/while/body/eval_jaxpr/all_gather | solution.py:406
  1742.9 21.2 reduce-scatter.31.cloned.1.call-done
  1822.8 15.2 reduce-scatter.35.cloned.1.call-done
  1917.5 20.4 reduce-scatter.43.cloned.1.call-done
  2009.0 37.6 %all-reduce.19 = (bf16[960]{0:T(1024)(128)(2,1)S(1)}, bf16[960]{0:T(1024)(128)(2,1)S(1)}, bf16[960,3]{0,1:T(4,128)(2,1)S(1)}) all-reduce(bf16[960]{0:T(1024)(128)(2,1)S(1)} %add_convert_fusion.27, bf16[960]{0:T(1024)(128)(2,1)S(1)} %copy-done.172, ...), channel_id=21, replica_groups=mesh['dp'=8,'blk'=4] {'dp'}, use_global_device_ids=true, to_apply=%region_48.48.clone | all-reduce | flops 4800 | bytes 19200 | tf_op jit(solution)/shard_map/while
  2049.7 45.9 %reduce-scatter.45.cloned.1.call-done = bf16[120,960]{1,0:T(8,128)(2,1)} async-done(((bf16[960,960]{1,0:T(8,128)(2,1)}), bf16[120,960]{1,0:T(8,128)(2,1)}) %reduce-scatter.45.cloned.1.call-update) | async-done | bytes 230416 | tf_op jit(solution)/shard_map/while/body/eval_jaxpr/reduce_scatter | solution.py:465
  2097.5 67.7 %reduce-scatter.39.cloned.1.call-done = bf16[120,960]{1,0:T(8,128)(2,1)} async-done(((bf16[960,960]{1,0:T(8,128)(2,1)}), bf16[120,960]{1,0:T(8,128)(2,1)}) %reduce-scatter.39.cloned.1.call-update) | async-done | bytes 230416 | tf_op jit(solution)/shard_map/while/body/eval_jaxpr/reduce_scatter | solution.py:456
  2166.3 104.0 %reduce-scatter.51.cloned.1.call-done = bf16[320,960]{1,0:T(8,128)(2,1)} async-done(((bf16[2560,960]{1,0:T(8,128)(2,1)}), bf16[320,960]{1,0:T(8,128)(2,1)}) %reduce-scatter.51.cloned.1.call-update) | async-done | bytes 614416 | tf_op jit(solution)/shard_map/while/body/eval_jaxpr/reduce_scatter | solution.py:474
  2271.9 100.4 %reduce-scatter.49.cloned.1.call-done = bf16[120,2560]{1,0:T(8,128)(2,1)} async-done(((bf16[960,2560]{1,0:T(8,128)(2,1)}), bf16[120,2560]{1,0:T(8,128)(2,1)}) %reduce-scatter.49.cloned.1.call-update) | async-done | bytes 614416 | tf_op jit(solution)/shard_map/while/body/eval_jaxpr/reduce_scatter | solution.py:471
  2375.0 99.9 %reduce-scatter.47.cloned.1.call-done = bf16[120,2560]{1,0:T(8,128)(2,1)} async-done(((bf16[960,2560]{1,0:T(8,128)(2,1)}), bf16[120,2560]{1,0:T(8,128)(2,1)}) %reduce-scatter.47.cloned.1.call-update) | async-done | bytes 614416 | tf_op jit(solution)/shard_map/while/body/eval_jaxpr/reduce_scatter | solution.py:468
  2495.8 51.3 %all-reduce.23.cloned.1.call-done = (bf16[120,960]{1,0:T(8,128)(2,1)}, bf16[120,320]{0,1:T(8,128)(2,1)}, bf16[120,320]{0,1:T(8,128)(2,1)}, bf16[120,960]{1,0:T(8...) async-done(((bf16[120,960]{1,0:T(8,128)(2,1)}, bf16[120,320]{0,1:T(8,128)(2,1)}, bf16[120,320]{0,1:T(8,128)(2,1)}, ...) | async-done | bytes 2457616 | tf_op jit(solution)/shard_map/psum | solution.py:495
  (1709 shorter events, 954.9 us)
Async XLA Ops:
  8.5 166.9 %all-gather.42.cloned.1.call-start = ((), (), s32[]{:S(2)}) async-start(), calls=%async_computation.12 | async-start | bytes 2211840 | tf_op jit(solution)/shard_map/while/body/eval_jaxpr/all_gather | solution.py:400
  9.2 196.2 %all-gather.44.cloned.1.call-start = ((), (), s32[]{:S(2)}) async-start(), calls=%async_computation.13 | async-start | bytes 2211840 | tf_op jit(solution)/shard_map/while/body/eval_jaxpr/all_gather | solution.py:403
  10.0 200.2 %all-gather.46.cloned.1.call-start = ((), (), s32[]{:S(2)}) async-start(), calls=%async_computation.14 | async-start | bytes 5529600 | tf_op jit(solution)/shard_map/while/body/eval_jaxpr/all_gather | solution.py:404
  10.7 273.5 %all-gather.48.cloned.1.call-start = ((), (), s32[]{:S(2)}) async-start(), calls=%async_computation.15 | async-start | bytes 5529600 | tf_op jit(solution)/shard_map/while/body/eval_jaxpr/all_gather | solution.py:405
  11.3 359.6 %all-gather.50.cloned.1.call-start = ((), (), s32[]{:S(2)}) async-start(), calls=%async_computation.16 | async-start | bytes 5898240 | tf_op jit(solution)/shard_map/while/body/eval_jaxpr/all_gather | solution.py:406
  11.9 497.4 %reduce-scatter.33.cloned.1.call-start = ((), (), s32[]{:S(2)}) async-start(), calls=%async_computation.18 | async-start | bytes 245760 | tf_op jit(solution)/shard_map/while
  502.1 79.9 %reduce-scatter.37.cloned.1.call-start = ((), (), s32[]{:S(2)}) async-start(), calls=%async_computation.20 | async-start | bytes 491520 | tf_op jit(solution)/shard_map/while
  561.0 44.5 %reduce-scatter.35.cloned.1.call-start = ((), (), s32[]{:S(2)}) async-start(), calls=%async_computation.19 | async-start | bytes 491520 | tf_op jit(solution)/shard_map/while
  570.3 109.9 %reduce-scatter.41.cloned.1.call-start = ((), (), s32[]{:S(2)}) async-start(), calls=%async_computation.22 | async-start | bytes 819200 | tf_op jit(solution)/shard_map/while/body/eval_jaxpr/reduce_scatter | solution.py:297
  657.5 47.8 %reduce-scatter.43.cloned.1.call-start = ((), (), s32[]{:S(2)}) async-start(), calls=%async_computation.23 | async-start | bytes 819200 | tf_op jit(solution)/shard_map/while/body/eval_jaxpr/reduce_scatter | solution.py:303
  669.3 146.0 %all-reduce.25.cloned.1.call-start = ((), (), s32[]{:S(2)}) async-start(), calls=%async_computation.24 | async-start | bytes 2621440 | tf_op jit(solution)/shard_map/while
  708.1 154.8 %reduce-scatter.45.cloned.1.call-start = ((), (), s32[]{:S(2)}) async-start(), calls=%async_computation.25 | async-start | bytes 2211840 | tf_op jit(solution)/shard_map/while/body/eval_jaxpr/reduce_scatter | solution.py:465
  712.6 219.8 %reduce-scatter.39.cloned.1.call-start = ((), (), s32[]{:S(2)}) async-start(), calls=%async_computation.21 | async-start | bytes 2211840 | tf_op jit(solution)/shard_map/while/body/eval_jaxpr/reduce_scatter | solution.py:456
  723.5 313.8 %reduce-scatter.51.cloned.1.call-start = ((), (), s32[]{:S(2)}) async-start(), calls=%async_computation.28 | async-start | bytes 5898240 | tf_op jit(solution)/shard_map/while/body/eval_jaxpr/reduce_scatter | solution.py:474
  740.3 398.8 %reduce-scatter.49.cloned.1.call-start = ((), (), s32[]{:S(2)}) async-start(), calls=%async_computation.27 | async-start | bytes 5529600 | tf_op jit(solution)/shard_map/while/body/eval_jaxpr/reduce_scatter | solution.py:471
  749.0 492.5 %reduce-scatter.47.cloned.1.call-start = ((), (), s32[]{:S(2)}) async-start(), calls=%async_computation.26 | async-start | bytes 5529600 | tf_op jit(solution)/shard_map/while/body/eval_jaxpr/reduce_scatter | solution.py:468
  1244.3 163.2 %all-gather.42.cloned.1.call-start = ((), (), s32[]{:S(2)}) async-start(), calls=%async_computation.12 | async-start | bytes 2211840 | tf_op jit(solution)/shard_map/while/body/eval_jaxpr/all_gather | solution.py:400
  1244.9 192.6 %all-gather.44.cloned.1.call-start = ((), (), s32[]{:S(2)}) async-start(), calls=%async_computation.13 | async-start | bytes 2211840 | tf_op jit(solution)/shard_map/while/body/eval_jaxpr/all_gather | solution.py:403
  1245.6 196.6 %all-gather.46.cloned.1.call-start = ((), (), s32[]{:S(2)}) async-start(), calls=%async_computation.14 | async-start | bytes 5529600 | tf_op jit(solution)/shard_map/while/body/eval_jaxpr/all_gather | solution.py:404
  1246.2 270.5 %all-gather.48.cloned.1.call-start = ((), (), s32[]{:S(2)}) async-start(), calls=%async_computation.15 | async-start | bytes 5529600 | tf_op jit(solution)/shard_map/while/body/eval_jaxpr/all_gather | solution.py:405
  1246.9 356.7 %all-gather.50.cloned.1.call-start = ((), (), s32[]{:S(2)}) async-start(), calls=%async_computation.16 | async-start | bytes 5898240 | tf_op jit(solution)/shard_map/while/body/eval_jaxpr/all_gather | solution.py:406
  1247.7 494.2 %reduce-scatter.33.cloned.1.call-start = ((), (), s32[]{:S(2)}) async-start(), calls=%async_computation.18 | async-start | bytes 245760 | tf_op jit(solution)/shard_map/while
  1734.7 79.8 %reduce-scatter.37.cloned.1.call-start = ((), (), s32[]{:S(2)}) async-start(), calls=%async_computation.20 | async-start | bytes 491520 | tf_op jit(solution)/shard_map/while
  1802.9 110.0 %reduce-scatter.41.cloned.1.call-start = ((), (), s32[]{:S(2)}) async-start(), calls=%async_computation.22 | async-start | bytes 819200 | tf_op jit(solution)/shard_map/while/body/eval_jaxpr/reduce_scatter | solution.py:297
  1890.2 47.8 %reduce-scatter.43.cloned.1.call-start = ((), (), s32[]{:S(2)}) async-start(), calls=%async_computation.23 | async-start | bytes 819200 | tf_op jit(solution)/shard_map/while/body/eval_jaxpr/reduce_scatter | solution.py:303
  1901.6 146.2 %all-reduce.25.cloned.1.call-start = ((), (), s32[]{:S(2)}) async-start(), calls=%async_computation.24 | async-start | bytes 2621440 | tf_op jit(solution)/shard_map/while
  1940.7 154.9 %reduce-scatter.45.cloned.1.call-start = ((), (), s32[]{:S(2)}) async-start(), calls=%async_computation.25 | async-start | bytes 2211840 | tf_op jit(solution)/shard_map/while/body/eval_jaxpr/reduce_scatter | solution.py:465
  1945.2 220.0 %reduce-scatter.39.cloned.1.call-start = ((), (), s32[]{:S(2)}) async-start(), calls=%async_computation.21 | async-start | bytes 2211840 | tf_op jit(solution)/shard_map/while/body/eval_jaxpr/reduce_scatter | solution.py:456
  1956.2 314.2 %reduce-scatter.51.cloned.1.call-start = ((), (), s32[]{:S(2)}) async-start(), calls=%async_computation.28 | async-start | bytes 5898240 | tf_op jit(solution)/shard_map/while/body/eval_jaxpr/reduce_scatter | solution.py:474
  1973.0 399.3 %reduce-scatter.49.cloned.1.call-start = ((), (), s32[]{:S(2)}) async-start(), calls=%async_computation.27 | async-start | bytes 5529600 | tf_op jit(solution)/shard_map/while/body/eval_jaxpr/reduce_scatter | solution.py:471
  1981.7 493.1 %reduce-scatter.47.cloned.1.call-start = ((), (), s32[]{:S(2)}) async-start(), calls=%async_computation.26 | async-start | bytes 5529600 | tf_op jit(solution)/shard_map/while/body/eval_jaxpr/reduce_scatter | solution.py:468
  2479.3 67.7 %all-reduce.23.cloned.1.call-start = ((), (), s32[]{:S(2)}) async-start(), calls=%async_computation.11 | async-start | bytes 5079040 | tf_op jit(solution)/shard_map/psum | solution.py:495
  (462 other events, 11458.5 us)
Sparse Core Ops, SparseCore 0:
  11.7 50.5 all-gather.41
  64.8 50.6 all-gather.43
  117.9 83.4 all-gather.45
  203.7 80.4 all-gather.47
  286.4 84.4 all-gather.49
  511.8 19.7 reduce-scatter.30
  561.1 20.8 reduce-scatter.36
  584.7 20.8 reduce-scatter.34
  657.7 22.4 reduce-scatter.40
  682.8 22.4 reduce-scatter.42
  709.3 84.3 all-reduce.24
  797.1 65.7 reduce-scatter.44
  866.7 65.6 reduce-scatter.38
  935.8 101.4 reduce-scatter.50
  1040.8 98.2 reduce-scatter.48
  1143.1 98.4 reduce-scatter.46
  1247.2 47.6 all-gather.41
  1297.4 50.8 all-gather.43
  1350.5 83.2 all-gather.45
  1436.2 80.4 all-gather.47
  1519.1 84.4 all-gather.49
  1744.3 19.7 reduce-scatter.30
  1793.7 20.8 reduce-scatter.36
  1817.1 20.8 reduce-scatter.34
  1890.3 22.4 reduce-scatter.40
  1915.5 22.4 reduce-scatter.42
  1942.0 84.3 all-reduce.24
  2029.7 65.7 reduce-scatter.44
  2099.5 65.6 reduce-scatter.38
  2168.8 101.5 reduce-scatter.50
  2273.9 98.3 reduce-scatter.48
  2376.4 98.3 reduce-scatter.46
  (2 shorter events, 35.5 us)
Sparse Core Ops, SparseCore 1:
  2487.7 59.3 all-reduce.22
where the time goes:
time: 2570 us; the launch traced here: 2560 us
  waiting for transfers between devices  1340 us (52%)
  matrix products  411 us (16%)
  blocking collectives  372 us (14%)
  local copies, waits for them, and re-layouts  206 us (8%)
  other arithmetic  199 us (8%)
    reduce_scatter x2, waiting for transfers between devices, one_micro(): lax.psum_scatter(full_grads[6].astype(jnp.bfloat16), 'dp', scatter_dimens...  208 us
    reduce_scatter x2, waiting for transfers between devices, one_micro(): lax.psum_scatter(full_grads[5].astype(jnp.bfloat16), 'dp', scatter_dimens...  201 us
    reduce_scatter x2, waiting for transfers between devices, one_micro(): lax.psum_scatter(full_grads[4].astype(jnp.bfloat16), 'dp', scatter_dimens...  200 us
    all_gather x2, waiting for transfers between devices, one_micro(): lax.all_gather(down_weight, 'dp', axis=0, tiled=True)  159 us
    all_gather x2, waiting for transfers between devices, one_micro(): lax.all_gather(up_weight, 'dp', axis=0, tiled=True)  137 us
    reduce_scatter x2, waiting for transfers between devices, one_micro(): lax.psum_scatter(full_grads[0].astype(jnp.bfloat16), 'dp', scatter_dimens...  135 us
    while x4, blocking collectives  110 us
    while x44, waiting for transfers between devices  110 us
  transfers between devices with their start and end apart: 35, of which 27 were waited for; matrix products, arithmetic and copies ran while one was open for 17% of the time, Pallas kernels for 0%

commit v1 on v0

--- a/solution.py
+++ b/solution.py
@@ -1,9 +1,13 @@
+import functools
 import math
 
 import jax
 import jax.numpy as jnp
 from jax import lax
+from jax.experimental import pallas as pl
+from jax.experimental.pallas import tpu as pltpu
 from jax.sharding import PartitionSpec as P
+
 
 HEADS = 15
 KV_HEADS = 5
@@ -166,8 +170,8 @@
         middle,
         second_scale,
         normalized_second,
-        gate_preactivation,
-        up_preactivation,
+        gate_preactivation.astype(jnp.bfloat16),
+        up_preactivation.astype(jnp.bfloat16),
         hidden_activation,
         feedforward_output,
         router_gate,
@@ -227,6 +231,8 @@
     hidden_grad = jnp.einsum(
         "srd,fd->srf", feed_grad, down_projection, preferred_element_type=jnp.float32
     )
+    gate_preactivation = gate_preactivation.astype(jnp.float32)
+    up_preactivation = up_preactivation.astype(jnp.float32)
     gate_sigmoid = jax.nn.sigmoid(gate_preactivation)
     up_grad = (hidden_grad * gate_preactivation * gate_sigmoid).astype(jnp.bfloat16)
     gate_pre_grad = (
@@ -268,31 +274,43 @@
     )
     key_all = key_all.reshape(seq_count, -1, KV_HEADS, HEAD_DIM)
     value_all = value_all.reshape(seq_count, -1, KV_HEADS, HEAD_DIM)
-    allowed = attention_mask(positions, all_slots)
-    scores = (
-        jnp.einsum("sqgcd,skgd->sgcqk", queries, key_all, preferred_element_type=jnp.float32)
-        * attn_scale
-    )
-    chances = jnp.where(allowed, jnp.exp(scores - summary[..., None]), 0.0)
-    chance_grad = jnp.einsum(
-        "sqgcd,skgd->sgcqk", attn_grad, value_all, preferred_element_type=jnp.float32
-    )
-    row_dots = jnp.sum(chances * chance_grad, axis=-1)
-    score_grad = (chances * (chance_grad - row_dots[..., None])).astype(jnp.bfloat16)
-    query_grad = (
-        jnp.einsum("sgcqk,skgd->sqgcd", score_grad, key_all, preferred_element_type=jnp.float32)
-        * attn_scale
-    )
-    key_grad_all = (
-        jnp.einsum("sgcqk,sqgcd->skgd", score_grad, queries, preferred_element_type=jnp.float32)
-        * attn_scale
-    )
-    value_grad_all = jnp.einsum(
-        "sgcqk,sqgcd->skgd",
-        chances.astype(jnp.bfloat16),
-        attn_grad,
-        preferred_element_type=jnp.float32,
-    )
+    def one_sequence(queries, key_all, value_all, attn_grad, summary, positions, all_slots):
+        allowed = attention_mask(positions, all_slots)
+        scores = (
+            jnp.einsum("sqgcd,skgd->sgcqk", queries, key_all, preferred_element_type=jnp.float32)
+            * attn_scale
+        )
+        chances = jnp.where(allowed, jnp.exp(scores - summary[..., None]), 0.0)
+        chance_grad = jnp.einsum(
+            "sqgcd,skgd->sgcqk", attn_grad, value_all, preferred_element_type=jnp.float32
+        )
+        row_dots = jnp.sum(chances * chance_grad, axis=-1)
+        score_grad = (chances * (chance_grad - row_dots[..., None])).astype(jnp.bfloat16)
+        query_grad = (
+            jnp.einsum("sgcqk,skgd->sqgcd", score_grad, key_all, preferred_element_type=jnp.float32)
+            * attn_scale
+        )
+        key_grad_all = (
+            jnp.einsum("sgcqk,sqgcd->skgd", score_grad, queries, preferred_element_type=jnp.float32)
+            * attn_scale
+        )
+        value_grad_all = jnp.einsum(
+            "sgcqk,sqgcd->skgd",
+            chances.astype(jnp.bfloat16),
+            attn_grad,
+            preferred_element_type=jnp.float32,
+        )
+
+        return query_grad, key_grad_all.astype(jnp.bfloat16), value_grad_all.astype(jnp.bfloat16)
+
+    pieces, token = [], None
+    for s in range(seq_count):
+        args = tuple(v[s:s + 1] for v in (queries, key_all, value_all, attn_grad, summary, positions, all_slots))
+        if pieces:
+            args, last = lax.optimization_barrier((args, pieces[-1]))
+            pieces[-1] = last
+        pieces.append(one_sequence(*args))
+    query_grad, key_grad_all, value_grad_all = (jnp.concatenate(v, axis=0) for v in zip(*pieces))
     key_grad, value_grad = (
         lax.psum_scatter(
             key_grad_all.reshape(seq_count, -1, KV_HEADS * HEAD_DIM).astype(jnp.bfloat16),
@@ -357,6 +375,495 @@
         grad_second,
     )
     return (token_grad, matrices, router_grad)
+
+
+MESH = pl.DeviceIdType.MESH
+
+NZ, NX = 4, 2
+G = NZ * NX
+
+
+def gather_kernel(chunks, nslab, *refs):
+    ins, outs = refs[:nslab], refs[nslab:2 * nslab]
+    ls, zs, zr, xs, xr, ys, yr, cs, cr = refs[2 * nslab:]
+    dp, blk = lax.axis_index("dp"), lax.axis_index("blk")
+    z, x = dp // NX, lax.rem(dp, NX)
+    y, c = blk // 2, lax.rem(blk, 2)
+    left, right = (dp - NX, blk), (dp + NX, blk)
+    xm, ym, cm = (dp + 1 - 2 * x, blk), (dp, lax.rem(blk + 2, 4)), (dp, blk + 1 - 2 * c)
+    bar = pltpu.get_barrier_semaphore()
+    for t in (xm, ym, cm):
+        pl.semaphore_signal(bar, inc=1, device_id=t, device_id_type=MESH)
+
+    @pl.when(z > 0)
+    def _():
+        pl.semaphore_signal(bar, inc=1, device_id=left, device_id_type=MESH)
+
+    @pl.when(z < NZ - 1)
+    def _():
+        pl.semaphore_signal(bar, inc=1, device_id=right, device_id_type=MESH)
+
+    pl.semaphore_wait(bar, 3 + jnp.where(z > 0, 1, 0) + jnp.where(z < NZ - 1, 1, 0))
+
+    locs = [pltpu.make_async_copy(ins[s], outs[s].at[dp], ls.at[s]) for s in range(nslab)]
+    for l in locs:
+        l.start()
+
+    def piece(i, g, q):
+        s, c0, n, split = chunks[i]
+        return outs[s].at[g, q, :, pl.ds(c0, n)]
+
+    def myq(i):
+        return blk if chunks[i][3] == 4 else c
+
+    def rem(src, dst, a, b, to):
+        return pltpu.make_async_remote_copy(src_ref=src, dst_ref=dst, send_sem=a, recv_sem=b, device_id=to, device_id_type=MESH)
+
+    def own(i):
+        s, c0, n, split = chunks[i]
+        return ins[s].at[myq(i), :, pl.ds(c0, n)]
+
+    def zcopy(i, d, s, src_own):
+        zz = z - s if d == 0 else z + s
+        p = piece(i, zz * NX + x, myq(i))
+        return rem(own(i) if src_own else p, p, zs.at[i, d, s], zr.at[i, d, s], right if d == 0 else left)
+
+    def zrecv(i, d, s):
+        zz = z - 1 - s if d == 0 else z + 1 + s
+        p = piece(i, zz * NX + x, myq(i))
+        return rem(p, p, zs.at[i, d, s], zr.at[i, d, s], right if d == 0 else left)
+
+    def xcopy(i, zz, src_own=False):
+        p = piece(i, zz * NX + x, myq(i))
+        return rem(own(i) if src_own else p, p, xs.at[i, zz], xr.at[i, zz], xm)
+
+    def xrecv(i, zz):
+        p = piece(i, zz * NX + 1 - x, myq(i))
+        return rem(p, p, xs.at[i, zz], xr.at[i, zz], xm)
+
+    def ycopy(i, g):
+        p = piece(i, g, blk)
+        return rem(p, p, ys.at[i, g], yr.at[i, g], ym)
+
+    def yrecv(i, g):
+        p = piece(i, g, lax.rem(blk + 2, 4))
+        return rem(p, p, ys.at[i, g], yr.at[i, g], ym)
+
+    def ccopy(i, k, g):
+        q = myq(i) if k == 0 else lax.rem(blk + 2, 4)
+        p = piece(i, g, q)
+        return rem(p, p, cs.at[i, k, g], cr.at[i, k, g], cm)
+
+    def crecv(i, k, g):
+        if chunks[i][3] == 4:
+            mate = blk + 1 - 2 * c
+            q = mate if k == 0 else lax.rem(mate + 2, 4)
+        else:
+            q = 1 - c
+        p = piece(i, g, q)
+        return rem(p, p, cs.at[i, k, g], cr.at[i, k, g], cm)
+
+    def spread(i, g):
+        if chunks[i][3] == 4:
+            ycopy(i, g).start()
+        ccopy(i, 0, g).start()
+
+    nch = len(chunks)
+
+    def begin(i):
+        @pl.when(z < NZ - 1)
+        def _():
+            zcopy(i, 0, 0, True).start()
+
+        @pl.when(z > 0)
+        def _():
+            zcopy(i, 1, 0, True).start()
+        xcopy(i, z, True).start()
+
+    def zstep(i, s):
+        @pl.when(z - 1 - s >= 0)
+        def _():
+            zrecv(i, 0, s).wait_recv()
+            if s < NZ - 2:
+                @pl.when(z < NZ - 1)
+                def _():
+                    zcopy(i, 0, s + 1, False).start()
+            xcopy(i, z - 1 - s).start()
+            spread(i, (z - 1 - s) * NX + x)
+
+        @pl.when(z + 1 + s < NZ)
+        def _():
+            zrecv(i, 1, s).wait_recv()
+            if s < NZ - 2:
+                @pl.when(z > 0)
+                def _():
+                    zcopy(i, 1, s + 1, False).start()
+            xcopy(i, z + 1 + s).start()
+            spread(i, (z + 1 + s) * NX + x)
+
+    def xstep(i, k):
+        def one(zz):
+            xrecv(i, zz).wait_recv()
+            spread(i, zz * NX + 1 - x)
+        if k == 0:
+            one(z)
+        else:
+            pl.when(z - k >= 0)(lambda: one(z - k))
+            pl.when(z + k < NZ)(lambda: one(z + k))
+
+    def ystep(i, k):
+        g = lax.rem(dp + k, G)
+        yrecv(i, g).wait_recv()
+        ccopy(i, 1, g).start()
+
+    def cstep(i, k):
+        g = lax.rem(dp + k, G)
+        crecv(i, 0, g).wait_recv()
+        if chunks[i][3] == 4:
+            crecv(i, 1, g).wait_recv()
+
+    def sent(i):
+        @pl.when(z < NZ - 1)
+        def _():
+            zcopy(i, 0, 0, True).wait_send()
+
+        @pl.when(z > 0)
+        def _():
+            zcopy(i, 1, 0, True).wait_send()
+        for s in range(NZ - 1):
+            if s < NZ - 2:
+                @pl.when((z - 1 - s >= 0) & (z < NZ - 1))
+                def _():
+                    zcopy(i, 0, s + 1, False).wait_send()
+
+                @pl.when((z + 1 + s < NZ) & (z > 0))
+                def _():
+                    zcopy(i, 1, s + 1, False).wait_send()
+        xcopy(i, z, True).wait_send()
+        for k in range(1, NZ):
+            xcopy(i, lax.rem(z + k, NZ)).wait_send()
+        for k in range(1, G):
+            g = lax.rem(dp + k, G)
+            ccopy(i, 0, g).wait_send()
+            if chunks[i][3] == 4:
+                ycopy(i, g).wait_send()
+                ccopy(i, 1, g).wait_send()
+
+    stages = [begin] + [functools.partial(lambda i, s: (zstep(i, s), xstep(i, s)), s=s) for s in range(NZ - 1)]
+    stages.append(lambda i: xstep(i, NZ - 1))
+    stages.append(lambda i: [ystep(i, k) for k in range(1, G)] if chunks[i][3] == 4 else None)
+    stages.append(lambda i: [cstep(i, k) for k in range(1, G)])
+    stages.append(sent)
+    for t in range(nch + len(stages) - 1):
+        for s in reversed(range(len(stages))):
+            i = t - s
+            if 0 <= i < nch:
+                stages[s](i)
+    for l in locs:
+        l.wait()
+
+
+def gather(slabs, chunks):
+    n, nch = len(slabs), len(chunks)
+    dma = pltpu.SemaphoreType.DMA
+    return pl.pallas_call(
+        functools.partial(gather_kernel, chunks, n),
+        out_shape=[jax.ShapeDtypeStruct((G,) + s.shape, s.dtype) for s in slabs],
+        in_specs=[pl.BlockSpec(memory_space=pl.ANY)] * n,
+        out_specs=[pl.BlockSpec(memory_space=pl.ANY)] * n,
+        scratch_shapes=[dma((n,)), dma((nch, 2, NZ - 1)), dma((nch, 2, NZ - 1)), dma((nch, NZ)), dma((nch, NZ)),
+                        dma((nch, G)), dma((nch, G)), dma((nch, 2, G)), dma((nch, 2, G))],
+        compiler_params=pltpu.CompilerParams(collective_id=1, has_side_effects=True),
+        name="gather_weights",
+    )(*slabs)
+
+
+def add_into(dst, other, n):
+    def body(k, _):
+        dst[k] = (dst[k].astype(jnp.float32) + other(k).astype(jnp.float32)).astype(dst.dtype)
+        return 0
+    lax.fori_loop(0, n, body, 0)
+
+
+def reduce_kernel(chunks, nslab, *refs):
+    nch = len(chunks)
+    ins, outs = refs[:nslab], refs[nslab:2 * nslab]
+    bufs = refs[2 * nslab:]
+    own, crv, yrv, xrv, zrv, fin, s4b = (bufs[k * nch:(k + 1) * nch] for k in range(7))
+    ls, cs, cr, ys, yr, xs, xr, zs, zr, fs, fr = bufs[7 * nch:]
+    dp, blk = lax.axis_index("dp"), lax.axis_index("blk")
+    z, x = dp // NX, lax.rem(dp, NX)
+    y, c = blk // 2, lax.rem(blk, 2)
+    left, right = (dp - NX, blk), (dp + NX, blk)
+    xm, ym, cm = (dp + 1 - 2 * x, blk), (dp, lax.rem(blk + 2, 4)), (dp, blk + 1 - 2 * c)
+    bar = pltpu.get_barrier_semaphore()
+    for t in (xm, ym, cm):
+        pl.semaphore_signal(bar, inc=1, device_id=t, device_id_type=MESH)
+
+    @pl.when(z > 0)
+    def _():
+        pl.semaphore_signal(bar, inc=1, device_id=left, device_id_type=MESH)
+
+    @pl.when(z < NZ - 1)
+    def _():
+        pl.semaphore_signal(bar, inc=1, device_id=right, device_id_type=MESH)
+
+    pl.semaphore_wait(bar, 3 + jnp.where(z > 0, 1, 0) + jnp.where(z < NZ - 1, 1, 0))
+
+    def rem(src, dst, a, b, to):
+        return pltpu.make_async_remote_copy(src_ref=src, dst_ref=dst, send_sem=a, recv_sem=b, device_id=to, device_id_type=MESH)
+
+    def four(i):
+        return chunks[i][3] == 4
+
+    def part(i, core):
+        s, c0, n, split = chunks[i]
+        cols = pl.ds(c0, n)
+        return ins[s].at[:, :, :, core, :, cols] if split == 4 else ins[s].at[:, :, core, :, cols]
+
+    def load(i):
+        return pltpu.make_async_copy(part(i, c), own[i], ls.at[i])
+
+    def core_send(i):
+        return rem(part(i, 1 - c), crv[i], cs.at[i, 0], cr.at[i, 0], cm)
+
+    def y_send(i):
+        return rem(own[i].at[:, :, 1 - y], yrv[i], ys.at[i], yr.at[i], ym)
+
+    def s2(i):
+        return yrv[i] if four(i) else own[i]
+
+    def x_send(i):
+        return rem(s2(i).at[:, 1 - x], xrv[i], xs.at[i], xr.at[i], xm)
+
+    def z_copy(i, d, lo, hi, first, to):
+        src = xrv[i].at[pl.ds(lo, hi - lo)] if first else zrv[i].at[d, pl.ds(lo, hi - lo)]
+        return rem(src, zrv[i].at[d, pl.ds(lo, hi - lo)], zs.at[i, d], zr.at[i, d], to)
+
+    def right_send(i, k):
+        return z_copy(i, 0, k + 1, NZ, k == 0, right)
+
+    def left_send(i, k):
+        return z_copy(i, 1, 0, k, k == NZ - 1, left)
+
+    def st0(i):
+        load(i).start()
+        core_send(i).start()
+
+    def st1(i):
+        load(i).wait()
+        core_send(i).wait_recv()
+
+        def body(g, _):
+            zz, xx = g // NX, lax.rem(g, NX)
+            for yy in ((0, 1) if four(i) else (None,)):
+                at = (zz, xx) if yy is None else (zz, xx, yy)
+                own[i][at] = (own[i][at].astype(jnp.float32) + crv[i][at].astype(jnp.float32)).astype(jnp.bfloat16)
+            return 0
+        lax.fori_loop(0, G, body, 0)
+        if four(i):
+            y_send(i).start()
+
+    def st2(i):
+        if four(i):
+            y_send(i).wait_recv()
+
+            def body(g, _):
+                zz, xx = g // NX, lax.rem(g, NX)
+                yrv[i][zz, xx] = (yrv[i][zz, xx].astype(jnp.float32) + own[i][zz, xx, y].astype(jnp.float32)).astype(jnp.bfloat16)
+                return 0
+            lax.fori_loop(0, G, body, 0)
+        x_send(i).start()
+
+    def zstep(i, s):
+        if s < NZ - 1:
+            @pl.when(z == s)
+            def _():
+                if s > 0:
+                    z_copy(i, 0, s, NZ, False, right).wait_recv()
+                    for k in range(s + 1, NZ):
+                        zrv[i][0, k] = (zrv[i][0, k].astype(jnp.float32) + xrv[i][k].astype(jnp.float32)).astype(jnp.bfloat16)
+                right_send(i, s).start()
+
+            @pl.when(z == NZ - 1 - s)
+            def _():
+                k0 = NZ - 1 - s
+                if s > 0:
+                    z_copy(i, 1, 0, k0 + 1, False, left).wait_recv()
+                    for k in range(k0):
+                        zrv[i][1, k] = (zrv[i][1, k].astype(jnp.float32) + xrv[i][k].astype(jnp.float32)).astype(jnp.bfloat16)
+                left_send(i, k0).start()
+
+    def st3(i):
+        x_send(i).wait_recv()
+        add_into(xrv[i], lambda k: s2(i)[k, x], NZ)
+        zstep(i, 0)
+
+    def finish(i):
+        q = blk if four(i) else c
+        dst = fin[i].at[q] if four(i) else s4b[i]
+
+        def put(v):
+            if four(i):
+                fin[i][blk] = v.astype(jnp.bfloat16)
+            else:
+                s4b[i][...] = v.astype(jnp.bfloat16)
+
+        @pl.when(z == 0)
+        def _():
+            z_copy(i, 1, 0, 1, False, left).wait_recv()
+            put(xrv[i][0].astype(jnp.float32) + zrv[i][1, 0].astype(jnp.float32))
+
+        @pl.when(z == NZ - 1)
+        def _():
+            z_copy(i, 0, NZ - 1, NZ, False, right).wait_recv()
+            put(xrv[i][NZ - 1].astype(jnp.float32) + zrv[i][0, NZ - 1].astype(jnp.float32))
+
+        @pl.when((z > 0) & (z < NZ - 1))
+        def _():
+            put(xrv[i][z].astype(jnp.float32) + zrv[i][0, z].astype(jnp.float32) + zrv[i][1, z].astype(jnp.float32))
+        if four(i):
+            fin_send(i, 0).start()
+            fin_send(i, 1).start()
+        else:
+            fin_send(i, 0).start()
+
+    def fin_send(i, k):
+        if four(i):
+            q = blk if k < 2 else lax.rem(blk + 2, 4)
+            return rem(fin[i].at[q], fin[i].at[q], fs.at[i, k], fr.at[i, k], ym if k == 0 else cm)
+        if k == 0:
+            return rem(s4b[i], fin[i].at[2], fs.at[i, 0], fr.at[i, 0], ym)
+        return rem(fin[i].at[c], fin[i].at[c], fs.at[i, 1], fr.at[i, 1], cm)
+
+    def fin_recv(i, k):
+        if four(i):
+            mate = blk + 1 - 2 * c
+            q = lax.rem(blk + 2, 4) if k == 0 else mate if k == 1 else lax.rem(mate + 2, 4)
+            return rem(fin[i].at[q], fin[i].at[q], fs.at[i, k], fr.at[i, k], cm)
+        if k == 0:
+            return fin_send(i, 0)
+        return rem(fin[i].at[1 - c], fin[i].at[1 - c], fs.at[i, 1], fr.at[i, 1], cm)
+
+    def st8(i):
+        fin_recv(i, 0).wait_recv()
+        if four(i):
+            fin_send(i, 2).start()
+        else:
+            fin[i][c] = (fin[i][2].astype(jnp.float32) + s4b[i][...].astype(jnp.float32)).astype(jnp.bfloat16)
+            fin_send(i, 1).start()
+
+    def st9(i):
+        s, c0, n, split = chunks[i]
+        for k in ((1, 2) if four(i) else (1,)):
+            fin_recv(i, k).wait_recv()
+        for q in range(split):
+            outs[s][q, :, pl.ds(c0, n)] = fin[i][q].astype(jnp.float32)
+
+    def sent(i):
+        core_send(i).wait_send()
+        if four(i):
+            y_send(i).wait_send()
+        x_send(i).wait_send()
+        for k in range(NZ - 1):
+            pl.when(z == k)(lambda k=k: right_send(i, k).wait_send())
+            pl.when(z == k + 1)(lambda k=k: left_send(i, k + 1).wait_send())
+        for k in range(3 if four(i) else 2):
+            fin_send(i, k).wait_send()
+
+    stages = [st1, st2, st3] + [functools.partial(lambda i, s: zstep(i, s), s=s) for s in range(1, NZ - 1)] + [finish, st8, st9, sent]
+    for i in range(nch):
+        st0(i)
+    for t in range(nch + len(stages) - 1):
+        for s in reversed(range(len(stages))):
+            i = t - s
+            if 0 <= i < nch:
+                stages[s](i)
+
+
+def reduce(slabs, chunks):
+    n, nch = len(slabs), len(chunks)
+    dma = pltpu.SemaphoreType.DMA
+    bf = jnp.bfloat16
+
+    def shapes(kind):
+        out = []
+        for s, c0, nc, split in chunks:
+            h = slabs[s].shape[-2]
+            lead = (NZ, NX, 2) if split == 4 else (NZ, NX)
+            tiny = (1, 16, 128)
+            shape = dict(own=lead + (h, nc), crv=lead + (h, nc), yrv=(NZ, NX, h, nc) if split == 4 else tiny,
+                         xrv=(NZ, h, nc), zrv=(2, NZ, h, nc), fin=(4 if split == 4 else 3, h, nc),
+                         s4b=(h, nc) if split == 2 else tiny)[kind]
+            out.append(pltpu.VMEM(shape, bf))
+        return out
+    scratch = sum([shapes(k) for k in ("own", "crv", "yrv", "xrv", "zrv", "fin", "s4b")], [])
+    sems = [dma((nch,)), dma((nch, 1)), dma((nch, 1)), dma((nch,)), dma((nch,)), dma((nch,)), dma((nch,)),
+            dma((nch, 2)), dma((nch, 2)), dma((nch, 3)), dma((nch, 3))]
+    outs = []
+    for k, s in enumerate(slabs):
+        split = next(ch[3] for ch in chunks if ch[0] == k)
+        outs.append(jax.ShapeDtypeStruct((split,) + s.shape[-2:], jnp.float32))
+    return pl.pallas_call(
+        functools.partial(reduce_kernel, chunks, n),
+        out_shape=outs,
+        in_specs=[pl.BlockSpec(memory_space=pl.ANY)] * n,
+        out_specs=[pl.BlockSpec(memory_space=pltpu.VMEM)] * n,
+        scratch_shapes=scratch + sems,
+        compiler_params=pltpu.CompilerParams(collective_id=2, has_side_effects=True, vmem_limit_bytes=60 << 20),
+        name="reduce_grads",
+    )(*slabs)
+
+AG_CHUNKS = [(0, 0, 1664, 4), (1, 0, 1024, 2), (2, 0, 1280, 4), (2, 1280, 1280, 4), (3, 0, 512, 2), (2, 2560, 1280, 4),
+             (2, 3840, 1280, 4), (3, 512, 512, 2)]
+RS_CHUNKS = [(2, 0, 1280, 4), (3, 0, 512, 2), (2, 1280, 1280, 4), (2, 2560, 1280, 4), (3, 512, 512, 2), (2, 3840, 1280, 4),
+             (1, 0, 1024, 2), (0, 0, 896, 4), (0, 896, 768, 4)]
+
+
+def pad_to(v, shape):
+    return jnp.pad(v, [(0, b - a) for a, b in zip(v.shape, shape)])
+
+
+def gather_weights(weights):
+    n_dp, n_blk = lax.axis_size("dp"), lax.axis_size("blk")
+    if (n_dp, n_blk) != (G, 4):
+        return tuple(lax.all_gather(w, "dp", axis=0, tiled=True) for w in weights)
+    q, k, v, o, g, u, d, g1, g2, rt = weights
+    a = jnp.concatenate([q, k, v, g1[:, None], g2[:, None], rt], axis=1)
+    gu = jnp.concatenate([g, u], axis=1)
+    slabs = [pad_to(a, (128, 1664)).reshape(4, 32, 1664), pad_to(o, (128, 1024)).reshape(2, 64, 1024),
+             pad_to(gu, (128, 5120)).reshape(4, 32, 5120), pad_to(d, (320, 1024)).reshape(2, 160, 1024)]
+    a, o, gu, d = gather(slabs, AG_CHUNKS)
+    rows = q.shape[0]
+    a = a.reshape(G, 128, 1664)[:, :rows].reshape(G * rows, 1664)
+    o = o.reshape(G, 128, 1024)[:, :rows].reshape(G * rows, 1024)[:, :960]
+    gu = gu.reshape(G, 128, 5120)[:, :rows].reshape(G * rows, 5120)
+    d = d.reshape(2560, 1024)[:, :960]
+    return (a[:, :960], a[:, 960:1280], a[:, 1280:1600], o, gu[:, :2560], gu[:, 2560:], d,
+            a[:, 1600], a[:, 1601], a[:, 1602:1605])
+
+
+def reduce_grads(grads):
+    n_dp, n_blk = lax.axis_size("dp"), lax.axis_size("blk")
+    bf = jnp.bfloat16
+    if (n_dp, n_blk) != (G, 4):
+        shares = [lax.psum_scatter(v.astype(bf), "dp", scatter_dimension=0, tiled=True) for v in grads]
+        return tuple(lax.psum(v, "blk").astype(jnp.float32) for v in shares)
+    q, k, v, o, g, u, d, g1, g2, rt = grads
+    rows = q.shape[0] // G
+    a = jnp.concatenate([q, k, v, g1[:, None], g2[:, None], rt], axis=1).astype(bf)
+    gu = jnp.concatenate([g, u], axis=1).astype(bf)
+    a = pad_to(a.reshape(G, rows, -1), (G, 128, 1664)).reshape(NZ, NX, 2, 2, 32, 1664)
+    o = pad_to(o.astype(bf).reshape(G, rows, -1), (G, 128, 1024)).reshape(NZ, NX, 2, 64, 1024)
+    gu = pad_to(gu.reshape(G, rows, -1), (G, 128, 5120)).reshape(NZ, NX, 2, 2, 32, 5120)
+    d = pad_to(d.astype(bf), (2560, 1024)).reshape(NZ, NX, 2, 160, 1024)
+    a, o, gu, d = reduce([a, o, gu, d], RS_CHUNKS)
+    a = a.reshape(128, 1664)[:rows]
+    o = o.reshape(128, 1024)[:rows, :960]
+    gu = gu.reshape(128, 5120)[:rows]
+    d = d.reshape(320, 1024)[:, :960]
+    return (a[:, :960], a[:, 960:1280], a[:, 1280:1600], o, gu[:, :2560], gu[:, 2560:], d,
+            a[:, 1600], a[:, 1601], a[:, 1602:1605])
 
 
 def per_device(
@@ -381,33 +888,12 @@
     device = lax.axis_index("blk")
     capacity = (block_len, block_len // 2, block_len // 4)
     all_places = jnp.arange(block_len * blocks, dtype=jnp.int32)
-    shard_weights = (
-        query_weight,
-        key_weight,
-        value_weight,
-        output_weight,
-        gate_weight,
-        up_weight,
-        down_weight,
-        first_gain,
-        second_gain,
-        router_weight,
-    )
-
-    def one_micro(collected, inputs):
+    gathered = gather_weights((query_weight, key_weight, value_weight, output_weight, gate_weight, up_weight, down_weight,
+                               first_gain, second_gain, router_weight))
+    flat = lambda v: v.reshape((micro_count * seq_count,) + v.shape[2:])
+
+    def whole(inputs):
         micro_input, micro_cotangent, lengths_now, routes_now_two, routes_now_three = inputs
-        gathered = (
-            lax.all_gather(query_weight, "dp", axis=0, tiled=True),
-            lax.all_gather(key_weight, "dp", axis=0, tiled=True),
-            lax.all_gather(value_weight, "dp", axis=0, tiled=True),
-            lax.all_gather(output_weight, "dp", axis=0, tiled=True),
-            lax.all_gather(gate_weight, "dp", axis=0, tiled=True),
-            lax.all_gather(up_weight, "dp", axis=0, tiled=True),
-            lax.all_gather(down_weight, "dp", axis=0, tiled=True),
-            lax.all_gather(first_gain, "dp", axis=0, tiled=True),
-            lax.all_gather(second_gain, "dp", axis=0, tiled=True),
-            lax.all_gather(router_weight, "dp", axis=0, tiled=True),
-        )
         slot_sets = (
             jnp.where(all_places[None, :] < lengths_now[:, None], all_places[None, :], -1),
             routed_slots(routes_now_two, blocks, block_len, capacity[1]),
@@ -452,71 +938,11 @@
                     (earlier + latest for earlier, latest in zip(matrix_sums, matrices))
                 )
         full_grads = matrix_sums + (jnp.stack(router_columns, axis=1),)
-        shares = (
-            lax.psum_scatter(
-                full_grads[0].astype(jnp.bfloat16), "dp", scatter_dimension=0, tiled=True
-            ).astype(jnp.float32),
-            lax.psum_scatter(
-                full_grads[1].astype(jnp.bfloat16), "dp", scatter_dimension=0, tiled=True
-            ).astype(jnp.float32),
-            lax.psum_scatter(
-                full_grads[2].astype(jnp.bfloat16), "dp", scatter_dimension=0, tiled=True
-            ).astype(jnp.float32),
-            lax.psum_scatter(
-                full_grads[3].astype(jnp.bfloat16), "dp", scatter_dimension=0, tiled=True
-            ).astype(jnp.float32),
-            lax.psum_scatter(
-                full_grads[4].astype(jnp.bfloat16), "dp", scatter_dimension=0, tiled=True
-            ).astype(jnp.float32),
-            lax.psum_scatter(
-                full_grads[5].astype(jnp.bfloat16), "dp", scatter_dimension=0, tiled=True
-            ).astype(jnp.float32),
-            lax.psum_scatter(
-                full_grads[6].astype(jnp.bfloat16), "dp", scatter_dimension=0, tiled=True
-            ).astype(jnp.float32),
-            lax.psum_scatter(
-                full_grads[7].astype(jnp.bfloat16), "dp", scatter_dimension=0, tiled=True
-            ).astype(jnp.float32),
-            lax.psum_scatter(
-                full_grads[8].astype(jnp.bfloat16), "dp", scatter_dimension=0, tiled=True
-            ).astype(jnp.float32),
-            lax.psum_scatter(
-                full_grads[9].astype(jnp.bfloat16), "dp", scatter_dimension=0, tiled=True
-            ).astype(jnp.float32),
-        )
-        collected = tuple((earlier + latest for earlier, latest in zip(collected, shares)))
-        return (collected, (current.astype(jnp.bfloat16), upstream))
-
-    start_grads = tuple((jnp.zeros(matrix.shape, jnp.float32) for matrix in shard_weights))
-    collected, (outputs, input_grads) = lax.scan(
-        one_micro, start_grads, (block_input, cotangent, seq_lengths, routes_two, routes_three)
-    )
-    collected = (
-        lax.psum(collected[0].astype(jnp.bfloat16), "blk").astype(jnp.float32),
-        lax.psum(collected[1].astype(jnp.bfloat16), "blk").astype(jnp.float32),
-        lax.psum(collected[2].astype(jnp.bfloat16), "blk").astype(jnp.float32),
-        lax.psum(collected[3].astype(jnp.bfloat16), "blk").astype(jnp.float32),
-        lax.psum(collected[4].astype(jnp.bfloat16), "blk").astype(jnp.float32),
-        lax.psum(collected[5].astype(jnp.bfloat16), "blk").astype(jnp.float32),
-        lax.psum(collected[6].astype(jnp.bfloat16), "blk").astype(jnp.float32),
-        lax.psum(collected[7].astype(jnp.bfloat16), "blk").astype(jnp.float32),
-        lax.psum(collected[8].astype(jnp.bfloat16), "blk").astype(jnp.float32),
-        lax.psum(collected[9].astype(jnp.bfloat16), "blk").astype(jnp.float32),
-    )
-    return (
-        outputs,
-        input_grads,
-        collected[0],
-        collected[1],
-        collected[2],
-        collected[3],
-        collected[4],
-        collected[5],
-        collected[6],
-        collected[7],
-        collected[8],
-        collected[9],
-    )
+        return (full_grads, current.astype(jnp.bfloat16), upstream)
+
+    full_grads, outputs, input_grads = whole(tuple(map(flat, (block_input, cotangent, seq_lengths, routes_two, routes_three))))
+    unflat = lambda v: v.reshape(block_input.shape)
+    return (unflat(outputs), unflat(input_grads)) + reduce_grads(full_grads)
 
 
 def solution(mesh):

time: 2570 us -> 1140 us (0.44)
  waiting for transfers between devices: 1340 us -> 50 us
  blocking collectives: 372 us -> 29.6 us
  Pallas kernels: 0 us -> 228 us
  local copies, waits for them, and re-layouts: 206 us -> 361 us
  matrix products: 411 us -> 317 us
  other arithmetic: 199 us -> 123 us
    reduce_scatter x10 -> x0, waiting for transfers between devices: 836 us -> none  [the longest x2 208 us: one_micro(): lax.psum_scatter(full_grads[6].astype(jnp.bfloat16), 'dp', scatter_dimens...]
    all_gather x10 -> x2, waiting for transfers between devices: 296 us -> 0.01 us  [the longest x1 0.01 us: block_forward(): lax.all_gather(keyset, 'blk', axis=1, tiled=True)]
    pallas_call x0 -> x2, Pallas kernels: none -> 228 us  [the longest x1 139 us: reduce(): pl.pallas_call(functools.partial(reduce_kernel, chunks, n), out_shape=out...]
    all_gather x10 -> x0, blocking collectives: 198 us -> none  [the longest x2 66.5 us: one_micro(): lax.all_gather(value_weight, 'dp', axis=0, tiled=True)]
    scatter x14 -> x7, local copies, waits for them, and re-layouts: 16.6 us -> 159 us  [place_rows(): return block_vals.at[index_vals].set(new_vals, mode='drop')]
    while x4 -> x0, blocking collectives: 110 us -> none
    while x44 -> x0, waiting for transfers between devices: 110 us -> none
    while x942 -> x0, local copies, waits for them, and re-layouts: 79.1 us -> none
  transfers between devices with their start and end apart: 35 -> 8, of which waited for: 27 -> 3; matrix products, arithmetic and copies ran while one was open for 17% -> 22% of each run, Pallas kernels for 0% -> 0%
where the time goes in v1:
time: 1140 us; the launch traced here: 1130 us
  local copies, waits for them, and re-layouts  361 us (32%)
  matrix products  317 us (28%)
  Pallas kernels  228 us (20%)
  other arithmetic  123 us (11%)
  waiting for transfers between devices  50 us (4%)
  blocking collectives  29.6 us (3%)
  between operations  19.3 us (2%)
    scatter x7, local copies, waits for them, and re-layouts, place_rows(): return block_vals.at[index_vals].set(new_vals, mode='drop')  159 us
    pallas_call x1, Pallas kernels, reduce(): pl.pallas_call(functools.partial(reduce_kernel, chunks, n), out_shape=out...  139 us
    pallas_call x1, Pallas kernels, gather(): pl.pallas_call(functools.partial(gather_kernel, chunks, n), out_shape=[ja...  89.8 us
    unnamed x608, local copies, waits for them, and re-layouts  50.9 us
    unnamed x11, waiting for transfers between devices  31.2 us
    gather x10, local copies, waits for them, and re-layouts, pick_rows(): return block_vals[index_vals]  23.7 us
  transfers between devices with their start and end apart: 8, of which 3 were waited for; matrix products, arithmetic and copies ran while one was open for 22% of the time, Pallas kernels for 0%

profile of v1, /device:TPU:0, one launch (start us, length us, event | category | flops | bytes accessed | tf_op | source)
XLA Modules:
  0.0 1128.8 jit_solution(8007447992643282655)
XLA Ops:
  16.5 89.8 %gather_weights.1 = (bf16[8,4,32,1664]{3,2,1,0:T(8,128)(2,1)}, bf16[8,2,64,1024]{3,2,1,0:T(8,128)(2,1)}, bf16[8,4,32,5120]{3,2,1,0:T(8,128)(2,1)}, bf16[8,2,160,1024]{3,2,1,0:T(8,128)(2,1)}) custom-call(bf16[4,32,1664]{2,1,0:T(8,128)(2,1)} %bitcast.1314, bf16[2,64,1024]{2,1,0:T(8,128)(2,1)} %bitcast.1338, bf16[4,32,5120]{2,1,0:T(8,128)(2,1)} %bitcast.1267, ...), custom_call_target="tpu_custom_call" | custom-call | tf_op jit(solution)/shard_map/gather_weights/pallas_call | solution.py:569
  122.3 9.1 gather_fusion
  157.7 8.1 slice.490
  192.1 14.0 %fusion = (f32[2,5,3,256]{3,2,1,0:T(4,128)S(1)}, f32[2,5,1024,256,3]{3,2,4,1,0:T(8,128)}) fusion(pred[2,256,1024]{1,2,0:T(8,128)(4,1)} %compare_and_fusion, bf16[2,1024,5,64,1]{1,3,4,2,0:T(8,128)(2,1)} %bitcast.1230, bf16[2,256,5,3,64]{1,4,3,2,0:T(8,128)(2,1)} %bitcast.1228), kind=kOutput, calls=%fused_computation.16 | convolution fusion | flops 1030218240 | bytes 34306048 | tf_op jit(solution)/shard_map/sqgcd,skgd->sgcqk/dot_general | solution.py:124
  206.1 14.7 %fusion.1 = f32[2,5,3,256]{3,2,1,0:T(4,128)S(1)} fusion(f32[2,5,1024,256,3]{3,2,4,1,0:T(8,128)} %get-tuple-element.302, f32[2,5,3,256]{3,2,1,0:T(4,128)S(1)} %get-tuple-element.301, pred[2,256,1024]{1,2,0:T(8,128)(4,1)S(1)} %copy-done.44), kind=kLoop, calls=%fused_computation.17 | loop fusion | flops 39313920 | bytes 32043008 | tf_op jit(solution)/shard_map/reduce_sum | solution.py:130
  221.4 15.5 %fusion.91 = bf16[2,5,64,3,256]{4,2,3,1,0:T(8,128)(2,1)S(1)} fusion(bf16[2,1024,5,64,1]{1,3,4,2,0:T(8,128)(2,1)} %bitcast.1325, f32[2,5,1024,256,3]{3,2,4,1,0:T(8,128)} %get-tuple-element.302, f32[2,5,3,256]{3,2,1,0:T(4,128)S(1)} %get-tuple-element.253, f32[2,5,3,256]{3,2,1,0:T(4,128)S(1)} %get-tuple-element.301, pred[2,256,1024]{1,2,0:T(8,128)(4,1)S(1)} %copy-done.44), kind=kOutput, calls=%fused_computation.179 | convolution fusion | flops 1054310400 | bytes 34336768 | tf_op jit(solution)/shard_map/sgcqk,skgd->sqgcd/dot_general | solution.py:133
  259.6 49.3 %scatter_fusion = f32[2,256,960]{2,1,0:T(8,128)S(1)} fusion(f32[2,256,960]{2,1,0:T(8,128)S(1)} %copy-done.5, s32[512]{0:T(512)S(1)} %bitcast.1169, f32[512,960]{1,0:T(8,128)} %bitcast.1242), kind=kCustom, calls=%fused_computation.7 | custom fusion | bytes 5902336 | tf_op jit(solution)/shard_map/vmap()/scatter | solution.py:72
  321.9 8.0 all_gather.26
  330.0 8.2 all_gather.27
  357.4 14.7 %scatter_fusion.1 = f32[2,256,960]{2,1,0:T(8,128)S(1)} fusion(f32[2,256,960]{2,1,0:T(8,128)S(1)} %scatter_fusion, s32[256]{0:T(256)S(1)} %copy-done.10, f32[256,960]{1,0:T(8,128)S(1)} %bitcast.1270), kind=kCustom, calls=%fused_computation.8 | custom fusion | bytes 2951168 | tf_op jit(solution)/shard_map/vmap()/scatter | solution.py:72
  482.2 17.1 %all-reduce.11.cloned.1.call-done = bf16[2,256,320]{2,0,1:T(2,128)(2,1)} async-done(((bf16[2,256,320]{2,0,1:T(2,128)(2,1)}), bf16[2,256,320]{2,0,1:T(2,128)(2,1)}) %all-reduce.11.cloned.1.call-update) | async-done | bytes 327696
  504.0 18.8 %reduce-scatter.10.cloned.1.call-done = bf16[2,64,320]{2,1,0:T(8,128)(2,1)} async-done(((bf16[2,256,320]{2,1,0:T(8,128)(2,1)}), bf16[2,64,320]{2,1,0:T(8,128)(2,1)}) %reduce-scatter.10.cloned.1.call-update) | async-done | bytes 81936 | tf_op jit(solution)/shard_map/reduce_scatter | solution.py:321
  529.9 12.8 %scatter_fusion.3 = f32[2,256,960]{2,1,0:T(8,128)S(1)} fusion(f32[2,256,960]{2,1,0:T(8,128)S(1)} %copy-done.2, s32[128]{0:T(128)S(1)} %copy-done.17, f32[128,960]{1,0:T(8,128)} %bitcast.1307), kind=kCustom, calls=%fused_computation.10 | custom fusion | bytes 1475584 | tf_op jit(solution)/shard_map/vmap()/scatter | solution.py:72
  581.9 18.0 %scatter_fusion.2 = f32[2,256,960]{2,1,0:T(8,128)} fusion(f32[2,256,960]{2,1,0:T(8,128)} %copy-done.6, s32[128]{0:T(128)S(1)} %copy-done.17, f32[128,960]{1,0:T(8,128)S(1)} %bitcast.1306), kind=kCustom, calls=%fused_computation.9 | custom fusion | bytes 1475584 | tf_op jit(solution)/shard_map/vmap()/scatter | solution.py:72
  642.7 13.9 %reduce-scatter.18.cloned.1.call-done = bf16[128,640]{1,0:T(8,128)(2,1)} async-done(((bf16[512,640]{1,0:T(8,128)(2,1)}), bf16[128,640]{1,0:T(8,128)(2,1)}) %reduce-scatter.18.cloned.1.call-update) | async-done | bytes 163856
  668.0 14.7 %scatter_fusion.4 = f32[2,256,960]{2,1,0:T(8,128)S(1)} fusion(f32[2,256,960]{2,1,0:T(8,128)S(1)} %scatter_fusion.3, s32[256]{0:T(256)S(1)} %copy-done.10, f32[256,960]{1,0:T(8,128)S(1)} %bitcast.1271), kind=kCustom, calls=%fused_computation.11 | custom fusion | bytes 2951168 | tf_op jit(solution)/shard_map/vmap()/scatter | solution.py:72
  682.7 7.7 gather_fusion.6
  692.4 8.8 fusion.36
  718.6 7.7 fusion.372
  726.4 8.2 fusion.11
  734.5 7.2 fusion.19
  750.0 7.7 fusion.211
  758.0 8.2 fusion.8
  766.2 12.6 %fusion.20 = bf16[5,3,256,1024]{2,3,1,0:T(8,128)(2,1)S(1)} fusion(f32[1,5,3,256,1024]{3,4,2,1,0:T(8,128)S(1)} %get-tuple-element.339, f32[5,1024,256,3]{2,1,3,0:T(8,128)} %fusion.211, f32[5,3,256]{2,1,0:T(4,128)S(1)} %get-tuple-element.338), kind=kLoop, calls=%fused_computation.49 | loop fusion | flops 11796480 | bytes 39336960 | tf_op jit(solution)/shard_map/reshape.257
  803.4 10.6 fusion.16
  814.0 7.9 copy.595
  827.5 8.1 fusion.138
  846.0 11.7 %fusion.17 = bf16[960,2560]{1,0:T(8,128)(2,1)} fusion(f32[960,2560,1]{1,0,2:T(8,128)} %fusion.382, f32[960,2560,1]{1,0,2:T(8,128)} %fusion.381, bf16[2,256,960]{1,2,0:T(8,128)(2,1)S(1)} %copy-done.26, bf16[2,256,2560]{2,1,0:T(8,128)(2,1)} %copy-done.91), kind=kOutput, calls=%fused_computation.43 | convolution fusion | flops 2523955200 | bytes 28180480 | tf_op jit(solution)/shard_map/srd,srf->df/dot_general | solution.py:247
  857.7 7.4 fusion.18
  866.6 12.3 %fusion.15 = bf16[8,128,5120]{2,1,0:T(8,128)(2,1)} fusion(bf16[8,120,2560]{2,1,0:T(8,128)(2,1)} %bitcast.1221, bf16[8,120,2560]{2,1,0:T(8,128)(2,1)} %bitcast.1222), kind=kLoop, calls=%fused_computation.38 | loop fusion | flops 36700160 | bytes 20316160 | tf_op jit(solution)/shard_map/concatenate | solution.py:855
  911.1 138.6 %reduce_grads.1 = (f32[4,32,1664]{2,1,0:T(8,128)}, f32[2,64,1024]{2,1,0:T(8,128)}, f32[4,32,5120]{2,1,0:T(8,128)}, f32[2,160,1024]{2,1,0:T(8,128)}) custom-call(bf16[4,2,2,2,32,1664]{5,4,3,2,1,0:T(8,128)(2,1)} %bitcast.1227, bf16[4,2,2,64,1024]{4,3,2,1,0:T(8,128)(2,1)} %bitcast.1247, bf16[4,2,2,2,32,5120]{5,4,3,2,1,0:T(8,128)(2,1)} %bitcast.1214, ...), custom_call_target="tpu_custom_call" | custom-call | tf_op jit(solution)/shard_map/reduce_grads/pallas_call | solution.py:807
  1062.9 49.3 %scatter_fusion.5 = f32[2,256,960]{2,1,0:T(8,128)S(1)} fusion(f32[2,256,960]{2,1,0:T(8,128)S(1)} %copy-done.4, s32[512]{0:T(512)S(1)} %bitcast.1170, f32[512,960]{1,0:T(8,128)} %bitcast.1241), kind=kCustom, calls=%fused_computation.12 | custom fusion | bytes 5902336 | tf_op jit(solution)/shard_map/vmap()/scatter | solution.py:72
  (978 shorter events, 468.8 us)
Async XLA Ops:
  7.2 184.8 %all-gather.5.cloned.1.call-start = ((), (), s32[]{:S(2)}) async-start(), calls=%async_computation.6 | async-start | bytes 1638400 | tf_op jit(solution)/shard_map/all_gather | solution.py:117
  110.6 35.0 %copy-start.179 = (s32[2,1024]{1,0:T(2,128)}, s32[2,1024]{1,0:T(2,128)S(1)}, u32[]{:S(2)}) copy-start(s32[2,1024]{1,0:T(2,128)S(1)} %compare_select_fusion.5) | copy-start | bytes 24580
  111.4 38.5 %copy-start.189 = (f32[2,256]{1,0:T(2,128)}, f32[2,256]{1,0:T(2,128)S(1)}, u32[]{:S(2)}) copy-start(f32[2,256]{1,0:T(2,128)S(1)} %get-tuple-element.273) | copy-start | bytes 6148
  114.1 65.2 %copy-start.77 = (f32[2,256,64]{1,2,0:T(8,128)}, f32[2,256,64]{1,2,0:T(8,128)S(1)}, u32[]{:S(2)}) copy-start(f32[2,256,64]{1,2,0:T(8,128)S(1)} %get-tuple-element.271) | copy-start | bytes 393220
  114.2 65.1 %copy-start.79 = (f32[2,256,64]{1,2,0:T(8,128)}, f32[2,256,64]{1,2,0:T(8,128)S(1)}, u32[]{:S(2)}) copy-start(f32[2,256,64]{1,2,0:T(8,128)S(1)} %get-tuple-element.270) | copy-start | bytes 393220
  115.0 106.4 %all-gather.3.cloned.1.call-start = ((), (), s32[]{:S(2)}) async-start(), calls=%async_computation.5 | async-start | bytes 1638400 | tf_op jit(solution)/shard_map/all_gather | solution.py:118
  117.6 381.7 %all-reduce.11.cloned.1.call-start = ((), (), s32[]{:S(2)}) async-start(), calls=%async_computation.12 | async-start | bytes 786432
  145.6 114.0 %copy-start.8 = (s32[1,2,2,128]{3,1,2,0:T(2,128)}, s32[1,2,2,128]{3,1,2,0:T(2,128)S(1)}, u32[]{:S(2)}) copy-start(s32[1,2,2,128]{3,1,2,0:T(2,128)S(1)} %copy.596) | copy-start | bytes 6148
  167.2 437.0 %copy-start.99 = (f32[2,128,64]{1,2,0:T(8,128)}, f32[2,128,64]{1,2,0:T(8,128)S(1)}, u32[]{:S(2)}) copy-start(f32[2,128,64]{1,2,0:T(8,128)S(1)} %get-tuple-element.281) | copy-start | bytes 196612
  167.2 437.3 %copy-start.97 = (f32[2,128,64]{1,2,0:T(8,128)}, f32[2,128,64]{1,2,0:T(8,128)S(1)}, u32[]{:S(2)}) copy-start(f32[2,128,64]{1,2,0:T(8,128)S(1)} %get-tuple-element.280) | copy-start | bytes 196612
  167.9 17.9 %copy-start.18 = (s32[128]{0:T(128)}, s32[128]{0:T(128)S(1)}, u32[]{:S(2)}) copy-start(s32[128]{0:T(128)S(1)} %reshape.1773) | copy-start | bytes 1540
  221.4 15.6 %copy-start.47 = (bf16[8,120,1024]{2,1,0:T(8,128)(2,1)S(1)}, bf16[8,120,1024]{2,1,0:T(8,128)(2,1)}, u32[]{:S(2)}) copy-start(bf16[8,120,1024]{2,1,0:T(8,128)(2,1)} %slice.479) | copy-start | bytes 5898244
  221.4 15.6 %copy-start.202 = (f32[960]{0:T(1024)S(1)}, f32[960]{0:T(1024)}, u32[]{:S(2)}) copy-start(f32[960]{0:T(1024)} %get-tuple-element.154) | copy-start | bytes 11524
  321.8 16.4 %copy-start.38 = (f32[2,128,960]{1,2,0:T(8,128)}, f32[2,128,960]{1,2,0:T(8,128)S(1)}, u32[]{:S(2)}) copy-start(f32[2,128,960]{1,2,0:T(8,128)S(1)} %fusion.81) | copy-start | bytes 2949124
  375.0 149.3 %copy-start.210 = (f32[2,64]{1,0:T(2,128)}, f32[2,64]{1,0:T(2,128)S(1)}, u32[]{:S(2)}) copy-start(f32[2,64]{1,0:T(2,128)S(1)} %get-tuple-element.291) | copy-start | bytes 1540
  375.8 124.9 %copy-start.67 = (bf16[2,64,960]{2,1,0:T(8,128)(2,1)}, bf16[2,64,960]{2,1,0:T(8,128)(2,1)S(1)}, u32[]{:S(2)}) copy-start(bf16[2,64,960]{2,1,0:T(8,128)(2,1)S(1)} %multiply_convert_fusion.12) | copy-start | bytes 737284
  466.8 55.9 %reduce-scatter.10.cloned.1.call-start = ((), (), s32[]{:S(2)}) async-start(), calls=%async_computation.7 | async-start | bytes 491520 | tf_op jit(solution)/shard_map/reduce_scatter | solution.py:321
  479.2 160.3 %reduce-scatter.16.cloned.1.call-start = ((), (), s32[]{:S(2)}) async-start(), calls=%async_computation.10 | async-start | bytes 819200
  481.1 19.4 %copy-start.120 = (f32[2,64,64]{1,2,0:T(8,128)S(1)}, f32[2,64,64]{1,2,0:T(8,128)}, u32[]{:S(2)}) copy-start(f32[2,64,64]{1,2,0:T(8,128)} %copy-done.117) | copy-start | bytes 98308
  481.1 19.5 %copy-start.123 = (f32[2,64,64]{1,2,0:T(8,128)S(1)}, f32[2,64,64]{1,2,0:T(8,128)}, u32[]{:S(2)}) copy-start(f32[2,64,64]{1,2,0:T(8,128)} %copy-done.121) | copy-start | bytes 98308
  608.4 48.2 %reduce-scatter.18.cloned.1.call-start = ((), (), s32[]{:S(2)}) async-start(), calls=%async_computation.11 | async-start | bytes 819200
  631.5 247.4 %reduce-scatter.12.cloned.1.call-start = ((), (), s32[]{:S(2)}) async-start(), calls=%async_computation.8 | async-start | bytes 1638400 | tf_op jit(solution)/shard_map/reduce_scatter | solution.py:315
  642.6 19.0 %copy-start.207 = (f32[2,128]{1,0:T(2,128)S(1)}, f32[2,128]{1,0:T(2,128)}, u32[]{:S(2)}) copy-start(f32[2,128]{1,0:T(2,128)} %copy-done.206) | copy-start | bytes 3076
  642.7 21.4 %copy-start.126 = (bf16[2,128,320]{1,2,0:T(8,128)(2,1)}, bf16[2,128,320]{1,2,0:T(8,128)(2,1)S(1)}, u32[]{:S(2)}) copy-start(bf16[2,128,320]{1,2,0:T(8,128)(2,1)S(1)} %fusion.237) | copy-start | bytes 491524
  668.0 14.7 %copy-start.16 = (s32[1,2,2,128]{3,1,2,0:T(2,128)S(1)}, s32[1,2,2,128]{3,1,2,0:T(2,128)}, u32[]{:S(2)}) copy-start(s32[1,2,2,128]{3,1,2,0:T(2,128)} %copy.600) | copy-start | bytes 6148
  787.5 101.6 %reduce-scatter.14.cloned.1.call-start = ((), (), s32[]{:S(2)}) async-start(), calls=%async_computation.9 | async-start | bytes 1638400 | tf_op jit(solution)/shard_map/reduce_scatter | solution.py:321
  839.7 18.0 %slice-start.12 = ((s8[9830400]{0:T(1024)(128)(4,1)}), s8[4194304]{0:T(1024)(128)(4,1)S(1)}, s32[]{:S(2)}) async-start(s8[9830400]{0:T(1024)(128)(4,1)} %bitcast.1212), calls=%async_computation.25 | async-start | bytes 8388608
  911.1 144.3 %copy-start.193 = (f32[2,256]{1,0:T(2,128)S(1)}, f32[2,256]{1,0:T(2,128)}, u32[]{:S(2)}) copy-start(f32[2,256]{1,0:T(2,128)} %copy-done.191) | copy-start | bytes 6148
  911.1 144.3 %copy-start.198 = (f32[2,256]{1,0:T(2,128)S(1)}, f32[2,256]{1,0:T(2,128)}, u32[]{:S(2)}) copy-start(f32[2,256]{1,0:T(2,128)} %get-tuple-element.274) | copy-start | bytes 6148
  911.1 144.4 %copy-start.200 = (f32[2,256]{1,0:T(2,128)S(1)}, f32[2,256]{1,0:T(2,128)}, u32[]{:S(2)}) copy-start(f32[2,256]{1,0:T(2,128)} %copy-done.199) | copy-start | bytes 6148
  911.1 144.4 %copy-start.203 = (f32[960]{0:T(1024)S(1)}, f32[960]{0:T(1024)}, u32[]{:S(2)}) copy-start(f32[960]{0:T(1024)} %get-tuple-element.154) | copy-start | bytes 11524
  911.1 144.4 %copy-start.249 = (f32[2,256]{1,0:T(2,128)S(1)}, f32[2,256]{1,0:T(2,128)}, u32[]{:S(2)}) copy-start(f32[2,256]{1,0:T(2,128)} %get-tuple-element.272) | copy-start | bytes 6148
  (266 other events, 1151.4 us)
Sparse Core Ops, SparseCore 0:
  115.2 18.2 all-gather.4
  135.6 18.2 all-gather.2
  466.9 32.3 all-reduce.10
  501.9 20.8 reduce-scatter.9
  608.5 23.0 reduce-scatter.15
  634.1 22.4 reduce-scatter.17
  787.6 26.5 reduce-scatter.11
  839.8 26.7 reduce-scatter.13

commit v2 on v1

v2 whole, which is shorter than its diff:
```python
import functools
import math
import types

import jax
import jax.numpy as jnp
import numpy as np
from jax import lax
from jax.experimental import pallas as pl
from jax.experimental.pallas import tpu as pltpu
from jax.sharding import PartitionSpec as P

HEADS, KV_HEADS, HEAD_DIM, RECUR = 15, 5, 64, 3
GROUP = HEADS // KV_HEADS
eps = 1e-05
rope_base = 10000.0
masked_fill = -1e30
BF, F32 = jnp.bfloat16, jnp.float32
COLS_A = 1664
FT = 512


def dot(a, b):
    return lax.dot_general(a, b, (((1,), (0,)), ((), ())), preferred_element_type=F32)


def dot_nt(a, b):
    return lax.dot_general(a, b, (((1,), (1,)), ((), ())), preferred_element_type=F32)


def dot_tn(a, b):
    return lax.dot_general(a, b, (((0,), (0,)), ((), ())), preferred_element_type=F32)


def halves(v):
    high = v.astype(BF)
    return high, (v - high.astype(F32)).astype(BF)


def pick(choice, v):
    high, low = halves(v)
    return dot(choice, high) + dot(choice, low)


def put_back(choice, v):
    high, low = halves(v)
    return dot_tn(choice, high) + dot_tn(choice, low)


def lanes(shape):
    return lax.broadcasted_iota(jnp.int32, shape, len(shape) - 1)


def rowid(shape):
    return lax.broadcasted_iota(jnp.int32, shape, len(shape) - 2)


def swapped(x):
    first = lax.rem(lanes(x.shape), 64) < 32
    return jnp.where(first, pltpu.roll(x, 96, 1), pltpu.roll(x, 32, 1))


def call(name, body, ins, outs, scratch=None, limit=63, hbm=()):
    scratch = scratch or {}
    names = list(ins) + list(outs) + list(scratch)

    def kernel(*refs):
        body(types.SimpleNamespace(**dict(zip(names, refs))))

    vm, anyw = pl.BlockSpec(memory_space=pltpu.VMEM), pl.BlockSpec(memory_space=pl.ANY)
    got = pl.pallas_call(
        kernel,
        out_shape=[jax.ShapeDtypeStruct(s, d) for s, d in outs.values()],
        in_specs=[anyw if k in hbm else pl.BlockSpec(memory_space=pltpu.SMEM) if k == "lens" else vm for k in ins],
        out_specs=[anyw if k in hbm else vm for k in outs],
        scratch_shapes=list(scratch.values()),
        compiler_params=pltpu.CompilerParams(vmem_limit_bytes=limit << 20),
        name=name,
    )(*ins.values())
    return dict(zip(outs, got))


class Geo:
    def __init__(self, ns, bl, n_dp, n_blk, d, ff, tops):
        self.ns, self.bl, self.n_dp, self.n_blk, self.d, self.ff = ns, bl, n_dp, n_blk, d, ff
        self.gw = d // n_dp
        self.gp = -(-self.gw // 16) * 16
        self.dp = n_dp * self.gp
        self.slots = (bl, bl // 2, bl // 4)
        self.tops = tops

    def rows(self, r):
        return self.ns * self.slots[r]

    def keys(self, r):
        return self.n_blk * self.slots[r]

    def spread(self):
        e = np.zeros((1024, self.dp), np.float32)
        f = np.arange(self.d)
        e[f, f // self.gw * self.gp + f % self.gw] = 1
        return jnp.asarray(e, BF)

    def tables(self):
        f = rope_base ** (-(np.arange(32, dtype=np.float64) * 2.0) / 64)
        f32 = np.asarray(f, np.float32)
        ph = (np.arange(self.bl * self.n_blk, dtype=np.float32)[:, None] * f32).astype(np.float32).astype(np.float64)
        c, s = np.cos(ph), np.sin(ph)
        cos = np.concatenate([c, c, c, c], 1).astype(np.float32)
        sin = np.concatenate([-s, s, -s, s], 1).astype(np.float32)
        return jnp.asarray(cos), jnp.asarray(sin)


def gains(wa):
    sel = (lanes((8, 128)) == rowid((8, 128)) + 64).astype(BF)
    return dot_nt(sel, wa[:, 896:1024])


def choose(geo, r, routes, blk):
    s, t, bl = geo.slots[r], geo.tops[r], geo.bl
    before = jnp.sum((routes < blk * bl).astype(F32), axis=1, keepdims=True).astype(jnp.int32)
    shift = ((lanes((s, t)) - rowid((s, t))) == before).astype(BF)
    here = (routes == rowid((bl, t)) + blk * bl).astype(BF)
    return dot_nt(shift, here).astype(BF)


def allowed(geo, r, routes, blk, turned):
    s, kn, bl = geo.slots[r], geo.keys(r), geo.bl
    shape = (kn, s) if turned else (s, kn)
    key = rowid(shape) if turned else lanes(shape)
    query = lanes(shape) if turned else rowid(shape)
    ok = key <= blk * s + query
    if r > 0:
        t = geo.tops[r]
        inside = (routes // bl == rowid((kn, t)) // s)
        if turned:
            count = jnp.sum(inside.astype(F32), axis=1, keepdims=True)
        else:
            count = dot_nt(jnp.ones((8, t), BF), inside.astype(BF))[0:1]
        ok = ok & (lax.rem(key, s).astype(F32) < count)
    return jnp.where(ok, 0.0, masked_fill)


def project(geo, r, k):
    a = k.a[...].astype(F32)
    n1 = lax.rsqrt(jnp.sum(a * a, axis=-1, keepdims=True) * (1.0 / geo.d) + eps)
    k.u[...] = (a * n1 * k.gn[0:1]).astype(BF)
    k.st[...] = jnp.where(lanes(k.st.shape) == 0, n1, 0.0)
    u = k.u[...]
    cos, sin = k.cos[...], k.sin[...]
    left = lanes(cos.shape) < 64
    for t in range(4):
        both = dot(u, k.wa[:, 256 * t:256 * t + 256])
        for j in range(2):
            x = both[:, 128 * j:128 * j + 128]
            x = (x * cos + swapped(x) * sin).astype(BF).astype(F32) * 0.125
            h = 4 * t + 2 * j
            k.q16[h] = jnp.where(left, x, 0.0).astype(BF)
            if h + 1 < HEADS:
                k.q16[h + 1] = jnp.where(left, pltpu.roll(x, 64, 1), 0.0).astype(BF)
    ckv, skv = jnp.where(left, cos, 1.0), jnp.where(left, sin, 0.0)
    for c0, n in ((1024, 256), (1280, 256), (1536, 128)):
        some = dot(u, k.wa[:, c0:c0 + n])
        for j in range(n // 128):
            x = some[:, 128 * j:128 * j + 128]
            k.kv[:, c0 - 1024 + 128 * j:c0 - 1024 + 128 * j + 128] = (x * ckv + swapped(x) * skv).astype(BF)


def select_rows(geo, r, k, blk):
    s, bl = geo.slots[r], geo.bl
    for m in range(geo.ns):
        ch = choose(geo, r, k.routes[m:m + 1], blk)
        k.choice[m] = ch
        k.a[m * s:m * s + s] = pick(ch, k.h[m * bl:m * bl + bl])
        k.cos[m * s:m * s + s] = pick(ch, k.cosb[...])
        k.sin[m * s:m * s + s] = pick(ch, k.sinb[...])


def attend(geo, r, k, blk):
    s, kn = geo.slots[r], geo.keys(r)

    def seq(m, _):
        kv = k.kvall[:, m]
        k.kvg[...] = kv.reshape(kn, KV_HEADS * 128)
        k.bias[...] = allowed(geo, r, k.routes[pl.ds(m, 1)] if r else None, blk, False)
        row0 = pl.multiple_of(m * s, s)
        k.col[...] = jnp.zeros(k.col.shape, F32)

        def head(h, _):
            kvh = k.kvg[:, pl.ds(pl.multiple_of(h // GROUP * 128, 128), 128)]
            sc = dot_nt(k.q16[h, pl.ds(row0, s)], kvh) + k.bias[...]
            top = jnp.max(sc, axis=-1, keepdims=True)
            p = jnp.exp(sc - top)
            total = jnp.sum(p, axis=-1, keepdims=True)
            o2 = dot(p.astype(BF), kvh) * (1.0 / total)
            k.o16[h] = o2
            k.col[...] = jnp.where(lanes(k.col.shape) == h, top + jnp.log(total), k.col[...])
            return 0
        lax.fori_loop(0, HEADS, head, 0)
        left = lanes((s, 128)) < 64
        for t in range(8):
            odd = k.o16[2 * t + 1] if 2 * t + 1 < HEADS else 0.0
            k.o[pl.ds(row0, s), 128 * t:128 * t + 128] = jnp.where(left, pltpu.roll(k.o16[2 * t], 64, 1), odd).astype(BF)
        k.lse[m] = k.col[...].T[0:16]
        return 0
    lax.fori_loop(0, geo.ns, seq, 0)


class Tiles:
    def __init__(self, geo, k, pre=None):
        self.k, self.n, self.ff, self.pre = k, geo.ff // FT, geo.ff, pre

    def parts(self, t, slot):
        k, c0 = self.k, t * FT
        if not isinstance(t, int):
            c0 = pl.multiple_of(c0, FT)
        cu = c0 + self.ff
        return [pltpu.make_async_copy(k.gu.at[:, pl.ds(c0, FT)], k.gbuf.at[slot], k.tsem.at[slot, 0]),
                pltpu.make_async_copy(k.gu.at[:, pl.ds(cu, FT)], k.ubuf.at[slot], k.tsem.at[slot, 1]),
                pltpu.make_async_copy(k.wd.at[pl.ds(c0, FT)], k.dbuf.at[slot], k.tsem.at[slot, 2])] + [
                    pltpu.make_async_copy(v.at[:, pl.ds(c0, FT)], k.pre.at[slot, j], k.tsem.at[slot, 3 + j])
                    for j, v in enumerate(self.pre or ())]

    def start(self, t, slot):
        for c in self.parts(t, slot):
            c.start()

    def loop(self, step):
        def body(t, _):
            slot = lax.rem(t, 2)

            @pl.when(t + 1 < self.n)
            def _():
                self.start(t + 1, 1 - slot)
            for c in self.parts(t, slot):
                c.wait()
            step(t, slot)
            return 0
        lax.fori_loop(0, self.n, body, 0)

    @staticmethod
    def scratch(geo):
        return dict(gbuf=pltpu.VMEM((2, geo.dp, FT), BF), ubuf=pltpu.VMEM((2, geo.dp, FT), BF),
                    dbuf=pltpu.VMEM((2, FT, geo.dp), BF), tsem=pltpu.SemaphoreType.DMA((2, 5)))


def feed(geo, r, k, blk, tiles):
    s, bl = geo.slots[r], geo.bl
    y = dot(k.o[...], k.wou[...])
    a = k.a[...].astype(F32)
    b = a + y
    n2 = lax.rsqrt(jnp.sum(b * b, axis=-1, keepdims=True) * (1.0 / geo.d) + eps)
    gate = jax.nn.sigmoid(jnp.sum(a * k.gn[2 + r:3 + r], axis=-1, keepdims=True))
    k.b[...] = b.astype(BF)
    k.w[...] = (b * n2 * k.gn[1:2]).astype(BF)
    lane = lanes((geo.rows(r), 128))
    k.sx[...] = jnp.where(lane == 0, n2, jnp.where(lane == 1, gate, 0.0))
    k.acc[...] = y

    def wide(t, slot):
        c0 = t * FT if isinstance(t, int) else pl.multiple_of(t * FT, FT)
        return [pltpu.make_async_copy(k.keep.at[slot, j], ref.at[:, pl.ds(c0, FT)], k.ksem.at[slot, j])
                for j, ref in enumerate((k.gp, k.up))]

    def step(t, slot):
        @pl.when(t >= 2)
        def _():
            for c in wide(t - 2, slot):
                c.wait()
        gp = dot(k.w[...], k.gbuf[slot])
        up = dot(k.w[...], k.ubuf[slot])
        k.keep[slot, 0] = gp.astype(BF)
        k.keep[slot, 1] = up.astype(BF)
        z = (gp * jax.nn.sigmoid(gp) * up).astype(BF)
        k.acc[...] += dot(z, k.dbuf[slot])
        for c in wide(t, slot):
            c.start()
    tiles.loop(step)
    for t in range(max(tiles.n - 2, 0), tiles.n):
        for c in wide(t, t % 2):
            c.wait()
    yf = k.acc[...]
    k.yf[...] = yf.astype(BF)
    delta = yf * k.sx[:, 1:2]
    for m in range(geo.ns):
        if r == 0:
            here = rowid((bl, 1)) + blk * bl < k.lens[m]
            rows = slice(m * bl, m * bl + bl)
            k.h2[rows] = k.a[rows].astype(F32) + jnp.where(here, delta[rows], 0.0)
        else:
            k.h2[m * bl:m * bl + bl] = k.h[m * bl:m * bl + bl] + put_back(k.choice[m], delta[m * s:m * s + s])


def back_feed(geo, r, k, blk, tiles):
    s, bl, rows = geo.slots[r], geo.bl, geo.rows(r)
    k.small[2 + r:3 + r] = jnp.zeros((1, geo.dp), F32)
    k.small[1:2] = jnp.zeros((1, geo.dp), F32)

    def incoming(m):
        here = slice(m * s, m * s + s)
        if r == 0:
            return jnp.where(rowid((bl, 1)) + blk * bl < k.lens[m], k.dh[here], 0.0)
        return k.inc[here]
    for m in range(geo.ns):
        here = slice(m * s, m * s + s)
        if r > 0:
            k.inc[here] = pick(k.choice[m], k.dh[m * bl:m * bl + bl])
        inc = incoming(m)
        gate = k.sx[here, 1:2]
        dg = jnp.sum(inc * k.yf[here].astype(F32), axis=-1, keepdims=True)
        dl = dg * gate * (1.0 - gate)
        k.tok[here] = inc + dl * k.gn[2 + r:3 + r]
        k.small[2 + r:3 + r] += jnp.sum(k.a[here].astype(F32) * dl, axis=0, keepdims=True)
        k.df[here] = (gate * inc).astype(BF)
    k.acc[...] = jnp.zeros(k.acc.shape, F32)

    def wide(t, slot):
        c0 = t * FT if isinstance(t, int) else pl.multiple_of(t * FT, FT)
        return [pltpu.make_async_copy(k.wide.at[slot, j], ref.at[:, pl.ds(c0, FT)], k.wsem.at[slot, j])
                for j, ref in enumerate((k.dgp, k.dup, k.z))]

    def step(t, slot):
        @pl.when(t >= 2)
        def _():
            for c in wide(t - 2, slot):
                c.wait()
        dz = dot_nt(k.df[...], k.dbuf[slot])
        gp = k.pre[slot, 0].astype(F32)
        up = k.pre[slot, 1].astype(F32)
        sig = jax.nn.sigmoid(gp)
        silu = gp * sig
        k.wide[slot, 2] = (silu * up).astype(BF)
        dup = (dz * silu).astype(BF)
        dgp = (dz * up * (sig * (1.0 + gp * (1.0 - sig)))).astype(BF)
        k.wide[slot, 1] = dup
        k.wide[slot, 0] = dgp
        k.acc[...] += dot_nt(dgp, k.gbuf[slot]) + dot_nt(dup, k.ubuf[slot])
        for c in wide(t, slot):
            c.start()
    tiles.loop(step)
    for t in range(max(tiles.n - 2, 0), tiles.n):
        for c in wide(t, t % 2):
            c.wait()
    for m in range(geo.ns):
        here = slice(m * s, m * s + s)
        n2, gate = k.sx[here, 0:1], k.sx[here, 1:2]
        dw = k.acc[here]
        b = k.b[here].astype(F32)
        k.small[1:2] += jnp.sum(dw * (b * n2), axis=0, keepdims=True)
        t = dw * k.gn[1:2]
        db = n2 * t - n2 * n2 * n2 * b * (jnp.sum(t * b, axis=-1, keepdims=True) * (1.0 / geo.d))
        k.tok[here] += db
        k.dy[here] = (gate * incoming(m) + db).astype(BF)


def back_attend(geo, r, k, blk):
    s, kn = geo.slots[r], geo.keys(r)
    rows = geo.rows(r)
    left = lanes((rows, 128)) < 64
    lane = lanes((rows, 128))
    dcol = jnp.zeros((rows, 128), F32)
    for t in range(8):
        x = dot_nt(k.dy[...], k.wou[128 * t:128 * t + 128])
        x = x.astype(BF).astype(F32)
        prod = x * k.o[:, 128 * t:128 * t + 128].astype(F32)
        even = jnp.sum(jnp.where(left, prod, 0.0), axis=-1, keepdims=True)
        dcol = jnp.where(lane == 2 * t, even, dcol)
        k.do16[2 * t] = jnp.where(left, 0.0, pltpu.roll(x, 64, 1)).astype(BF)
        if 2 * t + 1 < HEADS:
            odd = jnp.sum(jnp.where(left, 0.0, prod), axis=-1, keepdims=True)
            dcol = jnp.where(lane == 2 * t + 1, odd, dcol)
            k.do16[2 * t + 1] = jnp.where(left, 0.0, x).astype(BF)
    k.dcol[...] = dcol

    def seq(m, _):
        row0 = pl.multiple_of(m * s, s)
        k.kvg[...] = k.kvall[:, m].reshape(kn, KV_HEADS * 128)
        for g in range(KV_HEADS):
            k.kvt[g] = k.kvg[:, 128 * g:128 * g + 128].astype(F32).T.astype(BF)
        k.bias[...] = allowed(geo, r, k.routes[pl.ds(m, 1)] if r else None, blk, True)
        k.dt[...] = k.dcol[pl.ds(row0, s)].T[0:16]
        k.ct[0] = k.cos[pl.ds(row0, s)].T[0:32] * 0.125
        k.ct[1] = k.sin[pl.ds(row0, s)].T[32:64] * 0.125

        def group(g, _):
            kvh = k.kvg[:, pl.ds(pl.multiple_of(g * 128, 128), 128)]
            total = None
            for j in range(GROUP):
                h = g * GROUP + j
                qh, doh = k.q16[h, pl.ds(row0, s)], k.do16[h, pl.ds(row0, s)]
                p = jnp.exp(dot_nt(kvh, qh) + k.bias[...] - k.lse[m, pl.ds(h, 1)])
                ds = (p * (dot_nt(kvh, doh) - k.dt[pl.ds(h, 1)])).astype(BF)
                part = dot(ds, qh) + dot(p.astype(BF), doh)
                total = part if total is None else total + part
                dqt = dot(k.kvt[g], ds)
                y1, y2 = dqt[0:32], dqt[32:64]
                c, sn = k.ct[0], k.ct[1]
                k.dqt[h, 0:32] = (y1 * c + y2 * sn)
                k.dqt[h, 32:64] = (y2 * c - y1 * sn)
            k.dkv[:, m, :, pl.ds(pl.multiple_of(g * 128, 128), 128)] = total.astype(BF).reshape(geo.n_blk, s, 128)
            return 0
        lax.fori_loop(0, KV_HEADS, group, 0)
        for t in range(8):
            if 2 * t + 1 < HEADS:
                x = k.dqt[2 * t:2 * t + 2].reshape(128, s).T
            else:
                x = jnp.concatenate([k.dqt[2 * t], jnp.zeros((64, s), F32)], axis=0).T
            k.da[pl.ds(row0, s), 128 * t:128 * t + 128] = x.astype(BF)
        return 0
    lax.fori_loop(0, geo.ns, seq, 0)


def back_project(geo, r, k, blk):
    s, bl, rows = geo.slots[r], geo.bl, geo.rows(r)
    cos, sin = k.cos[...], k.sin[...]
    left = lanes(cos.shape) < 64
    ckv, skv = jnp.where(left, cos, 1.0), jnp.where(left, sin, 0.0)
    k.da2[:, 0:1024] = k.da[...]
    for g in range(KV_HEADS):
        x = k.dkvown[:, 128 * g:128 * g + 128].astype(F32)
        k.da2[:, 1024 + 128 * g:1152 + 128 * g] = (x * ckv - swapped(x) * skv).astype(BF)
    for m in range(geo.ns):
        here = slice(m * bl, m * bl + bl)
        mine = slice(m * s, m * s + s)
        du = dot_nt(k.da2[mine], k.wa[...])
        a = k.a[mine].astype(F32)
        n1 = k.st[mine, 0:1]
        k.first[0:1] += jnp.sum(du * (a * n1), axis=0, keepdims=True)
        t1 = du * k.gn[0:1]
        tok = k.tok[mine] + n1 * t1 - n1 * n1 * n1 * a * (jnp.sum(t1 * a, axis=-1, keepdims=True) * (1.0 / geo.d))
        if r == 0:
            ok = rowid((bl, 1)) + blk * bl < k.lens[m]
            k.dh2[here] = jnp.where(ok, tok, k.dh[here])
        else:
            k.dh2[here] = k.dh[here] + put_back(k.choice[m], tok - k.inc[mine])


def ns(**kw):
    return types.SimpleNamespace(**kw)


def block(geo, x, cot, lens, routes, wa, wo, gu, wd, share, give_back):
    blk_of = lambda: lax.axis_index("blk")
    bl, d, dp, ff, nsq, nb = geo.bl, geo.d, geo.dp, geo.ff, geo.ns, geo.n_blk
    full = nsq * bl
    cos_all, sin_all = geo.tables()
    b0 = lax.axis_index("blk") * bl
    cosb = lax.dynamic_slice_in_dim(cos_all, b0, bl, 0)
    sinb = lax.dynamic_slice_in_dim(sin_all, b0, bl, 0)
    spread = geo.spread()
    R, S, KN = [geo.rows(r) for r in range(3)], geo.slots, [geo.keys(r) for r in range(3)]
    V = pltpu.VMEM

    def proj_outs(r):
        return {f"a{r}": ((R[r], dp), BF if r == 0 else F32), f"u{r}": ((R[r], dp), BF), f"q16{r}": ((HEADS, R[r], 128), BF),
                f"kv{r}": ((R[r], 640), BF), f"st{r}": ((R[r], 128), F32),
                f"cos{r}": ((R[r], 128), F32), f"sin{r}": ((R[r], 128), F32)}

    def feed_outs(r):
        return {f"o{r}": ((R[r], 1024), BF), f"lse{r}": ((nsq, 16, S[r]), F32), f"b{r}": ((R[r], dp), BF),
                f"w{r}": ((R[r], dp), BF), f"gp{r}": ((R[r], ff), BF), f"up{r}": ((R[r], ff), BF),
                f"yf{r}": ((R[r], dp), BF), f"sx{r}": ((R[r], 128), F32), f"h{r + 1}": ((full, dp), F32)}

    def attn_scratch(r):
        return dict(kvg=V((KN[r], 640), BF), bias=V((S[r], KN[r]), F32), col=V((S[r], 128), F32),
                    o16=V((HEADS, S[r], 128), F32), acc=V((R[r], dp), F32), keep=V((2, 2, R[r], FT), BF),
                    ksem=pltpu.SemaphoreType.DMA((2, 2)))

    def view(k, r, **more):
        names = ("a", "u", "q16", "kv", "st", "cos", "sin", "o", "lse", "b", "w", "gp", "up", "yf", "sx", "kvall", "routes",
                 "choice", "df", "dgp", "dup", "z", "dy", "tok", "inc", "da", "da2", "dkv", "dkvown")
        out = {n: getattr(k, f"{n}{r}") for n in names if hasattr(k, f"{n}{r}")}
        for n, v in vars(k).items():
            out.setdefault(n, v)
        out.update(more)
        return types.SimpleNamespace(**out)

    env = {}

    def need(*names):
        return {n: env[n] for n in names}

    def k_first(k):
        k.gn = gains(k.wa)
        k.a0[...] = dot(k.x[...], k.spread[0:d]).astype(BF)
        for m in range(nsq):
            k.cos0[m * bl:m * bl + bl] = k.cosb[...]
            k.sin0[m * bl:m * bl + bl] = k.sinb[...]
        project(geo, 0, view(k, 0))

    env.update(x=x, cot=cot, lens=lens, routes1=routes[0], routes2=routes[1], wa=wa, wo=wo, gu=gu, wd=wd, spread=spread,
               cosb=cosb, sinb=sinb)
    env.update(call("first_project", k_first, need("x", "spread", "wa", "cosb", "sinb"), proj_outs(0)))
    env["kvall0"] = share(env["kv0"].reshape(nsq, S[0], 640))

    def k_mid(r, k):
        blk = blk_of()
        tiles = Tiles(geo, k)
        tiles.start(0, 0)
        k.gn = gains(k.wa)
        if r == 0:
            k.wou[...] = dot(k.spread[...], k.wo[...]).astype(BF)
        v = view(k, r, h=getattr(k, f"h{r}", None), h2=getattr(k, f"h{r + 1}"))
        attend(geo, r, v, blk)
        feed(geo, r, v, blk, tiles)
        n = view(k, r + 1, h=getattr(k, f"h{r + 1}"))
        select_rows(geo, r + 1, n, blk)
        project(geo, r + 1, n)

    for r in range(2):
        ins = need("wa", "gu", "wd", f"a{r}", f"q16{r}", f"kvall{r}", "cosb", "sinb", f"routes{r + 1}",
                   *(("wo", "spread", "lens") if r == 0 else ("wou", f"routes{r}", f"choice{r}", f"h{r}")))
        outs = {**feed_outs(r), **proj_outs(r + 1), f"choice{r + 1}": ((nsq, S[r + 1], bl), BF)}
        if r == 0:
            outs["wou"] = ((1024, dp), BF)
        env.update(call(f"forward_{r}", functools.partial(k_mid, r), ins, outs, {**attn_scratch(r), **Tiles.scratch(geo)},
                        hbm=("gu", "wd", f"gp{r}", f"up{r}")))
        env[f"kvall{r + 1}"] = share(env[f"kv{r + 1}"].reshape(nsq, S[r + 1], 640))

    def back_outs(r):
        more = {f"inc{r}": ((R[r], dp), F32), **attend_outs(r)} if r else {}
        return {**more, f"tok{r}": ((R[r], dp), F32), f"df{r}": ((R[r], dp), BF),
                f"dgp{r}": ((R[r], ff), BF), f"dup{r}": ((R[r], ff), BF), f"z{r}": ((R[r], ff), BF),
                f"dy{r}": ((R[r], dp), BF), f"small{r}": ((8, dp), F32)}

    def attend_outs(r):
        return {f"da{r}": ((R[r], 1024), BF), f"dkv{r}": ((nb, nsq, S[r], 640), BF)}

    def back_scratch(r):
        return {**feed_scratch(r), **(turned_scratch(r) if r else {})}

    def turned_scratch(r):
        return dict(kvg=V((KN[r], 640), BF), kvt=V((KV_HEADS, 128, KN[r]), BF), bias=V((KN[r], S[r]), F32),
                    dcol=V((R[r], 128), F32), dt=V((16, S[r]), F32), ct=V((2, 32, S[r]), F32),
                    do16=V((HEADS, R[r], 128), BF), dqt=V((HEADS, 64, S[r]), F32))

    def feed_scratch(r):
        return dict(acc=V((R[r], dp), F32), pre=V((2, 2, R[r], FT), BF), wide=V((2, 3, R[r], FT), BF), wsem=pltpu.SemaphoreType.DMA((2, 3)))

    def back_one(r, k, blk, tiles, dh):
        v = view(k, r, dh=dh, small=getattr(k, f"small{r}"))
        v.small[...] = jnp.zeros(v.small.shape, F32)
        back_feed(geo, r, v, blk, tiles)
        if r > 0:
            back_attend(geo, r, v, blk)

    def k_turn(k):
        blk = blk_of()
        tiles = Tiles(geo, k)
        tiles.start(0, 0)
        k.gn = gains(k.wa)
        v = view(k, 2, h=k.h2, h2=k.h3, acc=k.acc)
        attend(geo, 2, v, blk)
        feed(geo, 2, v, blk, tiles)
        tiles = Tiles(geo, k, (k.gp2, k.up2))
        tiles.start(0, 0)
        k.out[...] = dot_nt(k.h3[...].astype(BF), k.spread[0:d]).astype(BF)
        k.dhe[...] = dot(k.cot[...], k.spread[0:d])
        back_one(2, view(k, 2, bias=k.biast), blk, tiles, k.dhe)

    ins = need("wa", "gu", "wd", "wou", "a2", "q162", "kvall2", "routes2", "choice2", "h2", "spread", "cot", "cos2", "sin2")
    sc = {**attn_scratch(2), **Tiles.scratch(geo)}
    bs = back_scratch(2)
    bs["biast"] = bs.pop("bias")
    outs = {**feed_outs(2), **back_outs(2), "out": ((full, d), BF), "dhe": ((full, dp), F32)}
    env.update(call("turn", k_turn, ins, outs, {**bs, **sc}, hbm=("gu", "wd", "gp2", "up2", "dgp2", "dup2", "z2")))
    env["dh3"] = env["dhe"]

    saved = ("a", "b", "gp", "up", "yf", "sx")
    kept = ("q16", "kvall", "o", "lse", "cos", "sin")
    for r in (1, 0):
        env[f"dkvown{r + 1}"] = give_back(env[f"dkv{r + 1}"]).reshape(R[r + 1], 640)

        def k_back(r, k):
            blk = blk_of()
            tiles = Tiles(geo, k, (getattr(k, f"gp{r}"), getattr(k, f"up{r}")))
            tiles.start(0, 0)
            k.gn = gains(k.wa)
            p = view(k, r + 1, a=getattr(k, f"a{r + 1}"), dh=getattr(k, f"dh{r + 2}"), dh2=getattr(k, f"dh{r + 1}"),
                     first=getattr(k, f"first{r + 1}"))
            p.first[...] = jnp.zeros(p.first.shape, F32)
            back_project(geo, r + 1, p, blk)
            back_one(r, k, blk, tiles, getattr(k, f"dh{r + 1}"))
        n = r + 1
        ins = need("wa", "gu", "wd", f"dkvown{n}", f"da{n}", f"tok{n}", f"inc{n}", f"dh{n + 1}", f"choice{n}", f"st{n}",
                   f"a{n}", f"cos{n}", f"sin{n}", *[s + str(r) for s in saved], *(("lens",) if r == 0 else ("wou", "routes1", "choice1", *[s + str(r) for s in kept])))
        outs = {**back_outs(r), f"da2{n}": ((R[n], COLS_A), BF), f"first{n}": ((8, dp), F32), f"dh{n}": ((full, dp), F32)}
        env.update(call(f"backward_{r}", functools.partial(k_back, r), ins, outs, {**back_scratch(r), **Tiles.scratch(geo)},
                        hbm=("gu", "wd", *[v + str(r) for v in ("gp", "up", "dgp", "dup", "z")])))
    env.update(call("backward_attend_0", lambda k: back_attend(geo, 0, view(k, 0), blk_of()),
                    need("wou", "dy0", *[s + "0" for s in kept]), attend_outs(0), turned_scratch(0)))
    env["dkvown0"] = give_back(env["dkv0"]).reshape(R[0], 640)

    def k_last(k):
        blk = blk_of()
        k.gn = gains(k.wa)
        k.first0[...] = jnp.zeros(k.first0.shape, F32)
        back_project(geo, 0, view(k, 0, dh=k.dh1, dh2=k.dh0, first=k.first0), blk)
        high, low = halves(k.dh0[...])
        k.grad[...] = dot_nt(high, k.spread[0:d]) + dot_nt(low, k.spread[0:d])
    ins = need("wa", "dkvown0", "da0", "tok0", "dh1", "lens", "st0", "a0", "cos0", "sin0", "spread")
    env.update(call("last_project", k_last, ins, {"da20": ((R[0], COLS_A), BF), "first0": ((8, dp), F32), "grad": ((full, d), F32)},
                    dict(dh0=V((full, dp), F32))))
    return env


def weight_grads(geo, env, h):
    R = [geo.rows(r) for r in range(3)]
    dp, ff = geo.dp, geo.ff

    def products(name, lefts, rights, width, tile, rows, spread=None, extra=None):
        ins, hbm = {}, []
        nl = len(lefts)
        for i, v in enumerate(lefts):
            ins[f"l{i}"] = v
        for j, group in enumerate(rights):
            for i, v in enumerate(group):
                ins[f"r{j}{i}"] = v
        if spread is not None:
            ins["spread"] = spread
        if extra is not None:
            ins.update(extra)
        total = sum(R)

        def body(k):
            at = 0
            for i in range(3):
                v = getattr(k, f"l{i}")
                if spread is not None:
                    k.left[at:at + R[i]] = dot(v[...], k.spread[...]).astype(BF)
                else:
                    k.left[at:at + R[i]] = v[...]
                at += R[i]
            c0 = 0
            for j in range(len(rights)):
                n = rights[j][0].shape[1]
                refs = [getattr(k, f"r{j}{i}") for i in range(3)]
                for t in range(0, n, tile):
                    w = min(tile, n - t)
                    right = jnp.concatenate([v[:, t:t + w] for v in refs], axis=0)
                    res = dot_tn(k.left[...], right)
                    k.res[:, c0 + t:c0 + t + w] = res.astype(BF)
                c0 += n
            if extra is not None:
                small = k.small0[...] + k.small1[...] + k.small2[...]
                f = k.first0[...] + k.first1[...] + k.first2[...]
                small = jnp.where(rowid(small.shape) == 0, f, small)
                cols = jnp.concatenate([small, jnp.zeros((120, dp), F32)], axis=0).T
                cols = pltpu.roll(cols, 64, 1)
                k.res[:, 896:1024] = jnp.where(lanes(cols.shape) < 64, k.res[:, 896:1024].astype(F32), cols).astype(BF)
        return call(name, body, ins, {"res": ((rows, width), BF)}, dict(left=pltpu.VMEM((total, rows), BF)))["res"]

    three = lambda n: [env[f"{n}{r}"] for r in range(3)]
    if h == "gu":
        return products("grad_gate_up", three("w"), [three("dgp"), three("dup")], 2 * ff, 512, dp)
    if h == "d":
        return products("grad_down", three("z"), [three("df")], dp, 256, ff)
    if h == "o":
        return products("grad_output", three("o"), [three("dy")], dp, 512, dp, spread=env["spread"])
    return products("grad_query_kv", three("u"), [three("da2")], COLS_A, 512, dp,
                    extra={f"{n}{r}": env[f"{n}{r}"] for n in ("small", "first") for r in range(3)})


MESH = pl.DeviceIdType.MESH

NZ, NX = 4, 2
G = NZ * NX


def gather_kernel(chunks, nslab, *refs):
    ins, outs = refs[:nslab], refs[nslab:2 * nslab]
    ls, zs, zr, xs, xr, ys, yr, cs, cr = refs[2 * nslab:]
    dp, blk = lax.axis_index("dp"), lax.axis_index("blk")
    z, x = dp // NX, lax.rem(dp, NX)
    y, c = blk // 2, lax.rem(blk, 2)
    left, right = (dp - NX, blk), (dp + NX, blk)
    xm, ym, cm = (dp + 1 - 2 * x, blk), (dp, lax.rem(blk + 2, 4)), (dp, blk + 1 - 2 * c)
    bar = pltpu.get_barrier_semaphore()
    for t in (xm, ym, cm):
        pl.semaphore_signal(bar, inc=1, device_id=t, device_id_type=MESH)

    @pl.when(z > 0)
    def _():
        pl.semaphore_signal(bar, inc=1, device_id=left, device_id_type=MESH)

    @pl.when(z < NZ - 1)
    def _():
        pl.semaphore_signal(bar, inc=1, device_id=right, device_id_type=MESH)

    pl.semaphore_wait(bar, 3 + jnp.where(z > 0, 1, 0) + jnp.where(z < NZ - 1, 1, 0))

    locs = [pltpu.make_async_copy(ins[s], outs[s].at[dp], ls.at[s]) for s in range(nslab)]
    for l in locs:
        l.start()

    def piece(i, g, q):
        s, c0, n, split = chunks[i]
        return outs[s].at[g, q, :, pl.ds(c0, n)]

    def myq(i):
        return blk if chunks[i][3] == 4 else c

    def rem(src, dst, a, b, to):
        return pltpu.make_async_remote_copy(src_ref=src, dst_ref=dst, send_sem=a, recv_sem=b, device_id=to, device_id_type=MESH)

    def own(i):
        s, c0, n, split = chunks[i]
        return ins[s].at[myq(i), :, pl.ds(c0, n)]

    def zcopy(i, d, s, src_own):
        zz = z - s if d == 0 else z + s
        p = piece(i, zz * NX + x, myq(i))
        return rem(own(i) if src_own else p, p, zs.at[i, d, s], zr.at[i, d, s], right if d == 0 else left)

    def zrecv(i, d, s):
        zz = z - 1 - s if d == 0 else z + 1 + s
        p = piece(i, zz * NX + x, myq(i))
        return rem(p, p, zs.at[i, d, s], zr.at[i, d, s], right if d == 0 else left)

    def xcopy(i, zz, src_own=False):
        p = piece(i, zz * NX + x, myq(i))
        return rem(own(i) if src_own else p, p, xs.at[i, zz], xr.at[i, zz], xm)

    def xrecv(i, zz):
        p = piece(i, zz * NX + 1 - x, myq(i))
        return rem(p, p, xs.at[i, zz], xr.at[i, zz], xm)

    def ycopy(i, g):
        p = piece(i, g, blk)
        return rem(p, p, ys.at[i, g], yr.at[i, g], ym)

    def yrecv(i, g):
        p = piece(i, g, lax.rem(blk + 2, 4))
        return rem(p, p, ys.at[i, g], yr.at[i, g], ym)

    def ccopy(i, k, g):
        q = myq(i) if k == 0 else lax.rem(blk + 2, 4)
        p = piece(i, g, q)
        return rem(p, p, cs.at[i, k, g], cr.at[i, k, g], cm)

    def crecv(i, k, g):
        if chunks[i][3] == 4:
            mate = blk + 1 - 2 * c
            q = mate if k == 0 else lax.rem(mate + 2, 4)
        else:
            q = 1 - c
        p = piece(i, g, q)
        return rem(p, p, cs.at[i, k, g], cr.at[i, k, g], cm)

    def spread(i, g):
        if chunks[i][3] == 4:
            ycopy(i, g).start()
        ccopy(i, 0, g).start()

    nch = len(chunks)

    def begin(i):
        @pl.when(z < NZ - 1)
        def _():
            zcopy(i, 0, 0, True).start()

        @pl.when(z > 0)
        def _():
            zcopy(i, 1, 0, True).start()
        xcopy(i, z, True).start()

    def zstep(i, s):
        @pl.when(z - 1 - s >= 0)
        def _():
            zrecv(i, 0, s).wait_recv()
            if s < NZ - 2:
                @pl.when(z < NZ - 1)
                def _():
                    zcopy(i, 0, s + 1, False).start()
            xcopy(i, z - 1 - s).start()
            spread(i, (z - 1 - s) * NX + x)

        @pl.when(z + 1 + s < NZ)
        def _():
            zrecv(i, 1, s).wait_recv()
            if s < NZ - 2:
                @pl.when(z > 0)
                def _():
                    zcopy(i, 1, s + 1, False).start()
            xcopy(i, z + 1 + s).start()
            spread(i, (z + 1 + s) * NX + x)

    def xstep(i, k):
        def one(zz):
            xrecv(i, zz).wait_recv()
            spread(i, zz * NX + 1 - x)
        if k == 0:
            one(z)
        else:
            pl.when(z - k >= 0)(lambda: one(z - k))
            pl.when(z + k < NZ)(lambda: one(z + k))

    def ystep(i, k):
        g = lax.rem(dp + k, G)
        yrecv(i, g).wait_recv()
        ccopy(i, 1, g).start()

    def cstep(i, k):
        g = lax.rem(dp + k, G)
        crecv(i, 0, g).wait_recv()
        if chunks[i][3] == 4:
            crecv(i, 1, g).wait_recv()

    def sent(i):
        @pl.when(z < NZ - 1)
        def _():
            zcopy(i, 0, 0, True).wait_send()

        @pl.when(z > 0)
        def _():
            zcopy(i, 1, 0, True).wait_send()
        for s in range(NZ - 1):
            if s < NZ - 2:
                @pl.when((z - 1 - s >= 0) & (z < NZ - 1))
                def _():
                    zcopy(i, 0, s + 1, False).wait_send()

                @pl.when((z + 1 + s < NZ) & (z > 0))
                def _():
                    zcopy(i, 1, s + 1, False).wait_send()
        xcopy(i, z, True).wait_send()
        for k in range(1, NZ):
            xcopy(i, lax.rem(z + k, NZ)).wait_send()
        for k in range(1, G):
            g = lax.rem(dp + k, G)
            ccopy(i, 0, g).wait_send()
            if chunks[i][3] == 4:
                ycopy(i, g).wait_send()
                ccopy(i, 1, g).wait_send()

    stages = [begin] + [functools.partial(lambda i, s: (zstep(i, s), xstep(i, s)), s=s) for s in range(NZ - 1)]
    stages.append(lambda i: xstep(i, NZ - 1))
    stages.append(lambda i: [ystep(i, k) for k in range(1, G)] if chunks[i][3] == 4 else None)
    stages.append(lambda i: [cstep(i, k) for k in range(1, G)])
    stages.append(sent)
    for t in range(nch + len(stages) - 1):
        for s in reversed(range(len(stages))):
            i = t - s
            if 0 <= i < nch:
                stages[s](i)
    for l in locs:
        l.wait()


def gather(slabs, chunks):
    n, nch = len(slabs), len(chunks)
    dma = pltpu.SemaphoreType.DMA
    return pl.pallas_call(
        functools.partial(gather_kernel, chunks, n),
        out_shape=[jax.ShapeDtypeStruct((G,) + s.shape, s.dtype) for s in slabs],
        in_specs=[pl.BlockSpec(memory_space=pl.ANY)] * n,
        out_specs=[pl.BlockSpec(memory_space=pl.ANY)] * n,
        scratch_shapes=[dma((n,)), dma((nch, 2, NZ - 1)), dma((nch, 2, NZ - 1)), dma((nch, NZ)), dma((nch, NZ)),
                        dma((nch, G)), dma((nch, G)), dma((nch, 2, G)), dma((nch, 2, G))],
        compiler_params=pltpu.CompilerParams(collective_id=1, has_side_effects=True),
        name="gather_weights",
    )(*slabs)


def add_into(dst, other, n):
    def body(k, _):
        dst[k] = (dst[k].astype(jnp.float32) + other(k).astype(jnp.float32)).astype(dst.dtype)
        return 0
    lax.fori_loop(0, n, body, 0)


def reduce_kernel(chunks, nslab, *refs):
    nch = len(chunks)
    ins, outs = refs[:nslab], refs[nslab:2 * nslab]
    bufs = refs[2 * nslab:]
    own, crv, yrv, xrv, zrv, fin, s4b = (bufs[k * nch:(k + 1) * nch] for k in range(7))
    ls, cs, cr, ys, yr, xs, xr, zs, zr, fs, fr = bufs[7 * nch:]
    dp, blk = lax.axis_index("dp"), lax.axis_index("blk")
    z, x = dp // NX, lax.rem(dp, NX)
    y, c = blk // 2, lax.rem(blk, 2)
    left, right = (dp - NX, blk), (dp + NX, blk)
    xm, ym, cm = (dp + 1 - 2 * x, blk), (dp, lax.rem(blk + 2, 4)), (dp, blk + 1 - 2 * c)
    bar = pltpu.get_barrier_semaphore()
    for t in (xm, ym, cm):
        pl.semaphore_signal(bar, inc=1, device_id=t, device_id_type=MESH)

    @pl.when(z > 0)
    def _():
        pl.semaphore_signal(bar, inc=1, device_id=left, device_id_type=MESH)

    @pl.when(z < NZ - 1)
    def _():
        pl.semaphore_signal(bar, inc=1, device_id=right, device_id_type=MESH)

    pl.semaphore_wait(bar, 3 + jnp.where(z > 0, 1, 0) + jnp.where(z < NZ - 1, 1, 0))

    def rem(src, dst, a, b, to):
        return pltpu.make_async_remote_copy(src_ref=src, dst_ref=dst, send_sem=a, recv_sem=b, device_id=to, device_id_type=MESH)

    def four(i):
        return chunks[i][3] == 4

    def part(i, core):
        s, c0, n, split = chunks[i]
        cols = pl.ds(c0, n)
        return ins[s].at[:, :, :, core, :, cols] if split == 4 else ins[s].at[:, :, core, :, cols]

    def load(i):
        return pltpu.make_async_copy(part(i, c), own[i], ls.at[i])

    def core_send(i):
        return rem(part(i, 1 - c), crv[i], cs.at[i, 0], cr.at[i, 0], cm)

    def y_send(i):
        return rem(own[i].at[:, :, 1 - y], yrv[i], ys.at[i], yr.at[i], ym)

    def s2(i):
        return yrv[i] if four(i) else own[i]

    def x_send(i):
        return rem(s2(i).at[:, 1 - x], xrv[i], xs.at[i], xr.at[i], xm)

    def z_copy(i, d, lo, hi, first, to):
        src = xrv[i].at[pl.ds(lo, hi - lo)] if first else zrv[i].at[d, pl.ds(lo, hi - lo)]
        return rem(src, zrv[i].at[d, pl.ds(lo, hi - lo)], zs.at[i, d], zr.at[i, d], to)

    def right_send(i, k):
        return z_copy(i, 0, k + 1, NZ, k == 0, right)

    def left_send(i, k):
        return z_copy(i, 1, 0, k, k == NZ - 1, left)

    def st0(i):
        load(i).start()
        core_send(i).start()

    def st1(i):
        load(i).wait()
        core_send(i).wait_recv()

        def body(g, _):
            zz, xx = g // NX, lax.rem(g, NX)
            for yy in ((0, 1) if four(i) else (None,)):
                at = (zz, xx) if yy is None else (zz, xx, yy)
                own[i][at] = (own[i][at].astype(jnp.float32) + crv[i][at].astype(jnp.float32)).astype(jnp.bfloat16)
            return 0
        lax.fori_loop(0, G, body, 0)
        if four(i):
            y_send(i).start()

    def st2(i):
        if four(i):
            y_send(i).wait_recv()

            def body(g, _):
                zz, xx = g // NX, lax.rem(g, NX)
                yrv[i][zz, xx] = (yrv[i][zz, xx].astype(jnp.float32) + own[i][zz, xx, y].astype(jnp.float32)).astype(jnp.bfloat16)
                return 0
            lax.fori_loop(0, G, body, 0)
        x_send(i).start()

    def zstep(i, s):
        if s < NZ - 1:
            @pl.when(z == s)
            def _():
                if s > 0:
                    z_copy(i, 0, s, NZ, False, right).wait_recv()
                    for k in range(s + 1, NZ):
                        zrv[i][0, k] = (zrv[i][0, k].astype(jnp.float32) + xrv[i][k].astype(jnp.float32)).astype(jnp.bfloat16)
                right_send(i, s).start()

            @pl.when(z == NZ - 1 - s)
            def _():
                k0 = NZ - 1 - s
                if s > 0:
                    z_copy(i, 1, 0, k0 + 1, False, left).wait_recv()
                    for k in range(k0):
                        zrv[i][1, k] = (zrv[i][1, k].astype(jnp.float32) + xrv[i][k].astype(jnp.float32)).astype(jnp.bfloat16)
                left_send(i, k0).start()

    def st3(i):
        x_send(i).wait_recv()
        add_into(xrv[i], lambda k: s2(i)[k, x], NZ)
        zstep(i, 0)

    def finish(i):
        q = blk if four(i) else c
        dst = fin[i].at[q] if four(i) else s4b[i]

        def put(v):
            if four(i):
                fin[i][blk] = v.astype(jnp.bfloat16)
            else:
                s4b[i][...] = v.astype(jnp.bfloat16)

        @pl.when(z == 0)
        def _():
            z_copy(i, 1, 0, 1, False, left).wait_recv()
            put(xrv[i][0].astype(jnp.float32) + zrv[i][1, 0].astype(jnp.float32))

        @pl.when(z == NZ - 1)
        def _():
            z_copy(i, 0, NZ - 1, NZ, False, right).wait_recv()
            put(xrv[i][NZ - 1].astype(jnp.float32) + zrv[i][0, NZ - 1].astype(jnp.float32))

        @pl.when((z > 0) & (z < NZ - 1))
        def _():
            put(xrv[i][z].astype(jnp.float32) + zrv[i][0, z].astype(jnp.float32) + zrv[i][1, z].astype(jnp.float32))
        if four(i):
            fin_send(i, 0).start()
            fin_send(i, 1).start()
        else:
            fin_send(i, 0).start()

    def fin_send(i, k):
        if four(i):
            q = blk if k < 2 else lax.rem(blk + 2, 4)
            return rem(fin[i].at[q], fin[i].at[q], fs.at[i, k], fr.at[i, k], ym if k == 0 else cm)
        if k == 0:
            return rem(s4b[i], fin[i].at[2], fs.at[i, 0], fr.at[i, 0], ym)
        return rem(fin[i].at[c], fin[i].at[c], fs.at[i, 1], fr.at[i, 1], cm)

    def fin_recv(i, k):
        if four(i):
            mate = blk + 1 - 2 * c
            q = lax.rem(blk + 2, 4) if k == 0 else mate if k == 1 else lax.rem(mate + 2, 4)
            return rem(fin[i].at[q], fin[i].at[q], fs.at[i, k], fr.at[i, k], cm)
        if k == 0:
            return fin_send(i, 0)
        return rem(fin[i].at[1 - c], fin[i].at[1 - c], fs.at[i, 1], fr.at[i, 1], cm)

    def st8(i):
        fin_recv(i, 0).wait_recv()
        if four(i):
            fin_send(i, 2).start()
        else:
            fin[i][c] = (fin[i][2].astype(jnp.float32) + s4b[i][...].astype(jnp.float32)).astype(jnp.bfloat16)
            fin_send(i, 1).start()

    def st9(i):
        s, c0, n, split = chunks[i]
        for k in ((1, 2) if four(i) else (1,)):
            fin_recv(i, k).wait_recv()
        for q in range(split):
            outs[s][q, :, pl.ds(c0, n)] = fin[i][q].astype(jnp.float32)

    def sent(i):
        core_send(i).wait_send()
        if four(i):
            y_send(i).wait_send()
        x_send(i).wait_send()
        for k in range(NZ - 1):
            pl.when(z == k)(lambda k=k: right_send(i, k).wait_send())
            pl.when(z == k + 1)(lambda k=k: left_send(i, k + 1).wait_send())
        for k in range(3 if four(i) else 2):
            fin_send(i, k).wait_send()

    stages = [st1, st2, st3] + [functools.partial(lambda i, s: zstep(i, s), s=s) for s in range(1, NZ - 1)] + [finish, st8, st9, sent]
    for i in range(nch):
        st0(i)
    for t in range(nch + len(stages) - 1):
        for s in reversed(range(len(stages))):
            i = t - s
            if 0 <= i < nch:
                stages[s](i)


def reduce(slabs, chunks):
    n, nch = len(slabs), len(chunks)
    dma = pltpu.SemaphoreType.DMA
    bf = jnp.bfloat16

    def shapes(kind):
        out = []
        for s, c0, nc, split in chunks:
            h = slabs[s].shape[-2]
            lead = (NZ, NX, 2) if split == 4 else (NZ, NX)
            tiny = (1, 16, 128)
            shape = dict(own=lead + (h, nc), crv=lead + (h, nc), yrv=(NZ, NX, h, nc) if split == 4 else tiny,
                         xrv=(NZ, h, nc), zrv=(2, NZ, h, nc), fin=(4 if split == 4 else 3, h, nc),
                         s4b=(h, nc) if split == 2 else tiny)[kind]
            out.append(pltpu.VMEM(shape, bf))
        return out
    scratch = sum([shapes(k) for k in ("own", "crv", "yrv", "xrv", "zrv", "fin", "s4b")], [])
    sems = [dma((nch,)), dma((nch, 1)), dma((nch, 1)), dma((nch,)), dma((nch,)), dma((nch,)), dma((nch,)),
            dma((nch, 2)), dma((nch, 2)), dma((nch, 3)), dma((nch, 3))]
    outs = []
    for k, s in enumerate(slabs):
        split = next(ch[3] for ch in chunks if ch[0] == k)
        outs.append(jax.ShapeDtypeStruct((split,) + s.shape[-2:], jnp.float32))
    return pl.pallas_call(
        functools.partial(reduce_kernel, chunks, n),
        out_shape=outs,
        in_specs=[pl.BlockSpec(memory_space=pl.ANY)] * n,
        out_specs=[pl.BlockSpec(memory_space=pltpu.VMEM)] * n,
        scratch_shapes=scratch + sems,
        compiler_params=pltpu.CompilerParams(collective_id=2, has_side_effects=True, vmem_limit_bytes=60 << 20),
        name="reduce_grads",
    )(*slabs)


AG_CHUNKS = [(0, 0, 1664, 4), (1, 0, 1024, 2), (2, 0, 1280, 4), (2, 1280, 1280, 4), (3, 0, 512, 2), (2, 2560, 1280, 4),
             (2, 3840, 1280, 4), (3, 512, 512, 2)]
RS_CHUNKS = [(2, 0, 1280, 4), (3, 0, 512, 2), (2, 1280, 1280, 4), (2, 2560, 1280, 4), (3, 512, 512, 2), (2, 3840, 1280, 4),
             (1, 0, 1024, 2), (0, 0, 896, 4), (0, 896, 768, 4)]


def pad_to(v, shape):
    return jnp.pad(v, [(0, b - a) for a, b in zip(v.shape, shape)])


def pad_cols(v, geo):
    v = v.reshape(v.shape[0], geo.n_dp, geo.gw)
    return jnp.pad(v, ((0, 0), (0, 0), (0, geo.gp - geo.gw))).reshape(v.shape[0], geo.dp)


def unpad_cols(v, geo):
    return v.reshape(v.shape[0], geo.n_dp, geo.gp)[:, :, :geo.gw].reshape(v.shape[0], geo.d)


def pack(geo, q, k, v, o, g, u, d, g1, g2, rt):
    rows = q.shape[0]
    kv = jnp.concatenate([k.reshape(rows, KV_HEADS, 64), v.reshape(rows, KV_HEADS, 64)], axis=2).reshape(rows, 640)
    small = pad_to(jnp.concatenate([g1[:, None], g2[:, None], rt], axis=1), (rows, 64))
    a = pad_to(jnp.concatenate([q, small, kv], axis=1), (geo.gp, COLS_A))
    gu = pad_to(jnp.concatenate([g, u], axis=1), (geo.gp, 2 * geo.ff))
    return a, pad_to(pad_cols(o, geo), (geo.gp, geo.dp)), gu, pad_cols(d, geo)


def whole_weights(geo, slabs):
    a, o, gu, d = slabs
    if (geo.n_dp, geo.n_blk) != (G, 4):
        return tuple(lax.all_gather(w, "dp", axis=0, tiled=True) for w in slabs)
    gp, rd = geo.gp, d.shape[0]
    got = gather([a.reshape(4, gp // 4, -1), o.reshape(2, gp // 2, -1), gu.reshape(4, gp // 4, -1), d.reshape(2, rd // 2, -1)],
                 AG_CHUNKS)
    return tuple(w.reshape(-1, w.shape[-1]) for w in got)


def summed_grads(geo, slabs):
    a, o, gu, d = slabs
    if (geo.n_dp, geo.n_blk) != (G, 4):
        shares = [lax.psum_scatter(v, "dp", scatter_dimension=0, tiled=True) for v in slabs]
        return tuple(lax.psum(v, "blk").astype(F32) for v in shares)
    gp, rd = geo.gp, d.shape[0] // G
    got = reduce([a.reshape(NZ, NX, 2, 2, gp // 4, -1), o.reshape(NZ, NX, 2, gp // 2, -1), gu.reshape(NZ, NX, 2, 2, gp // 4, -1),
                  d.reshape(NZ, NX, 2, rd // 2, -1)], RS_CHUNKS)
    return tuple(w.reshape(-1, w.shape[-1]) for w in got)


def unpack(geo, slabs):
    a, o, gu, d = slabs
    a, o, gu = a[:geo.gw], o[:geo.gw], gu[:geo.gw]
    kv = a[:, 1024:].reshape(geo.gw, KV_HEADS, 128)
    return (a[:, :960], kv[:, :, :64].reshape(geo.gw, 320), kv[:, :, 64:].reshape(geo.gw, 320), unpad_cols(o, geo),
            gu[:, :geo.ff], gu[:, geo.ff:], unpad_cols(d, geo), a[:, 960], a[:, 961], a[:, 962:965])


def meet(*others):
    bar = pltpu.get_barrier_semaphore()
    for t in others:
        pl.semaphore_signal(bar, inc=1, device_id=t, device_id_type=MESH)
    pl.semaphore_wait(bar, len(others))


def mates():
    dp, blk = lax.axis_index("dp"), lax.axis_index("blk")
    y, c = blk // 2, lax.rem(blk, 2)
    return dp, blk, y, c, (dp, lax.rem(blk + 2, 4)), (dp, blk + 1 - 2 * c)


def share_kernel(own, out, lsem, ssem, rsem):
    dp, blk, y, c, ym, cm = mates()
    meet(ym, cm)

    def rem(src, b, k, to):
        return pltpu.make_async_remote_copy(src_ref=src, dst_ref=out.at[b], send_sem=ssem.at[k], recv_sem=rsem.at[k],
                                            device_id=to, device_id_type=MESH)
    far, near = lax.rem(blk + 2, 4), blk + 1 - 2 * c
    rem(own, blk, 0, ym).start()
    rem(own, blk, 1, cm).start()
    local = pltpu.make_async_copy(own, out.at[blk], lsem)
    local.start()
    rem(out.at[far], far, 0, ym).wait_recv()
    rem(out.at[far], far, 2, cm).start()
    rem(out.at[near], near, 1, cm).wait_recv()
    both = lax.rem(near + 2, 4)
    rem(out.at[both], both, 2, cm).wait_recv()
    rem(own, blk, 0, ym).wait_send()
    rem(own, blk, 1, cm).wait_send()
    rem(out.at[far], far, 2, cm).wait_send()
    local.wait()


def share_rows(geo, ident, kv):
    if geo.n_blk != 4:
        return lax.all_gather(kv, "blk", axis=0, tiled=False)
    dma = pltpu.SemaphoreType.DMA
    return pl.pallas_call(
        share_kernel, out_shape=jax.ShapeDtypeStruct((4,) + kv.shape, kv.dtype),
        in_specs=[pl.BlockSpec(memory_space=pl.ANY)], out_specs=pl.BlockSpec(memory_space=pl.ANY),
        scratch_shapes=[dma, dma((3,)), dma((3,))],
        compiler_params=pltpu.CompilerParams(collective_id=ident, has_side_effects=True), name=f"share_rows_{ident}")(kv)


def give_kernel(dkv, out, got1, half, got2, ssem, rsem):
    dp, blk, y, c, ym, cm = mates()
    meet(ym, cm)

    def rem(src, dst, k, to):
        return pltpu.make_async_remote_copy(src_ref=src, dst_ref=dst, send_sem=ssem.at[k], recv_sem=rsem.at[k],
                                            device_id=to, device_id_type=MESH)
    first = [rem(dkv.at[yy, 1 - c], got1.at[yy], yy, cm) for yy in range(2)]
    for f in first:
        f.start()
    for f in first:
        f.wait_recv()
    half[...] = (got1[1 - y].astype(F32) + dkv[1 - y, c].astype(F32)).astype(BF)
    second = rem(half, got2, 2, ym)
    second.start()
    mine = got1[y].astype(F32) + dkv[y, c].astype(F32)
    second.wait_recv()
    out[...] = mine + got2[...].astype(F32)
    for f in first + [second]:
        f.wait_send()


def give_rows(geo, ident, dkv):
    if geo.n_blk != 4:
        return lax.psum_scatter(dkv, "blk", scatter_dimension=0, tiled=False).astype(F32)
    dma = pltpu.SemaphoreType.DMA
    piece = dkv.shape[1:]
    vm = pl.BlockSpec(memory_space=pltpu.VMEM)
    return pl.pallas_call(
        give_kernel, out_shape=jax.ShapeDtypeStruct(piece, F32), in_specs=[vm], out_specs=vm,
        scratch_shapes=[pltpu.VMEM((2,) + piece, BF), pltpu.VMEM(piece, BF), pltpu.VMEM(piece, BF), dma((3,)), dma((3,))],
        compiler_params=pltpu.CompilerParams(collective_id=ident, has_side_effects=True, vmem_limit_bytes=40 << 20),
        name=f"give_rows_{ident}")(dkv.reshape((2, 2) + piece))


def per_device(block_input, cotangent, seq_lengths, routes_two, routes_three, query_weight, key_weight, value_weight, output_weight,
               gate_weight, up_weight, down_weight, first_gain, second_gain, router_weight):
    micro, seqs, bl, d = block_input.shape
    n_dp, n_blk = lax.axis_size("dp"), lax.axis_size("blk")
    count = micro * seqs
    geo = Geo(count, bl, n_dp, n_blk, d, gate_weight.shape[1], (None, routes_two.shape[2], routes_three.shape[2]))
    slabs = pack(geo, query_weight, key_weight, value_weight, output_weight, gate_weight, up_weight, down_weight, first_gain,
                 second_gain, router_weight)
    wa, wo, gu, wd = whole_weights(geo, slabs)
    ids = iter(range(10, 30))
    env = block(geo, block_input.reshape(count * bl, d), cotangent.reshape(count * bl, d), seq_lengths.reshape(count),
                (routes_two.reshape(count, -1), routes_three.reshape(count, -1)), wa, wo, gu, wd,
                lambda kv: share_rows(geo, next(ids), kv), lambda dkv: give_rows(geo, next(ids), dkv))
    grads = [weight_grads(geo, env, h) for h in ("a", "o", "gu", "d")]
    grads = unpack(geo, summed_grads(geo, grads))
    return (env["out"].reshape(block_input.shape), env["grad"].reshape(block_input.shape)) + tuple(grads)


def solution(mesh):
    in_specs = (
        P(None, "dp", "blk", None),
        P(None, "dp", "blk", None),
        P(None, "dp"),
        P(None, "dp", None),
        P(None, "dp", None),
        P("dp", None),
        P("dp", None),
        P("dp", None),
        P("dp", None),
        P("dp", None),
        P("dp", None),
        P("dp", None),
        P("dp"),
        P("dp"),
        P("dp", None),
    )
    out_specs = (
        P(None, "dp", "blk", None),
        P(None, "dp", "blk", None),
        P("dp", None),
        P("dp", None),
        P("dp", None),
        P("dp", None),
        P("dp", None),
        P("dp", None),
        P("dp", None),
        P("dp"),
        P("dp"),
        P("dp", None),
    )
    return jax.shard_map(
        per_device, mesh=mesh, in_specs=in_specs, out_specs=out_specs, check_vma=False
    )
```

time: 1140 us -> 636 us (0.56)
  Pallas kernels: 228 us -> 595 us
  local copies, waits for them, and re-layouts: 361 us -> 32.3 us
  matrix products: 317 us -> 0 us
  other arithmetic: 123 us -> 2.86 us
  waiting for transfers between devices: 50 us -> 0 us
  blocking collectives: 29.6 us -> 0 us
  between operations: 19.3 us -> 1.37 us
    pallas_call x0 -> x18, Pallas kernels: none -> 367 us  [the longest x12 284 us: call(): pl.pallas_call(kernel, out_shape=[jax.ShapeDtypeStruct(s, d) for s, d in...]
    dot_general x102 -> x0, matrix products: 317 us -> none  [the longest x3 21.7 us: block_backward(): jnp.einsum('srd,srf->df', normalized_second, up_grad, preferred_element_t...]
    scatter x7 -> x0, local copies, waits for them, and re-layouts: 159 us -> none  [place_rows(): return block_vals.at[index_vals].set(new_vals, mode='drop')]
    slice x36 -> x7, local copies, waits for them, and re-layouts: 44.6 us -> 5.79 us  [the longest x1 3.25 us: unpack(): gu[:, geo.ff:]]
    gather x15 -> x0, local copies, waits for them, and re-layouts: 38.2 us -> none  [the longest x10 23.7 us: pick_rows(): return block_vals[index_vals]]
    unnamed x608 -> x39, local copies, waits for them, and re-layouts: 50.9 us -> 17.3 us
    unnamed x11 -> x0, waiting for transfers between devices: 31.2 us -> none
    all_gather x4 -> x0, blocking collectives: 29.6 us -> none  [the longest x2 14.9 us: block_forward(): lax.all_gather(keyset, 'blk', axis=1, tiled=True)]
  transfers between devices with their start and end apart: 8 -> 0, of which waited for: 3 -> 0; matrix products, arithmetic and copies ran while one was open for 22% -> 0% of each run, Pallas kernels for 0% -> 0%
where the time goes in v2:
time: 636 us; the launch traced here: 631 us
  Pallas kernels  595 us (94%)
  local copies, waits for them, and re-layouts  32.3 us (5%)
    pallas_call x12, Pallas kernels, call(): pl.pallas_call(kernel, out_shape=[jax.ShapeDtypeStruct(s, d) for s, d in...  284 us
    pallas_call x1, Pallas kernels, reduce(): pl.pallas_call(functools.partial(reduce_kernel, chunks, n), out_shape=out...  138 us
    pallas_call x1, Pallas kernels, gather(): pl.pallas_call(functools.partial(gather_kernel, chunks, n), out_shape=[ja...  89.8 us
    pallas_call x3, Pallas kernels, share_rows(): pl.pallas_call(share_kernel, out_shape=jax.ShapeDtypeStruct((4,) + kv.sha...  42.5 us
    pallas_call x3, Pallas kernels, give_rows(): pl.pallas_call(give_kernel, out_shape=jax.ShapeDtypeStruct(piece, F32), i...  40.1 us
    unnamed x39, local copies, waits for them, and re-layouts  17.3 us

profile of v2, /device:TPU:0, one launch (start us, length us, event | category | flops | bytes accessed | tf_op | source)
XLA Modules:
  0.0 631.2 jit_solution(13546801896775947139)
XLA Ops:
  0.7 1.3 copy.56
  7.0 1.7 constant_dynamic-slice_fusion
  10.7 1.3 copy.41
  12.0 1.3 copy.42
  13.4 1.2 fusion.2
  14.6 89.8 %gather_weights.1 = (bf16[8,4,32,1664]{3,2,1,0:T(8,128)(2,1)}, bf16[8,2,64,1024]{3,2,1,0:T(8,128)(2,1)}, bf16[8,4,32,5120]{3,2,1,0:T(8,128)(2,1)}, bf16[8,2,160,1024]{3,2,1,0:T(8,128)(2,1)}) custom-call(bf16[4,32,1664]{2,1,0:T(8,128)(2,1)} %bitcast.87, bf16[2,64,1024]{2,1,0:T(8,128)(2,1)} %bitcast.95, bf16[4,32,5120]{2,1,0:T(8,128)(2,1)} %bitcast.79, ...), custom_call_target="tpu_custom_call" | custom-call | tf_op jit(solution)/shard_map/gather_weights/pallas_call | solution.py:853
  104.4 8.1 %first_project.1 = (bf16[512,1024]{1,0:T(8,128)(2,1)}, bf16[512,1024]{1,0:T(8,128)(2,1)}, bf16[15,512,128]{2,1,0:T(8,128)(2,1)}, bf16[512,640]{1,0:T(8,128)(2,1)...) custom-call(bf16[512,960]{1,0:T(8,128)(2,1)} %bitcast.82, ...), custom_call_target="tpu_custom_call" | custom-call | tf_op jit(solution)/shard_map/first_project/pallas_call | solution.py:71
  112.5 22.6 %share_rows_10.1.refs_5_.refs_3_ = bf16[4,2,256,640]{3,2,1,0:T(8,128)(2,1)} custom-call(bf16[2,256,640]{2,1,0:T(8,128)(2,1)} %bitcast.99), custom_call_target="tpu_custom_call" | custom-call | tf_op jit(solution)/shard_map/share_rows_10/pallas_call | solution.py:1199
  135.0 44.4 %forward_0.1 = (bf16[512,1024]{1,0:T(8,128)(2,1)}, f32[2,16,256]{2,1,0:T(8,128)}, bf16[512,1024]{1,0:T(8,128)(2,1)}, bf16[512,1024]{1,0:T(8,128)(2,1)}, bf16[512...) custom-call(bf16[1024,1664]{1,0:T(8,128)(2,1)} %bitcast.64, ...), custom_call_target="tpu_custom_call" | custom-call | tf_op jit(solution)/shard_map/forward_0/pallas_call | solution.py:71
  179.5 11.7 %share_rows_11.1.refs_5_.refs_23_ = bf16[4,2,128,640]{3,2,1,0:T(8,128)(2,1)} custom-call(bf16[2,128,640]{2,1,0:T(8,128)(2,1)} %bitcast.101), custom_call_target="tpu_custom_call" | custom-call | tf_op jit(solution)/shard_map/share_rows_11/pallas_call | solution.py:1199
  191.2 30.5 %forward_1.1 = (bf16[256,1024]{1,0:T(8,128)(2,1)}, f32[2,16,128]{2,1,0:T(8,128)}, bf16[256,1024]{1,0:T(8,128)(2,1)}, bf16[256,1024]{1,0:T(8,128)(2,1)}, bf16[256...) custom-call(bf16[1024,1664]{1,0:T(8,128)(2,1)} %bitcast.65, ...), custom_call_target="tpu_custom_call" | custom-call | tf_op jit(solution)/shard_map/forward_1/pallas_call | solution.py:71
  221.7 8.3 %share_rows_12.1.refs_6_ = bf16[4,2,64,640]{3,2,1,0:T(8,128)(2,1)} custom-call(bf16[2,64,640]{2,1,0:T(8,128)(2,1)} %bitcast.104), custom_call_target="tpu_custom_call" | custom-call | tf_op jit(solution)/shard_map/share_rows_12/pallas_call | solution.py:1199
  230.0 49.8 %turn.1 = (bf16[128,1024]{1,0:T(8,128)(2,1)}, f32[2,16,64]{2,1,0:T(8,128)}, bf16[128,1024]{1,0:T(8,128)(2,1)}, bf16[128,1024]{1,0:T(8,128)(2,1)}, bf16[128,2560]...) custom-call(bf16[1024,1664]{1,0:T(8,128)(2,1)} %bitcast.66, ...), custom_call_target="tpu_custom_call" | custom-call | tf_op jit(solution)/shard_map/turn/pallas_call | solution.py:71
  279.8 2.3 copy.45
  282.1 8.2 %give_rows_13.1 = f32[2,64,640]{2,1,0:T(8,128)S(1)} custom-call(bf16[2,2,2,64,640]{4,3,2,1,0:T(8,128)(2,1)S(1)} %bitcast.57), custom_call_target="tpu_custom_call" | custom-call | tf_op jit(solution)/shard_map/give_rows_13/pallas_call | solution.py:1234
  291.0 34.8 %backward_1.1 = (f32[256,1024]{1,0:T(8,128)}, bf16[256,1024]{1,0:T(8,128)(2,1)}, bf16[4,2,128,640]{3,2,1,0:T(8,128)(2,1)}, f32[256,1024]{1,0:T(8,128)}, bf16[256...) custom-call(bf16[1024,1664]{1,0:T(8,128)(2,1)} %bitcast.67, ...), custom_call_target="tpu_custom_call" | custom-call | tf_op jit(solution)/shard_map/backward_1/pallas_call | solution.py:71
  325.8 1.3 copy-done.4
  327.1 11.7 %give_rows_14.1 = f32[2,128,640]{2,1,0:T(8,128)S(1)} custom-call(bf16[2,2,2,128,640]{4,3,2,1,0:T(8,128)(2,1)S(1)} %bitcast.56), custom_call_target="tpu_custom_call" | custom-call | tf_op jit(solution)/shard_map/give_rows_14/pallas_call | solution.py:1234
  339.7 23.8 %backward_0.1 = (f32[512,1024]{1,0:T(8,128)}, bf16[512,1024]{1,0:T(8,128)(2,1)}, bf16[512,2560]{1,0:T(8,128)(2,1)}, bf16[512,2560]{1,0:T(8,128)(2,1)}, bf16[512,...) custom-call(bf16[1024,1664]{1,0:T(8,128)(2,1)} %bitcast.68, ...), custom_call_target="tpu_custom_call" | custom-call | tf_op jit(solution)/shard_map/backward_0/pallas_call | solution.py:71
  363.5 34.9 %backward_attend_0.1 = (bf16[512,1024]{1,0:T(8,128)(2,1)}, bf16[4,2,256,640]{3,2,1,0:T(8,128)(2,1)}) custom-call(bf16[1024,1024]{1,0:T(8,128)(2,1)} %get-tuple-element.111.refs_9_.refs_3_.refs_19_.refs_0_, bf16[512,1024]{1,0:T(8,128)(2,1)} %get-tuple-element.151.refs_1_.refs_3_, bf16[15,512,128]{2,1,0:T(8,128)(2,1)} %get-tuple-element.108.refs_4_.refs_2_, ...), custom_call_target="tpu_custom_call" | custom-call | tf_op jit(solution)/shard_map/backward_attend_0/pallas_call | solution.py:71
  398.4 8.4 %grad_output.1 = bf16[1024,1024]{1,0:T(8,128)(2,1)} custom-call(bf16[512,1024]{1,0:T(8,128)(2,1)} %get-tuple-element.152.refs_4_.refs_0_, bf16[256,1024]{1,0:T(8,128)(2,1)} %get-tuple-element.136.refs_24_.refs_1_, bf16[128,1024]{1,0:T(8,128)(2,1)} %get-tuple-element.174.refs_2_, bf16[512,1024]{1,0:T(8,128)(2,1)} %get-tuple-element.151.refs_1_.refs_3_, ...), custom_call_target="tpu_custom_call" | custom-call | tf_op jit(solution)/shard_map/grad_output/pallas_call | solution.py:71
  406.8 1.7 copy-done.1
  408.5 20.3 %give_rows_15.1 = f32[2,256,640]{2,1,0:T(8,128)S(1)} custom-call(bf16[2,2,2,256,640]{4,3,2,1,0:T(8,128)(2,1)S(1)} %bitcast.53), custom_call_target="tpu_custom_call" | custom-call | tf_op jit(solution)/shard_map/give_rows_15/pallas_call | solution.py:1234
  429.9 11.3 %last_project.1 = (bf16[512,1664]{1,0:T(8,128)(2,1)}, f32[8,1024]{1,0:T(8,128)}, f32[512,960]{1,0:T(8,128)}) custom-call(bf16[1024,1664]{1,0:T(8,128)(2,1)} %bitcast.69, f32[512,640]{1,0:T(8,128)} %bitcast.52, bf16[512,1024]{1,0:T(8,128)(2,1)} %get-tuple-element.157.refs_2_, f32[512,1024]{1,0:T(8,128)} %get-tuple-element.158.refs_3_, ...), custom_call_target="tpu_custom_call" | custom-call | tf_op jit(solution)/shard_map/last_project/pallas_call | solution.py:71
  441.2 3.0 copy.46
  444.2 8.2 %grad_query_kv.1 = bf16[1024,1664]{1,0:T(8,128)(2,1)} custom-call(bf16[512,1024]{1,0:T(8,128)(2,1)} %get-tuple-element.162.refs_0_, bf16[256,1024]{1,0:T(8,128)(2,1)} %get-tuple-element.163.refs_1_, bf16[128,1024]{1,0:T(8,128)(2,1)} %get-tuple-element.164.refs_2_, bf16[512,1664]{1,0:T(8,128)(2,1)} %get-tuple-element.165.refs_3_, ...), custom_call_target="tpu_custom_call" | custom-call | tf_op jit(solution)/shard_map/grad_query_kv/pallas_call | solution.py:71
  452.4 10.7 %grad_down.1 = bf16[2560,1024]{1,0:T(8,128)(2,1)} custom-call(bf16[512,2560]{1,0:T(8,128)(2,1)} %get-tuple-element.186.refs_0_, bf16[256,2560]{1,0:T(8,128)(2,1)} %get-tuple-element.187.refs_1_, bf16[128,2560]{1,0:T(8,128)(2,1)} %get-tuple-element.188.refs_2_, bf16[512,1024]{1,0:T(8,128)(2,1)} %get-tuple-element.189.refs_3_, ...), custom_call_target="tpu_custom_call" | custom-call | tf_op jit(solution)/shard_map/grad_down/pallas_call | solution.py:71
  463.1 19.3 %grad_gate_up.1 = bf16[1024,5120]{1,0:T(8,128)(2,1)} custom-call(bf16[512,1024]{1,0:T(8,128)(2,1)} %get-tuple-element.177.refs_0_, bf16[256,1024]{1,0:T(8,128)(2,1)} %get-tuple-element.178.refs_1_, bf16[128,1024]{1,0:T(8,128)(2,1)} %get-tuple-element.179.refs_2_, bf16[512,2560]{1,0:T(8,128)(2,1)} %get-tuple-element.180.refs_3_, ...), custom_call_target="tpu_custom_call" | custom-call | tf_op jit(solution)/shard_map/grad_gate_up/pallas_call | solution.py:71
  482.5 137.9 %reduce_grads.1 = (f32[4,32,1664]{2,1,0:T(8,128)}, f32[2,64,1024]{2,1,0:T(8,128)}, f32[4,32,5120]{2,1,0:T(8,128)}, f32[2,160,1024]{2,1,0:T(8,128)}) custom-call(bf16[4,2,2,2,32,1664]{5,4,3,2,1,0:T(8,128)(2,1)} %bitcast.77, bf16[4,2,2,64,1024]{4,3,2,1,0:T(8,128)(2,1)} %bitcast.78, bf16[4,2,2,2,32,5120]{5,4,3,2,1,0:T(8,128)(2,1)} %bitcast.75, ...), custom_call_target="tpu_custom_call" | custom-call | tf_op jit(solution)/shard_map/reduce_grads/pallas_call | solution.py:1091
  620.4 1.1 slice_bitcast_fusion
  626.1 1.4 reshape.191
  627.5 3.2 fusion.3
  (50 shorter events, 14.2 us)
Async XLA Ops:
  0.6 5.2 copy-start.13
  3.9 4.7 copy-start.10
  8.7 2.1 copy-start.8
  9.5 2.6 copy-start.9
  10.7 2.6 copy-start.11
  10.7 2.6 copy-start.12
  279.8 2.3 copy-start.5
  290.3 0.7 copy-start.3
  325.8 1.3 copy-start.4
  338.8 0.9 copy-start.2
  406.8 1.7 copy-start.1
  428.8 1.1 copy-start
  620.4 2.2 copy-start.7
  621.7 4.2 copy-start.6

commit v3 on v2

--- a/solution.py
+++ b/solution.py
@@ -60,24 +60,50 @@
     return jnp.where(first, pltpu.roll(x, 96, 1), pltpu.roll(x, 32, 1))
 
 
-def call(name, body, ins, outs, scratch=None, limit=63, hbm=()):
-    scratch = scratch or {}
-    names = list(ins) + list(outs) + list(scratch)
+class Far:
+    def __init__(self, value):
+        self.value = value
+
+
+class Words:
+    def __init__(self, value):
+        self.value = value
+
+
+class Out:
+    def __init__(self, shape, dtype=F32, far=False):
+        self.shape, self.dtype, self.far = shape, dtype, far
+
+
+def join(*parts, **more):
+    got = types.SimpleNamespace()
+    for p in parts + (more,):
+        vars(got).update(p if isinstance(p, dict) else vars(p))
+    return got
+
+
+def call(name, body, ins, outs, scratch=None, limit=63, **params):
+    flat_in, tree_in = jax.tree.flatten(ins)
+    flat_out, tree_out = jax.tree.flatten(outs)
+    flat_scratch, tree_scratch = jax.tree.flatten(scratch or {})
+    n_in, n_out = len(flat_in), len(flat_out)
 
     def kernel(*refs):
-        body(types.SimpleNamespace(**dict(zip(names, refs))))
-
-    vm, anyw = pl.BlockSpec(memory_space=pltpu.VMEM), pl.BlockSpec(memory_space=pl.ANY)
+        body(join(tree_in.unflatten(refs[:n_in]), tree_out.unflatten(refs[n_in:n_in + n_out]),
+                  tree_scratch.unflatten(refs[n_in + n_out:])))
+
+    vm, far = pl.BlockSpec(memory_space=pltpu.VMEM), pl.BlockSpec(memory_space=pl.ANY)
+    words = pl.BlockSpec(memory_space=pltpu.SMEM)
     got = pl.pallas_call(
         kernel,
-        out_shape=[jax.ShapeDtypeStruct(s, d) for s, d in outs.values()],
-        in_specs=[anyw if k in hbm else pl.BlockSpec(memory_space=pltpu.SMEM) if k == "lens" else vm for k in ins],
-        out_specs=[anyw if k in hbm else vm for k in outs],
-        scratch_shapes=list(scratch.values()),
-        compiler_params=pltpu.CompilerParams(vmem_limit_bytes=limit << 20),
+        out_shape=[jax.ShapeDtypeStruct(o.shape, o.dtype) for o in flat_out],
+        in_specs=[far if isinstance(v, Far) else words if isinstance(v, Words) else vm for v in flat_in],
+        out_specs=[far if o.far else vm for o in flat_out],
+        scratch_shapes=flat_scratch,
+        compiler_params=pltpu.CompilerParams(vmem_limit_bytes=limit << 20, **params),
         name=name,
-    )(*ins.values())
-    return dict(zip(outs, got))
+    )(*[v.value if isinstance(v, (Far, Words)) else v for v in flat_in])
+    return types.SimpleNamespace(**tree_out.unflatten(got))
 
 
 class Geo:
@@ -126,9 +152,9 @@
 
 def allowed(geo, r, routes, blk, turned):
     s, kn, bl = geo.slots[r], geo.keys(r), geo.bl
-    shape = (kn, s) if turned else (s, kn)
+    shape = (kn, GROUP * s) if turned else (GROUP * s, kn)
     key = rowid(shape) if turned else lanes(shape)
-    query = lanes(shape) if turned else rowid(shape)
+    query = lax.rem(lanes(shape) if turned else rowid(shape), s)
     ok = key <= blk * s + query
     if r > 0:
         t = geo.tops[r]
@@ -141,11 +167,23 @@
     return jnp.where(ok, 0.0, masked_fill)
 
 
-def project(geo, r, k):
+def project_kv(geo, r, k):
     a = k.a[...].astype(F32)
     n1 = lax.rsqrt(jnp.sum(a * a, axis=-1, keepdims=True) * (1.0 / geo.d) + eps)
     k.u[...] = (a * n1 * k.gn[0:1]).astype(BF)
     k.st[...] = jnp.where(lanes(k.st.shape) == 0, n1, 0.0)
+    u = k.u[...]
+    cos, sin = k.cos[...], k.sin[...]
+    left = lanes(cos.shape) < 64
+    ckv, skv = jnp.where(left, cos, 1.0), jnp.where(left, sin, 0.0)
+    for c0, n in ((1024, 256), (1280, 256), (1536, 128)):
+        some = dot(u, k.wa[:, c0:c0 + n])
+        for j in range(n // 128):
+            x = some[:, 128 * j:128 * j + 128]
+            k.kv[:, c0 - 1024 + 128 * j:c0 - 1024 + 128 * j + 128] = (x * ckv + swapped(x) * skv).astype(BF)
+
+
+def project_q(geo, r, k):
     u = k.u[...]
     cos, sin = k.cos[...], k.sin[...]
     left = lanes(cos.shape) < 64
@@ -158,12 +196,11 @@
             k.q16[h] = jnp.where(left, x, 0.0).astype(BF)
             if h + 1 < HEADS:
                 k.q16[h + 1] = jnp.where(left, pltpu.roll(x, 64, 1), 0.0).astype(BF)
-    ckv, skv = jnp.where(left, cos, 1.0), jnp.where(left, sin, 0.0)
-    for c0, n in ((1024, 256), (1280, 256), (1536, 128)):
-        some = dot(u, k.wa[:, c0:c0 + n])
-        for j in range(n // 128):
-            x = some[:, 128 * j:128 * j + 128]
-            k.kv[:, c0 - 1024 + 128 * j:c0 - 1024 + 128 * j + 128] = (x * ckv + swapped(x) * skv).astype(BF)
+
+
+def project(geo, r, k):
+    project_kv(geo, r, k)
+    project_q(geo, r, k)
 
 
 def select_rows(geo, r, k, blk):
@@ -176,34 +213,42 @@
         k.sin[m * s:m * s + s] = pick(ch, k.sinb[...])
 
 
-def attend(geo, r, k, blk):
+def attend(geo, r, k, blk, pause=None):
     s, kn = geo.slots[r], geo.keys(r)
 
     def seq(m, _):
-        kv = k.kvall[:, m]
-        k.kvg[...] = kv.reshape(kn, KV_HEADS * 128)
+        row0 = m * s if isinstance(m, int) else pl.multiple_of(m * s, s)
+        k.kvg[...] = k.kvall[:, m].reshape(kn, KV_HEADS * 128)
         k.bias[...] = allowed(geo, r, k.routes[pl.ds(m, 1)] if r else None, blk, False)
-        row0 = pl.multiple_of(m * s, s)
         k.col[...] = jnp.zeros(k.col.shape, F32)
 
-        def head(h, _):
-            kvh = k.kvg[:, pl.ds(pl.multiple_of(h // GROUP * 128, 128), 128)]
-            sc = dot_nt(k.q16[h, pl.ds(row0, s)], kvh) + k.bias[...]
+        def group(g, _):
+            kvh = k.kvg[:, pl.ds(pl.multiple_of(g * 128, 128), 128)]
+            sc = dot_nt(k.q16[pl.ds(g * GROUP, GROUP), pl.ds(row0, s)].reshape(GROUP * s, 128), kvh) + k.bias[...]
             top = jnp.max(sc, axis=-1, keepdims=True)
             p = jnp.exp(sc - top)
             total = jnp.sum(p, axis=-1, keepdims=True)
-            o2 = dot(p.astype(BF), kvh) * (1.0 / total)
-            k.o16[h] = o2
-            k.col[...] = jnp.where(lanes(k.col.shape) == h, top + jnp.log(total), k.col[...])
+            k.o16[pl.ds(g * GROUP, GROUP)] = (dot(p.astype(BF), kvh) * (1.0 / total)).reshape(GROUP, s, 128)
+            k.col[...] = jnp.where(lanes(k.col.shape) == g, top + jnp.log(total), k.col[...])
             return 0
-        lax.fori_loop(0, HEADS, head, 0)
+        if pause is None:
+            lax.fori_loop(0, KV_HEADS, group, 0)
+        else:
+            lax.fori_loop(0, 3, group, 0)
+            pause()
+            lax.fori_loop(3, KV_HEADS, group, 0)
         left = lanes((s, 128)) < 64
         for t in range(8):
             odd = k.o16[2 * t + 1] if 2 * t + 1 < HEADS else 0.0
             k.o[pl.ds(row0, s), 128 * t:128 * t + 128] = jnp.where(left, pltpu.roll(k.o16[2 * t], 64, 1), odd).astype(BF)
-        k.lse[m] = k.col[...].T[0:16]
+        k.lse[m] = k.col[...].T[0:8]
         return 0
-    lax.fori_loop(0, geo.ns, seq, 0)
+    if pause is None:
+        lax.fori_loop(0, geo.ns, seq, 0)
+    else:
+        for m in range(geo.ns):
+            seq(m, 0)
+            pause()
 
 
 class Tiles:
@@ -378,25 +423,25 @@
         for g in range(KV_HEADS):
             k.kvt[g] = k.kvg[:, 128 * g:128 * g + 128].astype(F32).T.astype(BF)
         k.bias[...] = allowed(geo, r, k.routes[pl.ds(m, 1)] if r else None, blk, True)
-        k.dt[...] = k.dcol[pl.ds(row0, s)].T[0:16]
+        dt = k.dcol[pl.ds(row0, s)].T
+        for h in range(HEADS):
+            k.dt[h // GROUP:h // GROUP + 1, h % GROUP * s:(h % GROUP + 1) * s] = dt[h:h + 1]
         k.ct[0] = k.cos[pl.ds(row0, s)].T[0:32] * 0.125
         k.ct[1] = k.sin[pl.ds(row0, s)].T[32:64] * 0.125
 
         def group(g, _):
             kvh = k.kvg[:, pl.ds(pl.multiple_of(g * 128, 128), 128)]
-            total = None
+            heads = (pl.ds(g * GROUP, GROUP), pl.ds(row0, s))
+            qh, doh = k.q16[heads].reshape(GROUP * s, 128), k.do16[heads].reshape(GROUP * s, 128)
+            p = jnp.exp(dot_nt(kvh, qh) + k.bias[...] - k.lse[m, pl.ds(g, 1)])
+            ds = (p * (dot_nt(kvh, doh) - k.dt[pl.ds(g, 1)])).astype(BF)
+            total = dot(ds, qh) + dot(p.astype(BF), doh)
+            dqt = dot(k.kvt[g], ds)
+            c, sn = k.ct[0], k.ct[1]
             for j in range(GROUP):
-                h = g * GROUP + j
-                qh, doh = k.q16[h, pl.ds(row0, s)], k.do16[h, pl.ds(row0, s)]
-                p = jnp.exp(dot_nt(kvh, qh) + k.bias[...] - k.lse[m, pl.ds(h, 1)])
-                ds = (p * (dot_nt(kvh, doh) - k.dt[pl.ds(h, 1)])).astype(BF)
-                part = dot(ds, qh) + dot(p.astype(BF), doh)
-                total = part if total is None else total + part
-                dqt = dot(k.kvt[g], ds)
-                y1, y2 = dqt[0:32], dqt[32:64]
-                c, sn = k.ct[0], k.ct[1]
-                k.dqt[h, 0:32] = (y1 * c + y2 * sn)
-                k.dqt[h, 32:64] = (y2 * c - y1 * sn)
+                y1, y2 = dqt[0:32, j * s:j * s + s], dqt[32:64, j * s:j * s + s]
+                k.dqt[g * GROUP + j, 0:32] = (y1 * c + y2 * sn)
+                k.dqt[g * GROUP + j, 32:64] = (y2 * c - y1 * sn)
             k.dkv[:, m, :, pl.ds(pl.multiple_of(g * 128, 128), 128)] = total.astype(BF).reshape(geo.n_blk, s, 128)
             return 0
         lax.fori_loop(0, KV_HEADS, group, 0)
@@ -435,11 +480,7 @@
             k.dh2[here] = k.dh[here] + put_back(k.choice[m], tok - k.inc[mine])
 
 
-def ns(**kw):
-    return types.SimpleNamespace(**kw)
-
-
-def block(geo, x, cot, lens, routes, wa, wo, gu, wd, share, give_back):
+def block(geo, x, cot, lens, routes, slabs, share, give_back):
     blk_of = lambda: lax.axis_index("blk")
     bl, d, dp, ff, nsq, nb = geo.bl, geo.d, geo.dp, geo.ff, geo.ns, geo.n_blk
     full = nsq * bl
@@ -449,253 +490,295 @@
     sinb = lax.dynamic_slice_in_dim(sin_all, b0, bl, 0)
     spread = geo.spread()
     R, S, KN = [geo.rows(r) for r in range(3)], geo.slots, [geo.keys(r) for r in range(3)]
-    V = pltpu.VMEM
-
-    def proj_outs(r):
-        return {f"a{r}": ((R[r], dp), BF if r == 0 else F32), f"u{r}": ((R[r], dp), BF), f"q16{r}": ((HEADS, R[r], 128), BF),
-                f"kv{r}": ((R[r], 640), BF), f"st{r}": ((R[r], 128), F32),
-                f"cos{r}": ((R[r], 128), F32), f"sin{r}": ((R[r], 128), F32)}
+    V, dma = pltpu.VMEM, pltpu.SemaphoreType.DMA
+    lens = Words(lens)
+
+    def proj_outs(r, kv=True):
+        more = dict(choice=Out((nsq, S[r], bl), BF)) if r else {}
+        more = dict(kv=Out((R[r], 640), BF), **more) if kv else more
+        return dict(a=Out((R[r], dp), F32 if r else BF), u=Out((R[r], dp), BF), q16=Out((HEADS, R[r], 128), BF), st=Out((R[r], 128)), cos=Out((R[r], 128)), sin=Out((R[r], 128)), **more)
+
+    def seen_outs(r):
+        return dict(o=Out((R[r], 1024), BF), lse=Out((nsq, 8, GROUP * S[r])))
+
+    def fore_outs(r):
+        return dict(**(seen_outs(r) if r else {}), b=Out((R[r], dp), BF), w=Out((R[r], dp), BF),
+                    gp=Out((R[r], ff), BF, True), up=Out((R[r], ff), BF, True), yf=Out((R[r], dp), BF), sx=Out((R[r], 128)))
+
+    def seen_scratch(r):
+        return dict(kvg=V((KN[r], 640), BF), bias=V((GROUP * S[r], KN[r]), F32), col=V((GROUP * S[r], 128), F32),
+                    o16=V((HEADS, S[r], 128), F32))
+
+    def fore_scratch(r):
+        return dict(acc=V((R[r], dp), F32), keep=V((2, 2, R[r], FT), BF), ksem=dma((2, 2)), **(seen_scratch(r) if r else {}))
 
     def feed_outs(r):
-        return {f"o{r}": ((R[r], 1024), BF), f"lse{r}": ((nsq, 16, S[r]), F32), f"b{r}": ((R[r], dp), BF),
-                f"w{r}": ((R[r], dp), BF), f"gp{r}": ((R[r], ff), BF), f"up{r}": ((R[r], ff), BF),
-                f"yf{r}": ((R[r], dp), BF), f"sx{r}": ((R[r], 128), F32), f"h{r + 1}": ((full, dp), F32)}
-
-    def attn_scratch(r):
-        return dict(kvg=V((KN[r], 640), BF), bias=V((S[r], KN[r]), F32), col=V((S[r], 128), F32),
-                    o16=V((HEADS, S[r], 128), F32), acc=V((R[r], dp), F32), keep=V((2, 2, R[r], FT), BF),
-                    ksem=pltpu.SemaphoreType.DMA((2, 2)))
-
-    def view(k, r, **more):
-        names = ("a", "u", "q16", "kv", "st", "cos", "sin", "o", "lse", "b", "w", "gp", "up", "yf", "sx", "kvall", "routes",
-                 "choice", "df", "dgp", "dup", "z", "dy", "tok", "inc", "da", "da2", "dkv", "dkvown")
-        out = {n: getattr(k, f"{n}{r}") for n in names if hasattr(k, f"{n}{r}")}
-        for n, v in vars(k).items():
-            out.setdefault(n, v)
-        out.update(more)
-        return types.SimpleNamespace(**out)
-
-    env = {}
-
-    def need(*names):
-        return {n: env[n] for n in names}
-
-    def k_first(k):
-        k.gn = gains(k.wa)
-        k.a0[...] = dot(k.x[...], k.spread[0:d]).astype(BF)
+        more = dict(inc=Out((R[r], dp))) if r else {}
+        return dict(tok=Out((R[r], dp)), df=Out((R[r], dp), BF), dgp=Out((R[r], ff), BF, True), dup=Out((R[r], ff), BF, True),
+                    z=Out((R[r], ff), BF, True), dy=Out((R[r], dp), BF), small=Out((8, dp)), **more)
+
+    def feed_scratch(r):
+        return dict(acc=V((R[r], dp), F32), pre=V((2, 2, R[r], FT), BF), wide=V((2, 3, R[r], FT), BF), wsem=dma((2, 3)))
+
+    def turned_outs(r):
+        return dict(da=Out((R[r], 1024), BF), dkv=Out((nb, nsq, S[r], 640), BF))
+
+    def turned_scratch(r):
+        return dict(kvg=V((KN[r], 640), BF), kvt=V((KV_HEADS, 128, KN[r]), BF), bias=V((KN[r], GROUP * S[r]), F32),
+                    dcol=V((R[r], 128), F32), dt=V((8, GROUP * S[r]), F32), ct=V((2, 32, S[r]), F32),
+                    do16=V((HEADS, R[r], 128), BF), dqt=V((HEADS, 64, S[r]), F32))
+
+    P, F, B, T, L = [None] * 3, [None] * 3, [None] * 3, [None] * 3, [None] * 3
+    rt = [None] + list(routes)
+
+    def begin(k):
+        k.a[...] = dot(k.x[...], k.spread[0:d]).astype(BF)
         for m in range(nsq):
-            k.cos0[m * bl:m * bl + bl] = k.cosb[...]
-            k.sin0[m * bl:m * bl + bl] = k.sinb[...]
-        project(geo, 0, view(k, 0))
-
-    env.update(x=x, cot=cot, lens=lens, routes1=routes[0], routes2=routes[1], wa=wa, wo=wo, gu=gu, wd=wd, spread=spread,
-               cosb=cosb, sinb=sinb)
-    env.update(call("first_project", k_first, need("x", "spread", "wa", "cosb", "sinb"), proj_outs(0)))
-    env["kvall0"] = share(env["kv0"].reshape(nsq, S[0], 640))
-
-    def k_mid(r, k):
+            k.cos[m * bl:m * bl + bl] = k.cosb[...]
+            k.sin[m * bl:m * bl + bl] = k.sinb[...]
+
+    ins = dict(x=x, spread=spread, cosb=cosb, sinb=sinb)
+    afters = seen_outs(0)
+    if (geo.n_dp, geo.n_blk) != (G, 4):
+        wa, wo, gu, wd = (lax.all_gather(w, "dp", axis=0, tiled=True) for w in slabs)
+
+        def k_first(k):
+            k = join(k, k.p)
+            begin(k)
+            k.gn = gains(k.wa)
+            project(geo, 0, k)
+        P[0] = join(call("first_project", k_first, dict(wa=wa, **ins), dict(p=proj_outs(0))).p)
+        P[0].kvall = share(P[0].kv.reshape(nsq, S[0], 640))
+        F[0] = call("attend", lambda k: attend(geo, 0, k, blk_of()), dict(q16=P[0].q16, kvall=P[0].kvall), afters, seen_scratch(0))
+    else:
+        def k_head(k):
+            dp_, blk, y, c, ym, cm = mates()
+            z, x_ = dp_ // NX, lax.rem(dp_, NX)
+            k = join(k, k.p, k.f, k.fs)
+            ticks = gather_ticks(AG_CHUNKS, k.shards, k.slabs, k.sems)
+            meet((dp_ + 1 - 2 * x_, blk), ym, cm, z=z)
+
+            def tick(n=1):
+                for _ in range(min(n, len(ticks))):
+                    ticks.pop(0)()
+            tick(2)
+            begin(k)
+            tick(A_TICKS - 2)
+            load = pltpu.make_async_copy(k.slabs[0], k.wa, k.wsem)
+            load.start()
+            load.wait()
+            k.gn = gains(k.wa)
+            project_kv(geo, 0, k)
+            sharing = Share(k.own, k.kvall, k.ssem, k.rsem)
+            k.own[...] = k.kv[...].reshape(nsq, S[0], 640)
+            k.kvall[blk] = k.own[...]
+            sharing.start()
+            tick()
+            project_q(geo, 0, k)
+            tick()
+            sharing.forward()
+            tick()
+            sharing.arrive()
+            attend(geo, 0, k, blk, tick)
+            tick(len(ticks))
+            sharing.sent()
+        got = call("head", k_head, dict(shards=list(slabs), **ins),
+                   dict(slabs=[Out((v.shape[0] * geo.n_dp, v.shape[1]), BF, True) for v in slabs], p=proj_outs(0, False), f=afters,
+                        kvall=Out((nb, nsq, S[0], 640), BF)),
+                   dict(fs=seen_scratch(0), wa=V((dp, COLS_A), BF), kv=V((R[0], 640), BF), own=V((nsq, S[0], 640), BF),
+                        wsem=dma, ssem=dma((3,)), rsem=dma((3,)), sems=gather_sems(4, len(AG_CHUNKS))),
+                   collective_id=1, has_side_effects=True)
+        wa, wo, gu, wd = got.slabs
+        P[0], F[0] = join(got.p, kvall=got.kvall), join(got.f)
+    gu, wd = Far(gu), Far(wd)
+    wou = h = None
+
+    def k_fore(r, k):
         blk = blk_of()
+        k = join(k, k.s, k.tl)
         tiles = Tiles(geo, k)
         tiles.start(0, 0)
         k.gn = gains(k.wa)
         if r == 0:
             k.wou[...] = dot(k.spread[...], k.wo[...]).astype(BF)
-        v = view(k, r, h=getattr(k, f"h{r}", None), h2=getattr(k, f"h{r + 1}"))
-        attend(geo, r, v, blk)
+        v = join(k, k.p, k.f, k.fs)
+        if r:
+            attend(geo, r, v, blk)
         feed(geo, r, v, blk, tiles)
-        n = view(k, r + 1, h=getattr(k, f"h{r + 1}"))
+        n = join(k, k.n, h=k.h2, routes=k.routes2)
         select_rows(geo, r + 1, n, blk)
         project(geo, r + 1, n)
 
     for r in range(2):
-        ins = need("wa", "gu", "wd", f"a{r}", f"q16{r}", f"kvall{r}", "cosb", "sinb", f"routes{r + 1}",
-                   *(("wo", "spread", "lens") if r == 0 else ("wou", f"routes{r}", f"choice{r}", f"h{r}")))
-        outs = {**feed_outs(r), **proj_outs(r + 1), f"choice{r + 1}": ((nsq, S[r + 1], bl), BF)}
-        if r == 0:
-            outs["wou"] = ((1024, dp), BF)
-        env.update(call(f"forward_{r}", functools.partial(k_mid, r), ins, outs, {**attn_scratch(r), **Tiles.scratch(geo)},
-                        hbm=("gu", "wd", f"gp{r}", f"up{r}")))
-        env[f"kvall{r + 1}"] = share(env[f"kv{r + 1}"].reshape(nsq, S[r + 1], 640))
-
-    def back_outs(r):
-        more = {f"inc{r}": ((R[r], dp), F32), **attend_outs(r)} if r else {}
-        return {**more, f"tok{r}": ((R[r], dp), F32), f"df{r}": ((R[r], dp), BF),
-                f"dgp{r}": ((R[r], ff), BF), f"dup{r}": ((R[r], ff), BF), f"z{r}": ((R[r], ff), BF),
-                f"dy{r}": ((R[r], dp), BF), f"small{r}": ((8, dp), F32)}
-
-    def attend_outs(r):
-        return {f"da{r}": ((R[r], 1024), BF), f"dkv{r}": ((nb, nsq, S[r], 640), BF)}
-
-    def back_scratch(r):
-        return {**feed_scratch(r), **(turned_scratch(r) if r else {})}
-
-    def turned_scratch(r):
-        return dict(kvg=V((KN[r], 640), BF), kvt=V((KV_HEADS, 128, KN[r]), BF), bias=V((KN[r], S[r]), F32),
-                    dcol=V((R[r], 128), F32), dt=V((16, S[r]), F32), ct=V((2, 32, S[r]), F32),
-                    do16=V((HEADS, R[r], 128), BF), dqt=V((HEADS, 64, S[r]), F32))
-
-    def feed_scratch(r):
-        return dict(acc=V((R[r], dp), F32), pre=V((2, 2, R[r], FT), BF), wide=V((2, 3, R[r], FT), BF), wsem=pltpu.SemaphoreType.DMA((2, 3)))
-
-    def back_one(r, k, blk, tiles, dh):
-        v = view(k, r, dh=dh, small=getattr(k, f"small{r}"))
-        v.small[...] = jnp.zeros(v.small.shape, F32)
-        back_feed(geo, r, v, blk, tiles)
-        if r > 0:
-            back_attend(geo, r, v, blk)
+        p = dict(a=P[r].a, q16=P[r].q16, kvall=P[r].kvall) if r else dict(a=P[0].a, o=F[0].o)
+        more = dict(choice=P[r].choice, h=h, routes=rt[r], wou=wou) if r else dict(wo=wo, spread=spread, lens=lens)
+        got = call("forward", functools.partial(k_fore, r),
+                   dict(wa=wa, gu=gu, wd=wd, p=p, cosb=cosb, sinb=sinb, routes2=rt[r + 1], s=more),
+                   dict(f=fore_outs(r), n=proj_outs(r + 1), h2=Out((full, dp)), **({} if r else dict(wou=Out((1024, dp), BF)))),
+                   dict(fs=fore_scratch(r), tl=Tiles.scratch(geo)))
+        h, F[r], P[r + 1] = got.h2, join(F[r] or {}, got.f), join(got.n)
+        wou = wou if r else got.wou
+        P[r + 1].kvall = share(P[r + 1].kv.reshape(nsq, S[r + 1], 640))
 
     def k_turn(k):
         blk = blk_of()
+        k = join(k, k.tl)
         tiles = Tiles(geo, k)
         tiles.start(0, 0)
         k.gn = gains(k.wa)
-        v = view(k, 2, h=k.h2, h2=k.h3, acc=k.acc)
+        v = join(k, k.p, k.f, k.fs, h2=k.h3)
         attend(geo, 2, v, blk)
         feed(geo, 2, v, blk, tiles)
-        tiles = Tiles(geo, k, (k.gp2, k.up2))
+        tiles = Tiles(geo, join(k, k.bs), (v.gp, v.up))
         tiles.start(0, 0)
         k.out[...] = dot_nt(k.h3[...].astype(BF), k.spread[0:d]).astype(BF)
-        k.dhe[...] = dot(k.cot[...], k.spread[0:d])
-        back_one(2, view(k, 2, bias=k.biast), blk, tiles, k.dhe)
-
-    ins = need("wa", "gu", "wd", "wou", "a2", "q162", "kvall2", "routes2", "choice2", "h2", "spread", "cot", "cos2", "sin2")
-    sc = {**attn_scratch(2), **Tiles.scratch(geo)}
-    bs = back_scratch(2)
-    bs["biast"] = bs.pop("bias")
-    outs = {**feed_outs(2), **back_outs(2), "out": ((full, d), BF), "dhe": ((full, dp), F32)}
-    env.update(call("turn", k_turn, ins, outs, {**bs, **sc}, hbm=("gu", "wd", "gp2", "up2", "dgp2", "dup2", "z2")))
-    env["dh3"] = env["dhe"]
-
-    saved = ("a", "b", "gp", "up", "yf", "sx")
-    kept = ("q16", "kvall", "o", "lse", "cos", "sin")
+        k.dh[...] = dot(k.cot[...], k.spread[0:d])
+        v = join(v, k.bs, k.ts, k.b, k.t)
+        back_feed(geo, 2, v, blk, tiles)
+        back_attend(geo, 2, v, blk)
+
+    p = P[2]
+    got = call("turn", k_turn,
+               dict(wa=wa, gu=gu, wd=wd, wou=wou, h=h, spread=spread, cot=cot, routes=rt[2],
+                    p=dict(a=p.a, q16=p.q16, kvall=p.kvall, choice=p.choice, cos=p.cos, sin=p.sin)),
+               dict(f=fore_outs(2), b=feed_outs(2), t=turned_outs(2), out=Out((full, d), BF), dh=Out((full, dp))),
+               dict(fs=fore_scratch(2), bs=feed_scratch(2), ts=turned_scratch(2), tl=Tiles.scratch(geo), h3=V((full, dp), F32)))
+    F[2], B[2], T[2], out, dh = join(got.f), join(got.b), join(got.t), got.out, got.dh
+
+    def k_back(r, k):
+        blk = blk_of()
+        v = join(k, k.p, k.f, k.b, k.bs, k.tl)
+        tiles = Tiles(geo, v, (v.gp, v.up))
+        tiles.start(0, 0)
+        v.gn = k.gn = gains(k.wa)
+        k.first[...] = jnp.zeros(k.first.shape, F32)
+        back_project(geo, r + 1, join(k, k.n), blk)
+        v.dh = k.dh2
+        back_feed(geo, r, v, blk, tiles)
+        if r > 0:
+            back_attend(geo, r, join(v, k.t, k.ts), blk)
+
     for r in (1, 0):
-        env[f"dkvown{r + 1}"] = give_back(env[f"dkv{r + 1}"]).reshape(R[r + 1], 640)
-
-        def k_back(r, k):
-            blk = blk_of()
-            tiles = Tiles(geo, k, (getattr(k, f"gp{r}"), getattr(k, f"up{r}")))
-            tiles.start(0, 0)
-            k.gn = gains(k.wa)
-            p = view(k, r + 1, a=getattr(k, f"a{r + 1}"), dh=getattr(k, f"dh{r + 2}"), dh2=getattr(k, f"dh{r + 1}"),
-                     first=getattr(k, f"first{r + 1}"))
-            p.first[...] = jnp.zeros(p.first.shape, F32)
-            back_project(geo, r + 1, p, blk)
-            back_one(r, k, blk, tiles, getattr(k, f"dh{r + 1}"))
-        n = r + 1
-        ins = need("wa", "gu", "wd", f"dkvown{n}", f"da{n}", f"tok{n}", f"inc{n}", f"dh{n + 1}", f"choice{n}", f"st{n}",
-                   f"a{n}", f"cos{n}", f"sin{n}", *[s + str(r) for s in saved], *(("lens",) if r == 0 else ("wou", "routes1", "choice1", *[s + str(r) for s in kept])))
-        outs = {**back_outs(r), f"da2{n}": ((R[n], COLS_A), BF), f"first{n}": ((8, dp), F32), f"dh{n}": ((full, dp), F32)}
-        env.update(call(f"backward_{r}", functools.partial(k_back, r), ins, outs, {**back_scratch(r), **Tiles.scratch(geo)},
-                        hbm=("gu", "wd", *[v + str(r) for v in ("gp", "up", "dgp", "dup", "z")])))
-    env.update(call("backward_attend_0", lambda k: back_attend(geo, 0, view(k, 0), blk_of()),
-                    need("wou", "dy0", *[s + "0" for s in kept]), attend_outs(0), turned_scratch(0)))
-    env["dkvown0"] = give_back(env["dkv0"]).reshape(R[0], 640)
+        n, q, p, f = r + 1, P[r + 1], P[r], F[r]
+        mine = give_back(T[n].dkv).reshape(R[n], 640)
+        late = dict(q16=p.q16, kvall=p.kvall, cos=p.cos, sin=p.sin, choice=p.choice) if r else {}
+        more = dict(o=f.o, lse=f.lse) if r else {}
+        rest = dict(wou=wou, routes=rt[r]) if r else dict(lens=lens)
+        got = call("backward", functools.partial(k_back, r),
+                   dict(wa=wa, gu=gu, wd=wd, dh=dh, **rest,
+                        n=dict(dkvown=mine, da=T[n].da, tok=B[n].tok, inc=B[n].inc, choice=q.choice, st=q.st, a=q.a,
+                               cos=q.cos, sin=q.sin),
+                        p=dict(a=p.a, **late),
+                        f=dict(b=f.b, gp=Far(f.gp), up=Far(f.up), yf=f.yf, sx=f.sx, **more)),
+                   dict(b=feed_outs(r), da2=Out((R[n], COLS_A), BF), first=Out((8, dp)), dh2=Out((full, dp)),
+                        **(dict(t=turned_outs(r)) if r else {})),
+                   dict(bs=feed_scratch(r), tl=Tiles.scratch(geo), **(dict(ts=turned_scratch(r)) if r else {})))
+        dh, B[r], L[n] = got.dh2, join(got.b), join(da2=got.da2, first=got.first)
+        if r:
+            T[r] = join(got.t)
+    p, f = P[0], F[0]
+    T[0] = call("backward_attend", lambda k: back_attend(geo, 0, k, blk_of()),
+                dict(wou=wou, dy=B[0].dy, q16=p.q16, kvall=p.kvall, o=f.o, lse=f.lse, cos=p.cos, sin=p.sin),
+                turned_outs(0), turned_scratch(0))
+    mine = give_back(T[0].dkv).reshape(R[0], 640)
 
     def k_last(k):
         blk = blk_of()
         k.gn = gains(k.wa)
-        k.first0[...] = jnp.zeros(k.first0.shape, F32)
-        back_project(geo, 0, view(k, 0, dh=k.dh1, dh2=k.dh0, first=k.first0), blk)
-        high, low = halves(k.dh0[...])
+        k.first[...] = jnp.zeros(k.first.shape, F32)
+        back_project(geo, 0, k, blk)
+        high, low = halves(k.dh2[...])
         k.grad[...] = dot_nt(high, k.spread[0:d]) + dot_nt(low, k.spread[0:d])
-    ins = need("wa", "dkvown0", "da0", "tok0", "dh1", "lens", "st0", "a0", "cos0", "sin0", "spread")
-    env.update(call("last_project", k_last, ins, {"da20": ((R[0], COLS_A), BF), "first0": ((8, dp), F32), "grad": ((full, d), F32)},
-                    dict(dh0=V((full, dp), F32))))
-    return env
-
-
-def weight_grads(geo, env, h):
+    L[0] = call("last_project", k_last,
+                dict(wa=wa, dkvown=mine, da=T[0].da, tok=B[0].tok, dh=dh, lens=lens, st=p.st, a=p.a, cos=p.cos, sin=p.sin,
+                     spread=spread),
+                dict(da2=Out((R[0], COLS_A), BF), first=Out((8, dp)), grad=Out((full, d))), dict(dh2=V((full, dp), F32)))
+    return out, L[0].grad, spread, [join(P[r], F[r], B[r], L[r]) for r in range(3)]
+
+
+def products(geo, lefts, rights, width, tile, rows, spread=None, extra=None):
     R = [geo.rows(r) for r in range(3)]
+    dp = geo.dp
+
+    def body(k):
+        at = 0
+        for i in range(3):
+            for c in range(0, rows, 256):
+                v = k.lefts[i][:, c:c + 256] if spread is None else dot(k.lefts[i][...], k.spread[:, c:c + 256]).astype(BF)
+                k.left[c:c + 256, at:at + R[i]] = v.T
+            at += R[i]
+        c0 = 0
+        for refs in k.rights:
+            n = refs[0].shape[1]
+            for t in range(0, n, tile):
+                w = min(tile, n - t)
+                right = jnp.concatenate([v[:, t:t + w] for v in refs], axis=0)
+                k.res[:, c0 + t:c0 + t + w] = dot(k.left[...], right).astype(BF)
+            c0 += n
+        if extra is not None:
+            small = k.small[0][...] + k.small[1][...] + k.small[2][...]
+            f = k.first[0][...] + k.first[1][...] + k.first[2][...]
+            small = jnp.where(rowid(small.shape) == 0, f, small)
+            cols = jnp.concatenate([small, jnp.zeros((120, dp), F32)], axis=0).T
+            cols = pltpu.roll(cols, 64, 1)
+            k.res[:, 896:1024] = jnp.where(lanes(cols.shape) < 64, k.res[:, 896:1024].astype(F32), cols).astype(BF)
+    ins = dict(lefts=lefts, rights=rights, **(extra or {}), **({} if spread is None else dict(spread=spread)))
+    return call("weight_grads", body, ins, dict(res=Out((rows, width), BF)), dict(left=pltpu.VMEM((rows, sum(R)), BF))).res
+
+
+def weight_grads(geo, saved, spread):
     dp, ff = geo.dp, geo.ff
-
-    def products(name, lefts, rights, width, tile, rows, spread=None, extra=None):
-        ins, hbm = {}, []
-        nl = len(lefts)
-        for i, v in enumerate(lefts):
-            ins[f"l{i}"] = v
-        for j, group in enumerate(rights):
-            for i, v in enumerate(group):
-                ins[f"r{j}{i}"] = v
-        if spread is not None:
-            ins["spread"] = spread
-        if extra is not None:
-            ins.update(extra)
-        total = sum(R)
-
-        def body(k):
-            at = 0
-            for i in range(3):
-                v = getattr(k, f"l{i}")
-                if spread is not None:
-                    k.left[at:at + R[i]] = dot(v[...], k.spread[...]).astype(BF)
-                else:
-                    k.left[at:at + R[i]] = v[...]
-                at += R[i]
-            c0 = 0
-            for j in range(len(rights)):
-                n = rights[j][0].shape[1]
-                refs = [getattr(k, f"r{j}{i}") for i in range(3)]
-                for t in range(0, n, tile):
-                    w = min(tile, n - t)
-                    right = jnp.concatenate([v[:, t:t + w] for v in refs], axis=0)
-                    res = dot_tn(k.left[...], right)
-                    k.res[:, c0 + t:c0 + t + w] = res.astype(BF)
-                c0 += n
-            if extra is not None:
-                small = k.small0[...] + k.small1[...] + k.small2[...]
-                f = k.first0[...] + k.first1[...] + k.first2[...]
-                small = jnp.where(rowid(small.shape) == 0, f, small)
-                cols = jnp.concatenate([small, jnp.zeros((120, dp), F32)], axis=0).T
-                cols = pltpu.roll(cols, 64, 1)
-                k.res[:, 896:1024] = jnp.where(lanes(cols.shape) < 64, k.res[:, 896:1024].astype(F32), cols).astype(BF)
-        return call(name, body, ins, {"res": ((rows, width), BF)}, dict(left=pltpu.VMEM((total, rows), BF)))["res"]
-
-    three = lambda n: [env[f"{n}{r}"] for r in range(3)]
-    if h == "gu":
-        return products("grad_gate_up", three("w"), [three("dgp"), three("dup")], 2 * ff, 512, dp)
-    if h == "d":
-        return products("grad_down", three("z"), [three("df")], dp, 256, ff)
-    if h == "o":
-        return products("grad_output", three("o"), [three("dy")], dp, 512, dp, spread=env["spread"])
-    return products("grad_query_kv", three("u"), [three("da2")], COLS_A, 512, dp,
-                    extra={f"{n}{r}": env[f"{n}{r}"] for n in ("small", "first") for r in range(3)})
+    a = products(geo, [v.u for v in saved], [[v.da2 for v in saved]], COLS_A, 512, dp,
+                 extra=dict(small=[v.small for v in saved], first=[v.first for v in saved]))
+    o = products(geo, [v.o for v in saved], [[v.dy for v in saved]], dp, 512, dp, spread=spread)
+    gu = products(geo, [v.w for v in saved], [[v.dgp for v in saved], [v.dup for v in saved]], 2 * ff, 512, dp)
+    d = products(geo, [v.z for v in saved], [[v.df for v in saved]], dp, 256, ff)
+    return a, o, gu, d
 
 
 MESH = pl.DeviceIdType.MESH
 
 NZ, NX = 4, 2
+AHEAD = 2
+OFFSETS = (0, 2, 4, 6, 8, 10, 12, 13, 14)
 G = NZ * NX
 
 
-def gather_kernel(chunks, nslab, *refs):
-    ins, outs = refs[:nslab], refs[nslab:2 * nslab]
-    ls, zs, zr, xs, xr, ys, yr, cs, cr = refs[2 * nslab:]
+def meet(*others, z=None):
+    dp, blk = lax.axis_index("dp"), lax.axis_index("blk")
+    bar = pltpu.get_barrier_semaphore()
+    for t in others:
+        pl.semaphore_signal(bar, inc=1, device_id=t, device_id_type=MESH)
+    count = len(others)
+    if z is not None:
+        @pl.when(z > 0)
+        def _():
+            pl.semaphore_signal(bar, inc=1, device_id=(dp - NX, blk), device_id_type=MESH)
+
+        @pl.when(z < NZ - 1)
+        def _():
+            pl.semaphore_signal(bar, inc=1, device_id=(dp + NX, blk), device_id_type=MESH)
+        count = count + jnp.where(z > 0, 1, 0) + jnp.where(z < NZ - 1, 1, 0)
+    pl.semaphore_wait(bar, count)
+
+
+def gather_ticks(chunks, ins, outs, sems):
+    ls, zs, zr, xs, xr, ys, yr, cs, cr = sems
+    nslab = len(ins)
     dp, blk = lax.axis_index("dp"), lax.axis_index("blk")
     z, x = dp // NX, lax.rem(dp, NX)
     y, c = blk // 2, lax.rem(blk, 2)
     left, right = (dp - NX, blk), (dp + NX, blk)
     xm, ym, cm = (dp + 1 - 2 * x, blk), (dp, lax.rem(blk + 2, 4)), (dp, blk + 1 - 2 * c)
-    bar = pltpu.get_barrier_semaphore()
-    for t in (xm, ym, cm):
-        pl.semaphore_signal(bar, inc=1, device_id=t, device_id_type=MESH)
-
-    @pl.when(z > 0)
-    def _():
-        pl.semaphore_signal(bar, inc=1, device_id=left, device_id_type=MESH)
-
-    @pl.when(z < NZ - 1)
-    def _():
-        pl.semaphore_signal(bar, inc=1, device_id=right, device_id_type=MESH)
-
-    pl.semaphore_wait(bar, 3 + jnp.where(z > 0, 1, 0) + jnp.where(z < NZ - 1, 1, 0))
-
-    locs = [pltpu.make_async_copy(ins[s], outs[s].at[dp], ls.at[s]) for s in range(nslab)]
-    for l in locs:
-        l.start()
+
+    locs = [pltpu.make_async_copy(ins[s], outs[s].at[pl.ds(pl.multiple_of(dp * ins[s].shape[0], 16), ins[s].shape[0])], ls.at[s])
+            for s in range(nslab)]
 
     def piece(i, g, q):
         s, c0, n, split = chunks[i]
-        return outs[s].at[g, q, :, pl.ds(c0, n)]
+        rows = ins[s].shape[0]
+        h = rows // split
+        return outs[s].at[pl.ds(pl.multiple_of(g * rows + q * h, 16), h), pl.ds(c0, n)]
 
     def myq(i):
         return blk if chunks[i][3] == 4 else c
@@ -705,7 +788,8 @@
 
     def own(i):
         s, c0, n, split = chunks[i]
-        return ins[s].at[myq(i), :, pl.ds(c0, n)]
+        h = ins[s].shape[0] // split
+        return ins[s].at[pl.ds(pl.multiple_of(myq(i) * h, 16), h), pl.ds(c0, n)]
 
     def zcopy(i, d, s, src_own):
         zz = z - s if d == 0 else z + s
@@ -751,8 +835,6 @@
         if chunks[i][3] == 4:
             ycopy(i, g).start()
         ccopy(i, 0, g).start()
-
-    nch = len(chunks)
 
     def begin(i):
         @pl.when(z < NZ - 1)
@@ -833,33 +915,34 @@
                 ycopy(i, g).wait_send()
                 ccopy(i, 1, g).wait_send()
 
+    nch = len(chunks)
     stages = [begin] + [functools.partial(lambda i, s: (zstep(i, s), xstep(i, s)), s=s) for s in range(NZ - 1)]
     stages.append(lambda i: xstep(i, NZ - 1))
     stages.append(lambda i: [ystep(i, k) for k in range(1, G)] if chunks[i][3] == 4 else None)
     stages.append(lambda i: [cstep(i, k) for k in range(1, G)])
     stages.append(sent)
-    for t in range(nch + len(stages) - 1):
+
+    def first():
+        for l in locs:
+            l.start()
+
+    def tick(t):
+        if t == 6:
+            locs[0].wait()
+        if t == nch + len(stages) - 2:
+            for l in locs[1:]:
+                l.wait()
         for s in reversed(range(len(stages))):
             i = t - s
             if 0 <= i < nch:
                 stages[s](i)
-    for l in locs:
-        l.wait()
-
-
-def gather(slabs, chunks):
-    n, nch = len(slabs), len(chunks)
+    return [first] + [functools.partial(tick, t) for t in range(nch + len(stages) - 1)]
+
+
+def gather_sems(n, nch):
     dma = pltpu.SemaphoreType.DMA
-    return pl.pallas_call(
-        functools.partial(gather_kernel, chunks, n),
-        out_shape=[jax.ShapeDtypeStruct((G,) + s.shape, s.dtype) for s in slabs],
-        in_specs=[pl.BlockSpec(memory_space=pl.ANY)] * n,
-        out_specs=[pl.BlockSpec(memory_space=pl.ANY)] * n,
-        scratch_shapes=[dma((n,)), dma((nch, 2, NZ - 1)), dma((nch, 2, NZ - 1)), dma((nch, NZ)), dma((nch, NZ)),
-                        dma((nch, G)), dma((nch, G)), dma((nch, 2, G)), dma((nch, 2, G))],
-        compiler_params=pltpu.CompilerParams(collective_id=1, has_side_effects=True),
-        name="gather_weights",
-    )(*slabs)
+    return [dma((n,)), dma((nch, 2, NZ - 1)), dma((nch, 2, NZ - 1)), dma((nch, NZ)), dma((nch, NZ)),
+            dma((nch, G)), dma((nch, G)), dma((nch, 2, G)), dma((nch, 2, G))]
 
 
 def add_into(dst, other, n):
@@ -880,19 +963,7 @@
     y, c = blk // 2, lax.rem(blk, 2)
     left, right = (dp - NX, blk), (dp + NX, blk)
     xm, ym, cm = (dp + 1 - 2 * x, blk), (dp, lax.rem(blk + 2, 4)), (dp, blk + 1 - 2 * c)
-    bar = pltpu.get_barrier_semaphore()
-    for t in (xm, ym, cm):
-        pl.semaphore_signal(bar, inc=1, device_id=t, device_id_type=MESH)
-
-    @pl.when(z > 0)
-    def _():
-        pl.semaphore_signal(bar, inc=1, device_id=left, device_id_type=MESH)
-
-    @pl.when(z < NZ - 1)
-    def _():
-        pl.semaphore_signal(bar, inc=1, device_id=right, device_id_type=MESH)
-
-    pl.semaphore_wait(bar, 3 + jnp.where(z > 0, 1, 0) + jnp.where(z < NZ - 1, 1, 0))
+    meet(xm, ym, cm, z=z)
 
     def rem(src, dst, a, b, to):
         return pltpu.make_async_remote_copy(src_ref=src, dst_ref=dst, send_sem=a, recv_sem=b, device_id=to, device_id_type=MESH)
@@ -1056,11 +1127,13 @@
             fin_send(i, k).wait_send()
 
     stages = [st1, st2, st3] + [functools.partial(lambda i, s: zstep(i, s), s=s) for s in range(1, NZ - 1)] + [finish, st8, st9, sent]
-    for i in range(nch):
+    for i in range(min(AHEAD, nch)):
         st0(i)
-    for t in range(nch + len(stages) - 1):
+    for t in range(nch + max(OFFSETS)):
+        if t + AHEAD < nch:
+            st0(t + AHEAD)
         for s in reversed(range(len(stages))):
-            i = t - s
+            i = t - OFFSETS[s]
             if 0 <= i < nch:
                 stages[s](i)
 
@@ -1099,10 +1172,11 @@
     )(*slabs)
 
 
-AG_CHUNKS = [(0, 0, 1664, 4), (1, 0, 1024, 2), (2, 0, 1280, 4), (2, 1280, 1280, 4), (3, 0, 512, 2), (2, 2560, 1280, 4),
-             (2, 3840, 1280, 4), (3, 512, 512, 2)]
-RS_CHUNKS = [(2, 0, 1280, 4), (3, 0, 512, 2), (2, 1280, 1280, 4), (2, 2560, 1280, 4), (3, 512, 512, 2), (2, 3840, 1280, 4),
-             (1, 0, 1024, 2), (0, 0, 896, 4), (0, 896, 768, 4)]
+A_TICKS = 8
+AG_CHUNKS = [(0, 0, 1664, 4), (1, 0, 1024, 2), (2, 0, 2560, 4), (2, 2560, 2560, 4), (3, 0, 1024, 2)]
+RS_CHUNKS = [(2, 0, 640, 4), (3, 0, 256, 2), (2, 640, 640, 4), (3, 256, 256, 2), (2, 1280, 640, 4), (3, 512, 256, 2),
+             (2, 1920, 640, 4), (3, 768, 256, 2), (2, 2560, 640, 4), (0, 0, 512, 2), (2, 3200, 640, 4), (0, 512, 512, 2),
+             (2, 3840, 640, 4), (0, 1024, 640, 2), (2, 4480, 640, 4), (1, 0, 512, 2), (1, 512, 512, 2)]
 
 
 def pad_to(v, shape):
@@ -1127,23 +1201,13 @@
     return a, pad_to(pad_cols(o, geo), (geo.gp, geo.dp)), gu, pad_cols(d, geo)
 
 
-def whole_weights(geo, slabs):
-    a, o, gu, d = slabs
-    if (geo.n_dp, geo.n_blk) != (G, 4):
-        return tuple(lax.all_gather(w, "dp", axis=0, tiled=True) for w in slabs)
-    gp, rd = geo.gp, d.shape[0]
-    got = gather([a.reshape(4, gp // 4, -1), o.reshape(2, gp // 2, -1), gu.reshape(4, gp // 4, -1), d.reshape(2, rd // 2, -1)],
-                 AG_CHUNKS)
-    return tuple(w.reshape(-1, w.shape[-1]) for w in got)
-
-
 def summed_grads(geo, slabs):
     a, o, gu, d = slabs
     if (geo.n_dp, geo.n_blk) != (G, 4):
         shares = [lax.psum_scatter(v, "dp", scatter_dimension=0, tiled=True) for v in slabs]
         return tuple(lax.psum(v, "blk").astype(F32) for v in shares)
     gp, rd = geo.gp, d.shape[0] // G
-    got = reduce([a.reshape(NZ, NX, 2, 2, gp // 4, -1), o.reshape(NZ, NX, 2, gp // 2, -1), gu.reshape(NZ, NX, 2, 2, gp // 4, -1),
+    got = reduce([a.reshape(NZ, NX, 2, gp // 2, -1), o.reshape(NZ, NX, 2, gp // 2, -1), gu.reshape(NZ, NX, 2, 2, gp // 4, -1),
                   d.reshape(NZ, NX, 2, rd // 2, -1)], RS_CHUNKS)
     return tuple(w.reshape(-1, w.shape[-1]) for w in got)
 
@@ -1156,39 +1220,51 @@
             gu[:, :geo.ff], gu[:, geo.ff:], unpad_cols(d, geo), a[:, 960], a[:, 961], a[:, 962:965])
 
 
-def meet(*others):
-    bar = pltpu.get_barrier_semaphore()
-    for t in others:
-        pl.semaphore_signal(bar, inc=1, device_id=t, device_id_type=MESH)
-    pl.semaphore_wait(bar, len(others))
-
-
 def mates():
     dp, blk = lax.axis_index("dp"), lax.axis_index("blk")
     y, c = blk // 2, lax.rem(blk, 2)
     return dp, blk, y, c, (dp, lax.rem(blk + 2, 4)), (dp, blk + 1 - 2 * c)
 
 
+class Share:
+    def __init__(self, own, out, ssem, rsem):
+        dp, blk, y, c, ym, cm = mates()
+
+        def rem(src, b, k, to):
+            return pltpu.make_async_remote_copy(src_ref=src, dst_ref=out.at[b], send_sem=ssem.at[k], recv_sem=rsem.at[k],
+                                                device_id=to, device_id_type=MESH)
+        far, near = lax.rem(blk + 2, 4), blk + 1 - 2 * c
+        both = lax.rem(near + 2, 4)
+        self.out = [rem(own, blk, 0, ym), rem(own, blk, 1, cm), rem(out.at[far], far, 2, cm)]
+        self.come = [rem(out.at[far], far, 0, ym), rem(out.at[near], near, 1, cm), rem(out.at[both], both, 2, cm)]
+
+    def start(self):
+        self.out[0].start()
+        self.out[1].start()
+
+    def forward(self):
+        self.come[0].wait_recv()
+        self.out[2].start()
+
+    def arrive(self):
+        self.come[1].wait_recv()
+        self.come[2].wait_recv()
+
+    def sent(self):
+        for v in self.out:
+            v.wait_send()
+
+
 def share_kernel(own, out, lsem, ssem, rsem):
     dp, blk, y, c, ym, cm = mates()
     meet(ym, cm)
-
-    def rem(src, b, k, to):
-        return pltpu.make_async_remote_copy(src_ref=src, dst_ref=out.at[b], send_sem=ssem.at[k], recv_sem=rsem.at[k],
-                                            device_id=to, device_id_type=MESH)
-    far, near = lax.rem(blk + 2, 4), blk + 1 - 2 * c
-    rem(own, blk, 0, ym).start()
-    rem(own, blk, 1, cm).start()
+    s = Share(own, out, ssem, rsem)
+    s.start()
     local = pltpu.make_async_copy(own, out.at[blk], lsem)
     local.start()
-    rem(out.at[far], far, 0, ym).wait_recv()
-    rem(out.at[far], far, 2, cm).start()
-    rem(out.at[near], near, 1, cm).wait_recv()
-    both = lax.rem(near + 2, 4)
-    rem(out.at[both], both, 2, cm).wait_recv()
-    rem(own, blk, 0, ym).wait_send()
-    rem(own, blk, 1, cm).wait_send()
-    rem(out.at[far], far, 2, cm).wait_send()
+    s.forward()
+    s.arrive()
+    s.sent()
     local.wait()
 
 
@@ -1198,9 +1274,9 @@
     dma = pltpu.SemaphoreType.DMA
     return pl.pallas_call(
         share_kernel, out_shape=jax.ShapeDtypeStruct((4,) + kv.shape, kv.dtype),
-        in_specs=[pl.BlockSpec(memory_space=pl.ANY)], out_specs=pl.BlockSpec(memory_space=pl.ANY),
+        in_specs=[pl.BlockSpec(memory_space=pltpu.VMEM)], out_specs=pl.BlockSpec(memory_space=pl.ANY),
         scratch_shapes=[dma, dma((3,)), dma((3,))],
-        compiler_params=pltpu.CompilerParams(collective_id=ident, has_side_effects=True), name=f"share_rows_{ident}")(kv)
+        compiler_params=pltpu.CompilerParams(collective_id=ident, has_side_effects=True), name="share_rows")(kv)
 
 
 def give_kernel(dkv, out, got1, half, got2, ssem, rsem):
@@ -1235,7 +1311,7 @@
         give_kernel, out_shape=jax.ShapeDtypeStruct(piece, F32), in_specs=[vm], out_specs=vm,
         scratch_shapes=[pltpu.VMEM((2,) + piece, BF), pltpu.VMEM(piece, BF), pltpu.VMEM(piece, BF), dma((3,)), dma((3,))],
         compiler_params=pltpu.CompilerParams(collective_id=ident, has_side_effects=True, vmem_limit_bytes=40 << 20),
-        name=f"give_rows_{ident}")(dkv.reshape((2, 2) + piece))
+        name="give_rows")(dkv.reshape((2, 2) + piece))
 
 
 def per_device(block_input, cotangent, seq_lengths, routes_two, routes_three, query_weight, key_weight, value_weight, output_weight,
@@ -1246,14 +1322,12 @@
     geo = Geo(count, bl, n_dp, n_blk, d, gate_weight.shape[1], (None, routes_two.shape[2], routes_three.shape[2]))
     slabs = pack(geo, query_weight, key_weight, value_weight, output_weight, gate_weight, up_weight, down_weight, first_gain,
                  second_gain, router_weight)
-    wa, wo, gu, wd = whole_weights(geo, slabs)
     ids = iter(range(10, 30))
-    env = block(geo, block_input.reshape(count * bl, d), cotangent.reshape(count * bl, d), seq_lengths.reshape(count),
-                (routes_two.reshape(count, -1), routes_three.reshape(count, -1)), wa, wo, gu, wd,
+    out, grad, spread, saved = block(geo, block_input.reshape(count * bl, d), cotangent.reshape(count * bl, d), seq_lengths.reshape(count),
+                (routes_two.reshape(count, -1), routes_three.reshape(count, -1)), slabs,
                 lambda kv: share_rows(geo, next(ids), kv), lambda dkv: give_rows(geo, next(ids), dkv))
-    grads = [weight_grads(geo, env, h) for h in ("a", "o", "gu", "d")]
-    grads = unpack(geo, summed_grads(geo, grads))
-    return (env["out"].reshape(block_input.shape), env["grad"].reshape(block_input.shape)) + tuple(grads)
+    grads = unpack(geo, summed_grads(geo, weight_grads(geo, saved, spread)))
+    return (out.reshape(block_input.shape), grad.reshape(block_input.shape)) + tuple(grads)
 
 
 def solution(mesh):

time: 636 us -> 588 us (0.925)
  Pallas kernels: 595 us -> 544 us
    pallas_call x13 -> x12, Pallas kernels: 374 us -> 354 us  [call(): pl.pallas_call(kernel, out_shape=[jax.ShapeDtypeStruct(o.shape, o.dtype)...]
    pallas_call x3 -> x2, Pallas kernels: 42.5 us -> 23 us  [share_rows(): pl.pallas_call(share_kernel, out_shape=jax.ShapeDtypeStruct((4,) + kv.sha...]
    pallas_call x1, Pallas kernels: 138 us -> 126 us  [reduce(): pl.pallas_call(functools.partial(reduce_kernel, chunks, n), out_shape=out...]
where the time goes in v3:
time: 588 us; the launch traced here: 580 us
  Pallas kernels  544 us (93%)
  local copies, waits for them, and re-layouts  32.1 us (5%)
    pallas_call x12, Pallas kernels, call(): pl.pallas_call(kernel, out_shape=[jax.ShapeDtypeStruct(o.shape, o.dtype)...  354 us
    pallas_call x1, Pallas kernels, reduce(): pl.pallas_call(functools.partial(reduce_kernel, chunks, n), out_shape=out...  126 us
    pallas_call x3, Pallas kernels, give_rows(): pl.pallas_call(give_kernel, out_shape=jax.ShapeDtypeStruct(piece, F32), i...  40.3 us
    pallas_call x2, Pallas kernels, share_rows(): pl.pallas_call(share_kernel, out_shape=jax.ShapeDtypeStruct((4,) + kv.sha...  23 us
    unnamed x39, local copies, waits for them, and re-layouts  18.1 us

profile of v3, /device:TPU:0, one launch (start us, length us, event | category | flops | bytes accessed | tf_op | source)
XLA Modules:
  0.0 580.1 jit_solution(1834310320212981360)
XLA Ops:
  0.7 1.3 copy.71
  4.0 1.1 concatenate.14
  7.0 1.7 constant_dynamic-slice_fusion
  10.6 1.3 copy.55
  11.9 1.3 copy.52
  13.2 1.2 fusion.2.refs_3_
  14.4 123.1 %head.1 = (f32[2,8,768]{2,1,0:T(8,128)}, bf16[512,1024]{1,0:T(8,128)(2,1)}, bf16[4,2,256,640]{3,2,1,0:T(8,128)(2,1)}, bf16[512,1024]{1,0:T(8,128)(2,1)}, f32[512...) custom-call(f32[256,128]{1,0:T(8,128)} %get-tuple-element.239.refs_0, ...), custom_call_target="tpu_custom_call" | custom-call | tf_op jit(solution)/shard_map/head/pallas_call | solution.py:97
  137.5 21.8 %forward.2 = (bf16[512,1024]{1,0:T(8,128)(2,1)}, bf16[512,2560]{1,0:T(8,128)(2,1)}, f32[512,128]{1,0:T(8,128)}, bf16[512,2560]{1,0:T(8,128)(2,1)}, bf16[512,1024...) custom-call(f32[256,128]{1,0:T(8,128)} %get-tuple-element.239.refs_0, ...), custom_call_target="tpu_custom_call" | custom-call | tf_op jit(solution)/shard_map/forward/pallas_call | solution.py:97
  159.3 14.2 %share_rows.2.refs_3_.refs_21_ = bf16[4,2,128,640]{3,2,1,0:T(8,128)(2,1)} custom-call(bf16[2,128,640]{2,1,0:T(8,128)(2,1)} %bitcast.77), custom_call_target="tpu_custom_call" | custom-call | tf_op jit(solution)/shard_map/share_rows/pallas_call | solution.py:1275
  173.5 24.5 %forward.3 = (bf16[256,1024]{1,0:T(8,128)(2,1)}, bf16[256,2560]{1,0:T(8,128)(2,1)}, f32[2,8,384]{2,1,0:T(8,128)}, bf16[256,1024]{1,0:T(8,128)(2,1)}, f32[256,128...) custom-call(f32[256,128]{1,0:T(8,128)} %get-tuple-element.239.refs_0, ...), custom_call_target="tpu_custom_call" | custom-call | tf_op jit(solution)/shard_map/forward/pallas_call | solution.py:97
  198.0 8.8 %share_rows.3.refs_6_ = bf16[4,2,64,640]{3,2,1,0:T(8,128)(2,1)} custom-call(bf16[2,64,640]{2,1,0:T(8,128)(2,1)} %bitcast.80), custom_call_target="tpu_custom_call" | custom-call | tf_op jit(solution)/shard_map/share_rows/pallas_call | solution.py:1275
  206.8 39.4 %turn.1 = (bf16[128,1024]{1,0:T(8,128)(2,1)}, bf16[128,2560]{1,0:T(8,128)(2,1)}, bf16[128,2560]{1,0:T(8,128)(2,1)}, bf16[128,1024]{1,0:T(8,128)(2,1)}, f32[128,1...) custom-call(bf16[512,960]{1,0:T(8,128)(2,1)} %bitcast.59, ...), custom_call_target="tpu_custom_call" | custom-call | tf_op jit(solution)/shard_map/turn/pallas_call | solution.py:97
  246.2 2.3 copy.58
  248.5 8.1 %give_rows.3 = f32[2,64,640]{2,1,0:T(8,128)S(1)} custom-call(bf16[2,2,2,64,640]{4,3,2,1,0:T(8,128)(2,1)S(1)} %bitcast.53), custom_call_target="tpu_custom_call" | custom-call | tf_op jit(solution)/shard_map/give_rows/pallas_call | solution.py:1310
  257.4 31.6 %backward.2 = (bf16[256,1024]{1,0:T(8,128)(2,1)}, bf16[256,2560]{1,0:T(8,128)(2,1)}, bf16[256,2560]{1,0:T(8,128)(2,1)}, bf16[256,1024]{1,0:T(8,128)(2,1)}, f32[2...) custom-call(f32[512,1024]{1,0:T(8,128)} %get-tuple-element.125.refs_, ...), custom_call_target="tpu_custom_call" | custom-call | tf_op jit(solution)/shard_map/backward/pallas_call | solution.py:97
  289.0 1.3 copy-done.4
  290.3 12.2 %give_rows.4 = f32[2,128,640]{2,1,0:T(8,128)S(1)} custom-call(bf16[2,2,2,128,640]{4,3,2,1,0:T(8,128)(2,1)S(1)} %bitcast.52), custom_call_target="tpu_custom_call" | custom-call | tf_op jit(solution)/shard_map/give_rows/pallas_call | solution.py:1310
  303.3 23.9 %backward.3 = (bf16[512,1024]{1,0:T(8,128)(2,1)}, bf16[512,2560]{1,0:T(8,128)(2,1)}, bf16[512,2560]{1,0:T(8,128)(2,1)}, bf16[512,1024]{1,0:T(8,128)(2,1)}, f32[8...) custom-call(f32[512,1024]{1,0:T(8,128)} %get-tuple-element.140.refs_, ...), custom_call_target="tpu_custom_call" | custom-call | tf_op jit(solution)/shard_map/backward/pallas_call | solution.py:97
  327.2 31.7 %backward_attend.1 = (bf16[512,1024]{1,0:T(8,128)(2,1)}, bf16[4,2,256,640]{3,2,1,0:T(8,128)(2,1)}) custom-call(f32[512,128]{1,0:T(8,128)} %get-tuple-element.124.refs_0_.refs_1_, bf16[512,1024]{1,0:T(8,128)(2,1)} %get-tuple-element.151.refs_1_.refs_3_, bf16[4,2,256,640]{3,2,1,0:T(8,128)(2,1)} %get-tuple-element.152.refs_2_, ...), custom_call_target="tpu_custom_call" | custom-call | tf_op jit(solution)/shard_map/backward_attend/pallas_call | solution.py:97
  359.0 8.4 %weight_grads.5 = bf16[1024,1024]{1,0:T(8,128)(2,1)} custom-call(bf16[512,1024]{1,0:T(8,128)(2,1)} %get-tuple-element.106.refs_3_.refs_4_.refs_0_, bf16[256,1024]{1,0:T(8,128)(2,1)} %get-tuple-element.129.refs_4_.refs_1_, bf16[128,1024]{1,0:T(8,128)(2,1)} %get-tuple-element.174.refs_2_, bf16[512,1024]{1,0:T(8,128)(2,1)} %get-tuple-element.151.refs_1_.refs_3_, ...), custom_call_target="tpu_custom_call" | custom-call | tf_op jit(solution)/shard_map/weight_grads/pallas_call | solution.py:97
  367.3 1.7 copy-done.1
  369.1 19.9 %give_rows.5 = f32[2,256,640]{2,1,0:T(8,128)S(1)} custom-call(bf16[2,2,2,256,640]{4,3,2,1,0:T(8,128)(2,1)S(1)} %bitcast.49), custom_call_target="tpu_custom_call" | custom-call | tf_op jit(solution)/shard_map/give_rows/pallas_call | solution.py:1310
  389.0 1.0 copy-done
  390.1 11.3 %last_project.1 = (bf16[512,1664]{1,0:T(8,128)(2,1)}, f32[8,1024]{1,0:T(8,128)}, f32[512,960]{1,0:T(8,128)}) custom-call(bf16[512,1024]{1,0:T(8,128)(2,1)} %get-tuple-element.105.refs_2_.refs_17_.refs_0_, f32[512,128]{1,0:T(8,128)} %get-tuple-element.124.refs_0_.refs_1_, bf16[512,1024]{1,0:T(8,128)(2,1)} %get-tuple-element.156.refs_2_, ...), custom_call_target="tpu_custom_call" | custom-call | tf_op jit(solution)/shard_map/last_project/pallas_call | solution.py:97
  401.4 3.0 copy.59
  404.4 8.2 %weight_grads.4 = bf16[1024,1664]{1,0:T(8,128)(2,1)} custom-call(f32[8,1024]{1,0:T(8,128)} %get-tuple-element.162.refs_0_, f32[8,1024]{1,0:T(8,128)} %get-tuple-element.163.refs_1_, f32[8,1024]{1,0:T(8,128)} %get-tuple-element.164.refs_2_, bf16[512,1024]{1,0:T(8,128)(2,1)} %get-tuple-element.165.refs_3_, bf16[256,1024]{1,0:T(8,128)(2,1)} %get-tuple-element.166.refs_4_, ...), custom_call_target="tpu_custom_call" | custom-call | tf_op jit(solution)/shard_map/weight_grads/pallas_call | solution.py:97
  412.6 10.8 %weight_grads.7 = bf16[2560,1024]{1,0:T(8,128)(2,1)} custom-call(bf16[512,2560]{1,0:T(8,128)(2,1)} %get-tuple-element.186.refs_0_, bf16[256,2560]{1,0:T(8,128)(2,1)} %get-tuple-element.187.refs_1_, bf16[128,2560]{1,0:T(8,128)(2,1)} %get-tuple-element.188.refs_2_, bf16[512,1024]{1,0:T(8,128)(2,1)} %get-tuple-element.189.refs_3_, ...), custom_call_target="tpu_custom_call" | custom-call | tf_op jit(solution)/shard_map/weight_grads/pallas_call | solution.py:97
  423.4 19.4 %weight_grads.6 = bf16[1024,5120]{1,0:T(8,128)(2,1)} custom-call(bf16[512,1024]{1,0:T(8,128)(2,1)} %get-tuple-element.177.refs_0_, bf16[256,1024]{1,0:T(8,128)(2,1)} %get-tuple-element.178.refs_1_, bf16[128,1024]{1,0:T(8,128)(2,1)} %get-tuple-element.179.refs_2_, bf16[512,2560]{1,0:T(8,128)(2,1)} %get-tuple-element.180.refs_3_, ...), custom_call_target="tpu_custom_call" | custom-call | tf_op jit(solution)/shard_map/weight_grads/pallas_call | solution.py:97
  442.9 126.5 %reduce_grads.1 = (f32[2,64,1664]{2,1,0:T(8,128)}, f32[2,64,1024]{2,1,0:T(8,128)}, f32[4,32,5120]{2,1,0:T(8,128)}, f32[2,160,1024]{2,1,0:T(8,128)}) custom-call(bf16[4,2,2,64,1664]{4,3,2,1,0:T(8,128)(2,1)} %bitcast.56, bf16[4,2,2,64,1024]{4,3,2,1,0:T(8,128)(2,1)} %bitcast.57, bf16[4,2,2,2,32,5120]{5,4,3,2,1,0:T(8,128)(2,1)} %bitcast.54, ...), custom_call_target="tpu_custom_call" | custom-call | tf_op jit(solution)/shard_map/reduce_grads/pallas_call | solution.py:1164
  569.3 1.1 slice_bitcast_fusion
  575.0 1.4 reshape.163
  576.5 3.2 fusion.3
  (48 shorter events, 11.9 us)
Async XLA Ops:
  0.6 5.2 copy-start.13
  3.9 4.7 copy-start.10
  8.7 1.9 copy-start.8
  9.5 2.4 copy-start.9
  10.6 2.6 copy-start.11
  10.6 2.6 copy-start.12
  246.2 2.3 copy-start.5
  256.7 0.7 copy-start.3
  289.0 1.3 copy-start.4
  302.5 0.8 copy-start.2
  367.3 1.7 copy-start.1
  389.0 1.1 copy-start
  569.3 2.2 copy-start.7
  570.6 4.2 copy-start.6

commit v4 on v3

--- a/solution.py
+++ b/solution.py
@@ -150,9 +150,9 @@
     return dot_nt(shift, here).astype(BF)
 
 
-def allowed(geo, r, routes, blk, turned):
+def allowed(geo, r, routes, blk, turned, heads=GROUP):
     s, kn, bl = geo.slots[r], geo.keys(r), geo.bl
-    shape = (kn, GROUP * s) if turned else (GROUP * s, kn)
+    shape = (kn, heads * s) if turned else (heads * s, kn)
     key = rowid(shape) if turned else lanes(shape)
     query = lax.rem(lanes(shape) if turned else rowid(shape), s)
     ok = key <= blk * s + query
@@ -398,7 +398,7 @@
         k.dy[here] = (gate * incoming(m) + db).astype(BF)
 
 
-def back_attend(geo, r, k, blk):
+def back_out(geo, r, k):
     s, kn = geo.slots[r], geo.keys(r)
     rows = geo.rows(r)
     left = lanes((rows, 128)) < 64
@@ -417,12 +417,24 @@
             k.do16[2 * t + 1] = jnp.where(left, 0.0, x).astype(BF)
     k.dcol[...] = dcol
 
+
+def back_attend(geo, r, k, blk, pause=None):
+    s, kn = geo.slots[r], geo.keys(r)
+    batch = GROUP if pause is None else 1
+
     def seq(m, _):
-        row0 = pl.multiple_of(m * s, s)
-        k.kvg[...] = k.kvall[:, m].reshape(kn, KV_HEADS * 128)
+        row0 = m * s if isinstance(m, int) else pl.multiple_of(m * s, s)
+        if pause is None:
+            k.kvg[...] = k.kvall[:, m].reshape(kn, KV_HEADS * 128)
+        else:
+            loads = [pltpu.make_async_copy(k.kvall.at[b, m], k.kvg.at[pl.ds(b * s, s)], k.lsem.at[b]) for b in range(geo.n_blk)]
+            for v in loads:
+                v.start()
+            for v in loads:
+                v.wait()
         for g in range(KV_HEADS):
             k.kvt[g] = k.kvg[:, 128 * g:128 * g + 128].astype(F32).T.astype(BF)
-        k.bias[...] = allowed(geo, r, k.routes[pl.ds(m, 1)] if r else None, blk, True)
+        k.bias[...] = allowed(geo, r, k.routes[pl.ds(m, 1)] if r else None, blk, True, batch)
         dt = k.dcol[pl.ds(row0, s)].T
         for h in range(HEADS):
             k.dt[h // GROUP:h // GROUP + 1, h % GROUP * s:(h % GROUP + 1) * s] = dt[h:h + 1]
@@ -430,29 +442,52 @@
         k.ct[1] = k.sin[pl.ds(row0, s)].T[32:64] * 0.125
 
         def group(g, _):
-            kvh = k.kvg[:, pl.ds(pl.multiple_of(g * 128, 128), 128)]
-            heads = (pl.ds(g * GROUP, GROUP), pl.ds(row0, s))
-            qh, doh = k.q16[heads].reshape(GROUP * s, 128), k.do16[heads].reshape(GROUP * s, 128)
-            p = jnp.exp(dot_nt(kvh, qh) + k.bias[...] - k.lse[m, pl.ds(g, 1)])
-            ds = (p * (dot_nt(kvh, doh) - k.dt[pl.ds(g, 1)])).astype(BF)
-            total = dot(ds, qh) + dot(p.astype(BF), doh)
-            dqt = dot(k.kvt[g], ds)
-            c, sn = k.ct[0], k.ct[1]
-            for j in range(GROUP):
-                y1, y2 = dqt[0:32, j * s:j * s + s], dqt[32:64, j * s:j * s + s]
-                k.dqt[g * GROUP + j, 0:32] = (y1 * c + y2 * sn)
-                k.dqt[g * GROUP + j, 32:64] = (y2 * c - y1 * sn)
-            k.dkv[:, m, :, pl.ds(pl.multiple_of(g * 128, 128), 128)] = total.astype(BF).reshape(geo.n_blk, s, 128)
+            lane0 = pl.multiple_of(g * 128, 128)
+            kvh = k.kvg[:, pl.ds(lane0, 128)]
+            total = None
+            for j0 in range(0, GROUP, batch):
+                heads = (pl.ds(g * GROUP + j0, batch), pl.ds(row0, s))
+                cols = slice(j0 * s, (j0 + batch) * s)
+                qh, doh = k.q16[heads].reshape(batch * s, 128), k.do16[heads].reshape(batch * s, 128)
+                p = jnp.exp(dot_nt(kvh, qh) + k.bias[...] - k.lse[m, pl.ds(g, 1), cols])
+                ds = (p * (dot_nt(kvh, doh) - k.dt[pl.ds(g, 1), cols])).astype(BF)
+                part = dot(ds, qh) + dot(p.astype(BF), doh)
+                total = part if total is None else total + part
+                dqt = dot(k.kvt[g], ds)
+                c, sn = k.ct[0], k.ct[1]
+                for j in range(batch):
+                    y1, y2 = dqt[0:32, j * s:j * s + s], dqt[32:64, j * s:j * s + s]
+                    k.dqt[g * GROUP + j0 + j, 0:32] = (y1 * c + y2 * sn)
+                    k.dqt[g * GROUP + j0 + j, 32:64] = (y2 * c - y1 * sn)
+            total = total.astype(BF).reshape(geo.n_blk, s, 128)
+            if pause is None:
+                k.dkv[:, m, :, pl.ds(lane0, 128)] = total
+            else:
+                k.dkvm[:, :, pl.ds(lane0, 128)] = total
             return 0
-        lax.fori_loop(0, KV_HEADS, group, 0)
+        if pause is None:
+            lax.fori_loop(0, KV_HEADS, group, 0)
+        else:
+            lax.fori_loop(0, 3, group, 0)
+            pause()
+            lax.fori_loop(3, KV_HEADS, group, 0)
+            store = pltpu.make_async_copy(k.dkvm, k.dkv.at[:, m], k.lsem.at[0])
+            store.start()
         for t in range(8):
             if 2 * t + 1 < HEADS:
                 x = k.dqt[2 * t:2 * t + 2].reshape(128, s).T
             else:
                 x = jnp.concatenate([k.dqt[2 * t], jnp.zeros((64, s), F32)], axis=0).T
             k.da[pl.ds(row0, s), 128 * t:128 * t + 128] = x.astype(BF)
+        if pause is not None:
+            store.wait()
         return 0
-    lax.fori_loop(0, geo.ns, seq, 0)
+    if pause is None:
+        lax.fori_loop(0, geo.ns, seq, 0)
+    else:
+        for m in range(geo.ns):
+            seq(m, 0)
+            pause()
 
 
 def back_project(geo, r, k, blk):
@@ -523,10 +558,12 @@
     def turned_outs(r):
         return dict(da=Out((R[r], 1024), BF), dkv=Out((nb, nsq, S[r], 640), BF))
 
-    def turned_scratch(r):
-        return dict(kvg=V((KN[r], 640), BF), kvt=V((KV_HEADS, 128, KN[r]), BF), bias=V((KN[r], GROUP * S[r]), F32),
-                    dcol=V((R[r], 128), F32), dt=V((8, GROUP * S[r]), F32), ct=V((2, 32, S[r]), F32),
-                    do16=V((HEADS, R[r], 128), BF), dqt=V((HEADS, 64, S[r]), F32))
+    def out_parts(make, r=0):
+        return dict(do16=make((HEADS, R[r], 128), BF), dcol=make((R[r], 128), F32))
+
+    def turned_scratch(r, batch=GROUP):
+        return dict(kvg=V((KN[r], 640), BF), kvt=V((KV_HEADS, 128, KN[r]), BF), bias=V((KN[r], batch * S[r]), F32), dt=V((8, GROUP * S[r]), F32), ct=V((2, 32, S[r]), F32),
+                    dqt=V((HEADS, 64, S[r]), F32), **(out_parts(V, r) if r else {}))
 
     P, F, B, T, L = [None] * 3, [None] * 3, [None] * 3, [None] * 3, [None] * 3
     rt = [None] + list(routes)
@@ -635,6 +672,7 @@
         k.dh[...] = dot(k.cot[...], k.spread[0:d])
         v = join(v, k.bs, k.ts, k.b, k.t)
         back_feed(geo, 2, v, blk, tiles)
+        back_out(geo, 2, v)
         back_attend(geo, 2, v, blk)
 
     p = P[2]
@@ -656,29 +694,38 @@
         v.dh = k.dh2
         back_feed(geo, r, v, blk, tiles)
         if r > 0:
-            back_attend(geo, r, join(v, k.t, k.ts), blk)
+            v = join(v, k.t, k.ts)
+        back_out(geo, r, v)
+        if r > 0:
+            back_attend(geo, r, v, blk)
 
     for r in (1, 0):
         n, q, p, f = r + 1, P[r + 1], P[r], F[r]
         mine = give_back(T[n].dkv).reshape(R[n], 640)
         late = dict(q16=p.q16, kvall=p.kvall, cos=p.cos, sin=p.sin, choice=p.choice) if r else {}
-        more = dict(o=f.o, lse=f.lse) if r else {}
-        rest = dict(wou=wou, routes=rt[r]) if r else dict(lens=lens)
+        more = dict(lse=f.lse) if r else {}
+        rest = dict(wou=wou, routes=rt[r]) if r else dict(wou=wou, lens=lens)
         got = call("backward", functools.partial(k_back, r),
                    dict(wa=wa, gu=gu, wd=wd, dh=dh, **rest,
                         n=dict(dkvown=mine, da=T[n].da, tok=B[n].tok, inc=B[n].inc, choice=q.choice, st=q.st, a=q.a,
                                cos=q.cos, sin=q.sin),
                         p=dict(a=p.a, **late),
-                        f=dict(b=f.b, gp=Far(f.gp), up=Far(f.up), yf=f.yf, sx=f.sx, **more)),
+                        f=dict(o=f.o, b=f.b, gp=Far(f.gp), up=Far(f.up), yf=f.yf, sx=f.sx, **more)),
                    dict(b=feed_outs(r), da2=Out((R[n], COLS_A), BF), first=Out((8, dp)), dh2=Out((full, dp)),
-                        **(dict(t=turned_outs(r)) if r else {})),
+                        **(dict(t=turned_outs(r)) if r else out_parts(Out))),
                    dict(bs=feed_scratch(r), tl=Tiles.scratch(geo), **(dict(ts=turned_scratch(r)) if r else {})))
         dh, B[r], L[n] = got.dh2, join(got.b), join(da2=got.da2, first=got.first)
         if r:
             T[r] = join(got.t)
     p, f = P[0], F[0]
+    saved = [join(P[r], F[r], B[r], L[r] or {}) for r in range(3)]
+    if (geo.n_dp, geo.n_blk) == (G, 4):
+        gu_d = products(geo, saved, GU), products(geo, saved, DOWN)
+        grad, shards = tail(geo, join(p, f, B[0], got, wa=wa, dh=dh, lens=lens.value, spread=spread), saved, gu_d,
+                            turned_scratch(0, 1))
+        return out, grad, shards
     T[0] = call("backward_attend", lambda k: back_attend(geo, 0, k, blk_of()),
-                dict(wou=wou, dy=B[0].dy, q16=p.q16, kvall=p.kvall, o=f.o, lse=f.lse, cos=p.cos, sin=p.sin),
+                dict(do16=got.do16, dcol=got.dcol, q16=p.q16, kvall=p.kvall, lse=f.lse, cos=p.cos, sin=p.sin),
                 turned_outs(0), turned_scratch(0))
     mine = give_back(T[0].dkv).reshape(R[0], 640)
 
@@ -693,47 +740,178 @@
                 dict(wa=wa, dkvown=mine, da=T[0].da, tok=B[0].tok, dh=dh, lens=lens, st=p.st, a=p.a, cos=p.cos, sin=p.sin,
                      spread=spread),
                 dict(da2=Out((R[0], COLS_A), BF), first=Out((8, dp)), grad=Out((full, d))), dict(dh2=V((full, dp), F32)))
-    return out, L[0].grad, spread, [join(P[r], F[r], B[r], L[r]) for r in range(3)]
-
-
-def products(geo, lefts, rights, width, tile, rows, spread=None, extra=None):
+    saved[0] = join(saved[0], L[0])
+    slabs = [products(geo, saved, kind, spread) for kind in (QKV, OUT, GU, DOWN)]
+    shards = [lax.psum(lax.psum_scatter(v, "dp", scatter_dimension=0, tiled=True), "blk") for v in slabs]
+    return out, L[0].grad, shards
+
+
+QKV, OUT, GU, DOWN = range(4)
+
+
+def product_parts(geo, saved, kind, spread=None):
+    dp, ff = geo.dp, geo.ff
+    if kind == QKV:
+        ins = dict(lefts=[v.u for v in saved], rights=[[v.da2 for v in saved]], small=[v.small for v in saved],
+                   first=[v.first for v in saved])
+        return ins, (dp, COLS_A), 512
+    if kind == OUT:
+        return dict(lefts=[v.o for v in saved], rights=[[v.dy for v in saved]], spread=spread), (dp, dp), 512
+    if kind == GU:
+        return dict(lefts=[v.w for v in saved], rights=[[v.dgp for v in saved], [v.dup for v in saved]]), (dp, 2 * ff), 512
+    return dict(lefts=[v.z for v in saved], rights=[[v.df for v in saved]]), (ff, dp), 256
+
+
+def product_body(geo, kind, shape, tile, k):
     R = [geo.rows(r) for r in range(3)]
-    dp = geo.dp
+    rows, dp = shape[0], geo.dp
+    at = 0
+    for i in range(3):
+        for c in range(0, rows, 256):
+            v = dot(k.lefts[i][...], k.spread[:, c:c + 256]).astype(BF) if kind == OUT else k.lefts[i][:, c:c + 256]
+            k.left[c:c + 256, at:at + R[i]] = v.T
+        at += R[i]
+    c0 = 0
+    for refs in k.rights:
+        n = refs[0].shape[1]
+        for t in range(0, n, tile):
+            w = min(tile, n - t)
+            right = jnp.concatenate([v[:, t:t + w] for v in refs], axis=0)
+            k.res[:, c0 + t:c0 + t + w] = dot(k.left[...], right).astype(BF)
+        c0 += n
+    if kind == QKV:
+        small = k.small[0][...] + k.small[1][...] + k.small[2][...]
+        f = k.first[0][...] + k.first[1][...] + k.first[2][...]
+        small = jnp.where(rowid(small.shape) == 0, f, small)
+        cols = jnp.concatenate([small, jnp.zeros((120, dp), F32)], axis=0).T
+        cols = pltpu.roll(cols, 64, 1)
+        k.res[:, 896:1024] = jnp.where(lanes(cols.shape) < 64, k.res[:, 896:1024].astype(F32), cols).astype(BF)
+
+
+def products(geo, saved, kind, spread=None):
+    ins, shape, tile = product_parts(geo, saved, kind, spread)
+    total = sum(geo.rows(r) for r in range(3))
+    return call("weight_grads", functools.partial(product_body, geo, kind, shape, tile), ins, dict(res=Out(shape, BF)),
+                dict(left=pltpu.VMEM((shape[0], total), BF))).res
+
+
+def phase(body, ins, outs, scratch=None):
+    leaf = lambda v: not isinstance(v, (dict, list, tuple))
+    fi, ti = jax.tree.flatten(ins, is_leaf=leaf)
+    fo, to = jax.tree.flatten(outs, is_leaf=leaf)
+
+    def run(vi, vo, sc, sems):
+        loads = [pltpu.make_async_copy(far, near, sems.at[i]) for i, (far, near) in enumerate(zip(fi, vi))]
+        for v in loads:
+            v.start()
+        for v in loads:
+            v.wait()
+        body(join(ti.unflatten(vi), to.unflatten(vo), sc))
+        stores = [pltpu.make_async_copy(near, far, sems.at[i]) for i, (far, near) in enumerate(zip(fo, vo))]
+        for v in stores:
+            v.start()
+        for v in stores:
+            v.wait()
+    near = lambda refs: [pltpu.VMEM(v.shape, v.dtype) for v in refs]
+    pl.run_scoped(run, near(fi), near(fo), scratch or {}, pltpu.SemaphoreType.DMA((max(len(fi), len(fo)),)))
+
+
+def tail(geo, v, saved, gu_d, turned):
+    dp, d, bl, nsq, s = geo.dp, geo.d, geo.bl, geo.ns, geo.slots[0]
+    full = nsq * bl
+    V, dma = pltpu.VMEM, pltpu.SemaphoreType.DMA
+    total = sum(geo.rows(r) for r in range(3))
+    one = Geo(1, bl, geo.n_dp, geo.n_blk, d, geo.ff, geo.tops)
+    part = (nsq, s, 640)
 
     def body(k):
-        at = 0
-        for i in range(3):
-            for c in range(0, rows, 256):
-                v = k.lefts[i][:, c:c + 256] if spread is None else dot(k.lefts[i][...], k.spread[:, c:c + 256]).astype(BF)
-                k.left[c:c + 256, at:at + R[i]] = v.T
-            at += R[i]
-        c0 = 0
-        for refs in k.rights:
-            n = refs[0].shape[1]
-            for t in range(0, n, tile):
-                w = min(tile, n - t)
-                right = jnp.concatenate([v[:, t:t + w] for v in refs], axis=0)
-                k.res[:, c0 + t:c0 + t + w] = dot(k.left[...], right).astype(BF)
-            c0 += n
-        if extra is not None:
-            small = k.small[0][...] + k.small[1][...] + k.small[2][...]
-            f = k.first[0][...] + k.first[1][...] + k.first[2][...]
-            small = jnp.where(rowid(small.shape) == 0, f, small)
-            cols = jnp.concatenate([small, jnp.zeros((120, dp), F32)], axis=0).T
-            cols = pltpu.roll(cols, 64, 1)
-            k.res[:, 896:1024] = jnp.where(lanes(cols.shape) < 64, k.res[:, 896:1024].astype(F32), cols).astype(BF)
-    ins = dict(lefts=lefts, rights=rights, **(extra or {}), **({} if spread is None else dict(spread=spread)))
-    return call("weight_grads", body, ins, dict(res=Out((rows, width), BF)), dict(left=pltpu.VMEM((rows, sum(R)), BF))).res
-
-
-def weight_grads(geo, saved, spread):
-    dp, ff = geo.dp, geo.ff
-    a = products(geo, [v.u for v in saved], [[v.da2 for v in saved]], COLS_A, 512, dp,
-                 extra=dict(small=[v.small for v in saved], first=[v.first for v in saved]))
-    o = products(geo, [v.o for v in saved], [[v.dy for v in saved]], dp, 512, dp, spread=spread)
-    gu = products(geo, [v.w for v in saved], [[v.dgp for v in saved], [v.dup for v in saved]], 2 * ff, 512, dp)
-    d = products(geo, [v.z for v in saved], [[v.df for v in saved]], dp, 256, ff)
-    return a, o, gu, d
+        dp_, blk, y, c, ym, cm = mates()
+        z, x_ = dp_ // NX, lax.rem(dp_, NX)
+        meet((dp_ + 1 - 2 * x_, blk), ym, cm, z=z)
+        slabs = [k.ga, k.go, k.gu, k.gd]
+        ticks = reduce_ticks(RS_CHUNKS, [slab_view(geo, i, w) for i, w in enumerate(slabs)], k.shards, k.bufs, k.sems)
+        ready = RS_CHUNKS_READY
+
+        def tick(n=1):
+            nonlocal ready
+            for _ in range(n):
+                if ready > 0:
+                    ready -= 1
+                    ticks.pop(0)()
+        tick(2)
+        a = k.at
+        phase(lambda q: back_attend(geo, 0, join(q, kvall=k.kvall, dkv=k.dkv), blk, tick),
+              dict(do16=a.do16, dcol=a.dcol, q16=a.q16, lse=a.lse, cos=a.cos, sin=a.sin), dict(da=k.da),
+              dict(dkvm=V((geo.n_blk, s, 640), BF), lsem=dma((geo.n_blk,)), **turned))
+
+        def rem(src, dst, i, to):
+            return pltpu.make_async_remote_copy(src_ref=src, dst_ref=dst, send_sem=k.gs.at[i], recv_sem=k.gr.at[i],
+                                                device_id=to, device_id_type=MESH)
+        first = [rem(k.dkv.at[2 * yy + 1 - c], k.got1.at[yy], yy, cm) for yy in range(2)]
+        for f in first:
+            f.start()
+        tick()
+        for f in first:
+            f.wait_recv()
+
+        def add(q):
+            for yy, mine in enumerate((q.p0, q.p1)):
+                k.got1[yy] = (k.got1[yy].astype(F32) + mine[...].astype(F32)).astype(BF)
+        phase(add, dict(p0=k.dkv.at[c], p1=k.dkv.at[2 + c]), {})
+        second = rem(k.got1.at[1 - y], k.got2, 2, ym)
+        second.start()
+        tick()
+        second.wait_recv()
+        tick()
+        k.first[...] = jnp.zeros(k.first.shape, F32)
+        for m in range(nsq):
+            rows = pl.ds(m * bl, bl)
+
+            def last(q):
+                q.gn = gains(q.wa)
+                q.dkvown[...] = k.got1[y, m].astype(F32) + k.got2[m].astype(F32)
+                back_project(one, 0, join(q, lens=[k.lens[m]], first=k.first), blk)
+                high, low = halves(q.dh2[...])
+                q.grad[...] = dot_nt(high, q.spread[0:d]) + dot_nt(low, q.spread[0:d])
+            phase(last, dict(wa=k.wa, da=k.da.at[rows], tok=a.tok.at[rows], dh=a.dh.at[rows], st=a.st.at[rows], a=a.a.at[rows],
+                             cos=a.cos.at[rows], sin=a.sin.at[rows], spread=k.spread),
+                  dict(da2=k.da2.at[rows], grad=k.grad.at[rows]),
+                  dict(dkvown=V((bl, 640), F32), dh2=V((bl, dp), F32)))
+            tick()
+        for kind, res in ((QKV, k.ga), (OUT, k.go)):
+            ins, shape, tile = product_parts(geo, [types.SimpleNamespace(**q) for q in k.saved], kind, k.spread)
+            if kind == QKV:
+                ins[FIRST] = ins[FIRST][1:]
+                ins[RIGHTS] = [[k.da2] + ins[RIGHTS][0][1:]]
+
+            def make(q, kind=kind, shape=shape, tile=tile):
+                if kind == QKV:
+                    q.first = [k.first] + q.first
+                product_body(geo, kind, shape, tile, q)
+            phase(make, ins, dict(res=res), dict(left=V((shape[0], total), BF)))
+            tick()
+        for t in ticks:
+            t()
+        for f in first + [second]:
+            f.wait_send()
+
+    FIRST, RIGHTS = tuple(dict(first=0, rights=0))
+    keep = [dict(u=Far(q.u), o=Far(q.o), dy=Far(q.dy), small=Far(q.small),
+                 **(dict(da2=Far(q.da2), first=Far(q.first)) if i else dict(da2=Far(q.u), first=Far(q.small))))
+            for i, q in enumerate(saved)]
+    bufs, sems = reduce_scratch(geo, RS_CHUNKS)
+    got = call("tail", lambda k: body(join(k, at=join(k.at))),
+               dict(at=dict(do16=Far(v.do16), dcol=Far(v.dcol), q16=Far(v.q16), lse=Far(v.lse), cos=Far(v.cos), sin=Far(v.sin),
+                            tok=Far(v.tok), dh=Far(v.dh), st=Far(v.st), a=Far(v.a)),
+                    kvall=Far(v.kvall), lens=Words(v.lens), wa=Far(v.wa), spread=Far(v.spread), gu=Far(gu_d[0]), gd=Far(gu_d[1]),
+                    saved=keep),
+               dict(shards=reduce_outs(geo), grad=Out((full, d), F32, True), ga=Out((dp, COLS_A), BF, True),
+                    go=Out((dp, dp), BF, True), da=Out((full, 1024), BF, True), da2=Out((full, COLS_A), BF, True),
+                    dkv=Out((geo.n_blk,) + part, BF, True)),
+               dict(bufs=bufs, sems=sems, got1=V((2,) + part, BF), got2=V(part, BF), first=V((8, dp), F32),
+                    gs=dma((3,)), gr=dma((3,))),
+               collective_id=2, has_side_effects=True)
+    return got.grad, got.shards
 
 
 MESH = pl.DeviceIdType.MESH
@@ -952,18 +1130,15 @@
     lax.fori_loop(0, n, body, 0)
 
 
-def reduce_kernel(chunks, nslab, *refs):
+def reduce_ticks(chunks, ins, outs, bufs, sems):
     nch = len(chunks)
-    ins, outs = refs[:nslab], refs[nslab:2 * nslab]
-    bufs = refs[2 * nslab:]
-    own, crv, yrv, xrv, zrv, fin, s4b = (bufs[k * nch:(k + 1) * nch] for k in range(7))
-    ls, cs, cr, ys, yr, xs, xr, zs, zr, fs, fr = bufs[7 * nch:]
+    own, crv, yrv, xrv, zrv, fin, s4b = bufs
+    ls, cs, cr, ys, yr, xs, xr, zs, zr, fs, fr = sems
     dp, blk = lax.axis_index("dp"), lax.axis_index("blk")
     z, x = dp // NX, lax.rem(dp, NX)
     y, c = blk // 2, lax.rem(blk, 2)
     left, right = (dp - NX, blk), (dp + NX, blk)
     xm, ym, cm = (dp + 1 - 2 * x, blk), (dp, lax.rem(blk + 2, 4)), (dp, blk + 1 - 2 * c)
-    meet(xm, ym, cm, z=z)
 
     def rem(src, dst, a, b, to):
         return pltpu.make_async_remote_copy(src_ref=src, dst_ref=dst, send_sem=a, recv_sem=b, device_id=to, device_id_type=MESH)
@@ -1113,7 +1288,7 @@
         for k in ((1, 2) if four(i) else (1,)):
             fin_recv(i, k).wait_recv()
         for q in range(split):
-            outs[s][q, :, pl.ds(c0, n)] = fin[i][q].astype(jnp.float32)
+            outs[s][q, :, pl.ds(c0, n)] = fin[i][q]
 
     def sent(i):
         core_send(i).wait_send()
@@ -1127,56 +1302,63 @@
             fin_send(i, k).wait_send()
 
     stages = [st1, st2, st3] + [functools.partial(lambda i, s: zstep(i, s), s=s) for s in range(1, NZ - 1)] + [finish, st8, st9, sent]
-    for i in range(min(AHEAD, nch)):
-        st0(i)
-    for t in range(nch + max(OFFSETS)):
+    def tick(t):
+        if t < 0:
+            for i in range(min(AHEAD, nch)):
+                st0(i)
+            return
         if t + AHEAD < nch:
             st0(t + AHEAD)
         for s in reversed(range(len(stages))):
             i = t - OFFSETS[s]
             if 0 <= i < nch:
                 stages[s](i)
-
-
-def reduce(slabs, chunks):
-    n, nch = len(slabs), len(chunks)
+    return [functools.partial(tick, t) for t in range(-1, nch + max(OFFSETS))]
+
+
+def slab_split(k):
+    return next(ch[3] for ch in RS_CHUNKS if ch[0] == k)
+
+
+def slab_rows(geo, k):
+    return (geo.ff // geo.n_dp if k == 3 else geo.gp) // slab_split(k)
+
+
+def slab_view(geo, k, ref):
+    lead = (NZ, NX, 2, 2) if slab_split(k) == 4 else (NZ, NX, 2)
+    return ref.reshape(*lead, slab_rows(geo, k), ref.shape[1])
+
+
+def reduce_scratch(geo, chunks):
+    nch = len(chunks)
     dma = pltpu.SemaphoreType.DMA
-    bf = jnp.bfloat16
 
     def shapes(kind):
         out = []
         for s, c0, nc, split in chunks:
-            h = slabs[s].shape[-2]
+            h = slab_rows(geo, s)
             lead = (NZ, NX, 2) if split == 4 else (NZ, NX)
             tiny = (1, 16, 128)
-            shape = dict(own=lead + (h, nc), crv=lead + (h, nc), yrv=(NZ, NX, h, nc) if split == 4 else tiny,
-                         xrv=(NZ, h, nc), zrv=(2, NZ, h, nc), fin=(4 if split == 4 else 3, h, nc),
-                         s4b=(h, nc) if split == 2 else tiny)[kind]
-            out.append(pltpu.VMEM(shape, bf))
+            shape = (lead + (h, nc), lead + (h, nc), (NZ, NX, h, nc) if split == 4 else tiny, (NZ, h, nc), (2, NZ, h, nc),
+                     (4 if split == 4 else 3, h, nc), (h, nc) if split == 2 else tiny)[kind]
+            out.append(pltpu.VMEM(shape, jnp.bfloat16))
         return out
-    scratch = sum([shapes(k) for k in ("own", "crv", "yrv", "xrv", "zrv", "fin", "s4b")], [])
     sems = [dma((nch,)), dma((nch, 1)), dma((nch, 1)), dma((nch,)), dma((nch,)), dma((nch,)), dma((nch,)),
             dma((nch, 2)), dma((nch, 2)), dma((nch, 3)), dma((nch, 3))]
-    outs = []
-    for k, s in enumerate(slabs):
-        split = next(ch[3] for ch in chunks if ch[0] == k)
-        outs.append(jax.ShapeDtypeStruct((split,) + s.shape[-2:], jnp.float32))
-    return pl.pallas_call(
-        functools.partial(reduce_kernel, chunks, n),
-        out_shape=outs,
-        in_specs=[pl.BlockSpec(memory_space=pl.ANY)] * n,
-        out_specs=[pl.BlockSpec(memory_space=pltpu.VMEM)] * n,
-        scratch_shapes=scratch + sems,
-        compiler_params=pltpu.CompilerParams(collective_id=2, has_side_effects=True, vmem_limit_bytes=60 << 20),
-        name="reduce_grads",
-    )(*slabs)
+    return [shapes(k) for k in range(7)], sems
+
+
+def reduce_outs(geo):
+    cols = (COLS_A, geo.dp, 2 * geo.ff, geo.dp)
+    return [Out((slab_split(k), slab_rows(geo, k), cols[k]), BF) for k in range(4)]
 
 
 A_TICKS = 8
 AG_CHUNKS = [(0, 0, 1664, 4), (1, 0, 1024, 2), (2, 0, 2560, 4), (2, 2560, 2560, 4), (3, 0, 1024, 2)]
-RS_CHUNKS = [(2, 0, 640, 4), (3, 0, 256, 2), (2, 640, 640, 4), (3, 256, 256, 2), (2, 1280, 640, 4), (3, 512, 256, 2),
-             (2, 1920, 640, 4), (3, 768, 256, 2), (2, 2560, 640, 4), (0, 0, 512, 2), (2, 3200, 640, 4), (0, 512, 512, 2),
-             (2, 3840, 640, 4), (0, 1024, 640, 2), (2, 4480, 640, 4), (1, 0, 512, 2), (1, 512, 512, 2)]
+RS_CHUNKS = [(2, 0, 640, 4), (3, 0, 256, 2), (2, 640, 640, 4), (2, 1280, 640, 4), (3, 256, 256, 2), (2, 1920, 640, 4),
+             (2, 2560, 640, 4), (3, 512, 256, 2), (2, 3200, 640, 4), (2, 3840, 640, 4), (3, 768, 256, 2), (2, 4480, 640, 4),
+             (0, 0, 896, 4), (1, 0, 512, 2), (0, 896, 768, 4), (1, 512, 512, 2)]
+RS_CHUNKS_READY = 12 - AHEAD + 1
 
 
 def pad_to(v, shape):
@@ -1201,23 +1383,12 @@
     return a, pad_to(pad_cols(o, geo), (geo.gp, geo.dp)), gu, pad_cols(d, geo)
 
 
-def summed_grads(geo, slabs):
-    a, o, gu, d = slabs
-    if (geo.n_dp, geo.n_blk) != (G, 4):
-        shares = [lax.psum_scatter(v, "dp", scatter_dimension=0, tiled=True) for v in slabs]
-        return tuple(lax.psum(v, "blk").astype(F32) for v in shares)
-    gp, rd = geo.gp, d.shape[0] // G
-    got = reduce([a.reshape(NZ, NX, 2, gp // 2, -1), o.reshape(NZ, NX, 2, gp // 2, -1), gu.reshape(NZ, NX, 2, 2, gp // 4, -1),
-                  d.reshape(NZ, NX, 2, rd // 2, -1)], RS_CHUNKS)
-    return tuple(w.reshape(-1, w.shape[-1]) for w in got)
-
-
 def unpack(geo, slabs):
-    a, o, gu, d = slabs
+    a, o, gu, d = (w.reshape(-1, w.shape[-1]) for w in slabs)
     a, o, gu = a[:geo.gw], o[:geo.gw], gu[:geo.gw]
     kv = a[:, 1024:].reshape(geo.gw, KV_HEADS, 128)
-    return (a[:, :960], kv[:, :, :64].reshape(geo.gw, 320), kv[:, :, 64:].reshape(geo.gw, 320), unpad_cols(o, geo),
-            gu[:, :geo.ff], gu[:, geo.ff:], unpad_cols(d, geo), a[:, 960], a[:, 961], a[:, 962:965])
+    return tuple(w.astype(F32) for w in (a[:, :960], kv[:, :, :64].reshape(geo.gw, 320), kv[:, :, 64:].reshape(geo.gw, 320), unpad_cols(o, geo),
+            gu[:, :geo.ff], gu[:, geo.ff:], unpad_cols(d, geo), a[:, 960], a[:, 961], a[:, 962:965]))
 
 
 def mates():
@@ -1323,11 +1494,10 @@
     slabs = pack(geo, query_weight, key_weight, value_weight, output_weight, gate_weight, up_weight, down_weight, first_gain,
                  second_gain, router_weight)
     ids = iter(range(10, 30))
-    out, grad, spread, saved = block(geo, block_input.reshape(count * bl, d), cotangent.reshape(count * bl, d), seq_lengths.reshape(count),
+    out, grad, shards = block(geo, block_input.reshape(count * bl, d), cotangent.reshape(count * bl, d), seq_lengths.reshape(count),
                 (routes_two.reshape(count, -1), routes_three.reshape(count, -1)), slabs,
                 lambda kv: share_rows(geo, next(ids), kv), lambda dkv: give_rows(geo, next(ids), dkv))
-    grads = unpack(geo, summed_grads(geo, weight_grads(geo, saved, spread)))
-    return (out.reshape(block_input.shape), grad.reshape(block_input.shape)) + tuple(grads)
+    return (out.reshape(block_input.shape), grad.reshape(block_input.shape)) + unpack(geo, shards)
 
 
 def solution(mesh):

time: 588 us -> 546 us (0.929)
  Pallas kernels: 544 us -> 507 us
  local copies, waits for them, and re-layouts: 32.1 us -> 21.8 us
    pallas_call x1 -> x0, Pallas kernels: 126 us -> none  [reduce(): pl.pallas_call(functools.partial(reduce_kernel, chunks, n), out_shape=out...]
    pallas_call x12 -> x9, Pallas kernels: 354 us -> 464 us  [call(): pl.pallas_call(kernel, out_shape=[jax.ShapeDtypeStruct(o.shape, o.dtype)...]
    pallas_call x3 -> x2, Pallas kernels: 40.3 us -> 20.3 us  [give_rows(): pl.pallas_call(give_kernel, out_shape=jax.ShapeDtypeStruct(piece, F32), i...]
where the time goes in v4:
time: 546 us; the launch traced here: 538 us
  Pallas kernels  507 us (93%)
  local copies, waits for them, and re-layouts  21.8 us (4%)
  other arithmetic  8.21 us (2%)
    pallas_call x9, Pallas kernels, call(): pl.pallas_call(kernel, out_shape=[jax.ShapeDtypeStruct(o.shape, o.dtype)...  464 us
    pallas_call x2, Pallas kernels, share_rows(): pl.pallas_call(share_kernel, out_shape=jax.ShapeDtypeStruct((4,) + kv.sha...  23.1 us
    pallas_call x2, Pallas kernels, give_rows(): pl.pallas_call(give_kernel, out_shape=jax.ShapeDtypeStruct(piece, F32), i...  20.3 us
    unnamed x39, local copies, waits for them, and re-layouts  13.3 us

profile of v4, /device:TPU:0, one launch (start us, length us, event | category | flops | bytes accessed | tf_op | source)
XLA Modules:
  0.0 538.4 jit_solution(5461967770900512145)
XLA Ops:
  0.7 1.3 copy.71
  2.8 1.0 pad_maximum_fusion
  4.0 1.1 concatenate.14
  5.1 0.8 pad.25.refs_1_
  6.3 0.7 pad.27.refs_2_
  7.0 1.7 constant_dynamic-slice_fusion
  8.7 0.8 reshape.121
  9.6 1.0 copy.69
  10.6 1.3 copy.55
  11.9 1.3 copy.52
  13.2 1.2 fusion.2.refs_3_
  14.4 123.2 %head.1 = (f32[2,8,768]{2,1,0:T(8,128)}, bf16[512,1024]{1,0:T(8,128)(2,1)}, bf16[4,2,256,640]{3,2,1,0:T(8,128)(2,1)}, bf16[512,1024]{1,0:T(8,128)(2,1)}, f32[512...) custom-call(f32[256,128]{1,0:T(8,128)} %get-tuple-element.235.refs_0, ...), custom_call_target="tpu_custom_call" | custom-call | tf_op jit(solution)/shard_map/head/pallas_call | solution.py:97
  137.6 22.0 %forward.2 = (bf16[512,1024]{1,0:T(8,128)(2,1)}, bf16[512,2560]{1,0:T(8,128)(2,1)}, f32[512,128]{1,0:T(8,128)}, bf16[512,2560]{1,0:T(8,128)(2,1)}, bf16[512,1024...) custom-call(f32[256,128]{1,0:T(8,128)} %get-tuple-element.235.refs_0, ...), custom_call_target="tpu_custom_call" | custom-call | tf_op jit(solution)/shard_map/forward/pallas_call | solution.py:97
  159.6 14.3 %share_rows.2.refs_3_.refs_21_ = bf16[4,2,128,640]{3,2,1,0:T(8,128)(2,1)} custom-call(bf16[2,128,640]{2,1,0:T(8,128)(2,1)} %bitcast.66), custom_call_target="tpu_custom_call" | custom-call | tf_op jit(solution)/shard_map/share_rows/pallas_call | solution.py:1446
  173.9 24.5 %forward.3 = (bf16[256,1024]{1,0:T(8,128)(2,1)}, bf16[256,2560]{1,0:T(8,128)(2,1)}, f32[2,8,384]{2,1,0:T(8,128)}, bf16[256,1024]{1,0:T(8,128)(2,1)}, f32[256,128...) custom-call(f32[256,128]{1,0:T(8,128)} %get-tuple-element.235.refs_0, ...), custom_call_target="tpu_custom_call" | custom-call | tf_op jit(solution)/shard_map/forward/pallas_call | solution.py:97
  198.3 8.8 %share_rows.3.refs_6_ = bf16[4,2,64,640]{3,2,1,0:T(8,128)(2,1)} custom-call(bf16[2,64,640]{2,1,0:T(8,128)(2,1)} %bitcast.68), custom_call_target="tpu_custom_call" | custom-call | tf_op jit(solution)/shard_map/share_rows/pallas_call | solution.py:1446
  207.2 39.3 %turn.1 = (bf16[128,1024]{1,0:T(8,128)(2,1)}, bf16[128,2560]{1,0:T(8,128)(2,1)}, bf16[128,2560]{1,0:T(8,128)(2,1)}, bf16[128,1024]{1,0:T(8,128)(2,1)}, f32[128,1...) custom-call(bf16[512,960]{1,0:T(8,128)(2,1)} %bitcast.48, ...), custom_call_target="tpu_custom_call" | custom-call | tf_op jit(solution)/shard_map/turn/pallas_call | solution.py:97
  246.4 2.3 copy.58
  248.8 8.1 %give_rows.2 = f32[2,64,640]{2,1,0:T(8,128)S(1)} custom-call(bf16[2,2,2,64,640]{4,3,2,1,0:T(8,128)(2,1)S(1)} %bitcast.47), custom_call_target="tpu_custom_call" | custom-call | tf_op jit(solution)/shard_map/give_rows/pallas_call | solution.py:1481
  257.6 31.6 %backward.2 = (bf16[256,1024]{1,0:T(8,128)(2,1)}, bf16[256,2560]{1,0:T(8,128)(2,1)}, bf16[256,2560]{1,0:T(8,128)(2,1)}, bf16[256,1024]{1,0:T(8,128)(2,1)}, f32[2...) custom-call(f32[512,1024]{1,0:T(8,128)} %get-tuple-element.123.refs_, ...), custom_call_target="tpu_custom_call" | custom-call | tf_op jit(solution)/shard_map/backward/pallas_call | solution.py:97
  289.2 1.3 copy-done.2
  290.5 12.2 %give_rows.3 = f32[2,128,640]{2,1,0:T(8,128)S(1)} custom-call(bf16[2,2,2,128,640]{4,3,2,1,0:T(8,128)(2,1)S(1)} %bitcast.46), custom_call_target="tpu_custom_call" | custom-call | tf_op jit(solution)/shard_map/give_rows/pallas_call | solution.py:1481
  302.7 0.8 copy-done
  303.6 27.3 %backward.3 = (bf16[512,1024]{1,0:T(8,128)(2,1)}, bf16[512,2560]{1,0:T(8,128)(2,1)}, bf16[512,2560]{1,0:T(8,128)(2,1)}, bf16[512,1024]{1,0:T(8,128)(2,1)}, f32[8...) custom-call(f32[512,1024]{1,0:T(8,128)} %get-tuple-element.138.refs_, ...), custom_call_target="tpu_custom_call" | custom-call | tf_op jit(solution)/shard_map/backward/pallas_call | solution.py:97
  330.9 10.8 %weight_grads.2.refs_10_ = bf16[2560,1024]{1,0:T(8,128)(2,1)} custom-call(bf16[512,2560]{1,0:T(8,128)(2,1)} %get-tuple-element.157.refs_0_, bf16[256,2560]{1,0:T(8,128)(2,1)} %get-tuple-element.158.refs_1_, bf16[128,2560]{1,0:T(8,128)(2,1)} %get-tuple-element.159.refs_2_, bf16[512,1024]{1,0:T(8,128)(2,1)} %get-tuple-element.160.refs_3_, ...), custom_call_target="tpu_custom_call" | custom-call | tf_op jit(solution)/shard_map/weight_grads/pallas_call | solution.py:97
  341.7 19.3 %weight_grads.3.refs_11_ = bf16[1024,5120]{1,0:T(8,128)(2,1)} custom-call(bf16[512,1024]{1,0:T(8,128)(2,1)} %get-tuple-element.163.refs_0_, bf16[256,1024]{1,0:T(8,128)(2,1)} %get-tuple-element.164.refs_1_, bf16[128,1024]{1,0:T(8,128)(2,1)} %get-tuple-element.165.refs_2_, bf16[512,2560]{1,0:T(8,128)(2,1)} %get-tuple-element.166.refs_3_, ...), custom_call_target="tpu_custom_call" | custom-call | tf_op jit(solution)/shard_map/weight_grads/pallas_call | solution.py:97
  361.0 165.7 %tail.1 = (bf16[512,1024]{1,0:T(8,128)(2,1)}, bf16[512,1664]{1,0:T(8,128)(2,1)}, bf16[4,2,256,640]{3,2,1,0:T(8,128)(2,1)}, bf16[1024,1664]{1,0:T(8,128)(2,1)}, b...) custom-call(bf16[512,1024]{1,0:T(8,128)(2,1)} %get-tuple-element.103, ...), custom_call_target="tpu_custom_call" | custom-call | tf_op jit(solution)/shard_map/tail/pallas_call | solution.py:97
  526.7 2.9 copy.59
  531.3 0.8 slice_convert_fusion.4
  533.6 1.0 reshape.142
  534.8 1.4 reshape.143
  536.2 1.7 slice_convert_fusion.1
  (48 shorter events, 5.6 us)
Async XLA Ops:
  0.6 5.2 copy-start.12
  3.9 4.7 copy-start.7
  8.7 1.9 copy-start.5
  9.5 2.4 copy-start.6
  10.6 2.6 copy-start.9
  10.6 2.6 copy-start.10
  246.4 2.3 copy-start.3
  256.9 0.7 copy-start.1
  289.2 1.3 copy-start.2
  302.7 0.8 copy-start
  526.7 2.9 copy-start.11
  529.6 3.9 copy-start.13
  531.3 3.3 copy-start.8
  534.7 1.5 copy-start.4

commit v5 on v4

--- a/solution.py
+++ b/solution.py
@@ -338,8 +338,7 @@
 
 def back_feed(geo, r, k, blk, tiles):
     s, bl, rows = geo.slots[r], geo.bl, geo.rows(r)
-    k.small[2 + r:3 + r] = jnp.zeros((1, geo.dp), F32)
-    k.small[1:2] = jnp.zeros((1, geo.dp), F32)
+    k.small[...] = jnp.zeros(k.small.shape, F32)
 
     def incoming(m):
         here = slice(m * s, m * s + s)
@@ -556,7 +555,9 @@
         return dict(acc=V((R[r], dp), F32), pre=V((2, 2, R[r], FT), BF), wide=V((2, 3, R[r], FT), BF), wsem=dma((2, 3)))
 
     def turned_outs(r):
-        return dict(da=Out((R[r], 1024), BF), dkv=Out((nb, nsq, S[r], 640), BF))
+        piece = (nsq, S[r], 640)
+        last = dict(dkvown=Out(piece)) if near and r else dict(dkv=Out((nb,) + piece, BF))
+        return dict(da=Out((R[r], 1024), BF), **last)
 
     def out_parts(make, r=0):
         return dict(do16=make((HEADS, R[r], 128), BF), dcol=make((R[r], 128), F32))
@@ -564,6 +565,16 @@
     def turned_scratch(r, batch=GROUP):
         return dict(kvg=V((KN[r], 640), BF), kvt=V((KV_HEADS, 128, KN[r]), BF), bias=V((KN[r], batch * S[r]), F32), dt=V((8, GROUP * S[r]), F32), ct=V((2, 32, S[r]), F32),
                     dqt=V((HEADS, 64, S[r]), F32), **(out_parts(V, r) if r else {}))
+
+    near = (geo.n_dp, geo.n_blk) == (G, 4)
+
+    def share_scratch(r):
+        return dict(kv=V((R[r], 640), BF), own=V((nsq, S[r], 640), BF), ssem=dma((3,)), rsem=dma((3,)))
+
+    def give_scratch(r):
+        piece = (nsq, S[r], 640)
+        return dict(dkv=V((nb,) + piece, BF), got1=V((2,) + piece, BF), half=V(piece, BF), got2=V(piece, BF), ssem=dma((3,)),
+                    rsem=dma((3,)))
 
     P, F, B, T, L = [None] * 3, [None] * 3, [None] * 3, [None] * 3, [None] * 3
     rt = [None] + list(routes)
@@ -576,7 +587,7 @@
 
     ins = dict(x=x, spread=spread, cosb=cosb, sinb=sinb)
     afters = seen_outs(0)
-    if (geo.n_dp, geo.n_blk) != (G, 4):
+    if not near:
         wa, wo, gu, wd = (lax.all_gather(w, "dp", axis=0, tiled=True) for w in slabs)
 
         def k_first(k):
@@ -630,8 +641,13 @@
     gu, wd = Far(gu), Far(wd)
     wou = h = None
 
+    def remote(ident):
+        return dict(collective_id=ident, has_side_effects=True) if near else {}
+
     def k_fore(r, k):
         blk = blk_of()
+        if near:
+            meet(*mates()[4:])
         k = join(k, k.s, k.tl)
         tiles = Tiles(geo, k)
         tiles.start(0, 0)
@@ -644,21 +660,36 @@
         feed(geo, r, v, blk, tiles)
         n = join(k, k.n, h=k.h2, routes=k.routes2)
         select_rows(geo, r + 1, n, blk)
-        project(geo, r + 1, n)
+        if not near:
+            project(geo, r + 1, n)
+            return
+        n = join(n, k.sh, k.sh_)
+        project_kv(geo, r + 1, n)
+        n.own[...] = n.kv[...].reshape(n.own.shape)
+        n.kvall[blk] = n.own[...]
+        sharing = Share(n.own, n.kvall, n.ssem, n.rsem)
+        sharing.start()
+        project_q(geo, r + 1, n)
+        sharing.forward()
+        sharing.arrive()
+        sharing.sent()
 
     for r in range(2):
         p = dict(a=P[r].a, q16=P[r].q16, kvall=P[r].kvall) if r else dict(a=P[0].a, o=F[0].o)
         more = dict(choice=P[r].choice, h=h, routes=rt[r], wou=wou) if r else dict(wo=wo, spread=spread, lens=lens)
         got = call("forward", functools.partial(k_fore, r),
                    dict(wa=wa, gu=gu, wd=wd, p=p, cosb=cosb, sinb=sinb, routes2=rt[r + 1], s=more),
-                   dict(f=fore_outs(r), n=proj_outs(r + 1), h2=Out((full, dp)), **({} if r else dict(wou=Out((1024, dp), BF)))),
-                   dict(fs=fore_scratch(r), tl=Tiles.scratch(geo)))
+                   dict(f=fore_outs(r), n=proj_outs(r + 1, not near), h2=Out((full, dp)), **({} if r else dict(wou=Out((1024, dp), BF))),
+                        **(dict(sh=dict(kvall=Out((nb, nsq, S[r + 1], 640), BF))) if near else {})),
+                   dict(fs=fore_scratch(r), tl=Tiles.scratch(geo), **(dict(sh_=share_scratch(r + 1)) if near else {})), **remote(3 + r))
         h, F[r], P[r + 1] = got.h2, join(F[r] or {}, got.f), join(got.n)
         wou = wou if r else got.wou
-        P[r + 1].kvall = share(P[r + 1].kv.reshape(nsq, S[r + 1], 640))
+        P[r + 1].kvall = join(got.sh).kvall if near else share(P[r + 1].kv.reshape(nsq, S[r + 1], 640))
 
     def k_turn(k):
         blk = blk_of()
+        if near:
+            meet(*mates()[4:])
         k = join(k, k.tl)
         tiles = Tiles(geo, k)
         tiles.start(0, 0)
@@ -670,21 +701,26 @@
         tiles.start(0, 0)
         k.out[...] = dot_nt(k.h3[...].astype(BF), k.spread[0:d]).astype(BF)
         k.dh[...] = dot(k.cot[...], k.spread[0:d])
-        v = join(v, k.bs, k.ts, k.b, k.t)
+        v = join(v, k.bs, k.ts, k.b, k.t, k.gv if near else {})
         back_feed(geo, 2, v, blk, tiles)
         back_out(geo, 2, v)
         back_attend(geo, 2, v, blk)
+        if near:
+            give(v.dkv, v.dkvown, v.got1, v.half, v.got2, v.ssem, v.rsem)
 
     p = P[2]
     got = call("turn", k_turn,
                dict(wa=wa, gu=gu, wd=wd, wou=wou, h=h, spread=spread, cot=cot, routes=rt[2],
                     p=dict(a=p.a, q16=p.q16, kvall=p.kvall, choice=p.choice, cos=p.cos, sin=p.sin)),
                dict(f=fore_outs(2), b=feed_outs(2), t=turned_outs(2), out=Out((full, d), BF), dh=Out((full, dp))),
-               dict(fs=fore_scratch(2), bs=feed_scratch(2), ts=turned_scratch(2), tl=Tiles.scratch(geo), h3=V((full, dp), F32)))
+               dict(fs=fore_scratch(2), bs=feed_scratch(2), ts=turned_scratch(2), tl=Tiles.scratch(geo), h3=V((full, dp), F32),
+                    **(dict(gv=give_scratch(2)) if near else {})), **remote(5))
     F[2], B[2], T[2], out, dh = join(got.f), join(got.b), join(got.t), got.out, got.dh
 
     def k_back(r, k):
         blk = blk_of()
+        if near and r:
+            meet(*mates()[4:])
         v = join(k, k.p, k.f, k.b, k.bs, k.tl)
         tiles = Tiles(geo, v, (v.gp, v.up))
         tiles.start(0, 0)
@@ -694,14 +730,16 @@
         v.dh = k.dh2
         back_feed(geo, r, v, blk, tiles)
         if r > 0:
-            v = join(v, k.t, k.ts)
+            v = join(v, k.t, k.ts, k.gv if near else {})
         back_out(geo, r, v)
         if r > 0:
             back_attend(geo, r, v, blk)
+            if near:
+                give(v.dkv, v.dkvown, v.got1, v.half, v.got2, v.ssem, v.rsem)
 
     for r in (1, 0):
         n, q, p, f = r + 1, P[r + 1], P[r], F[r]
-        mine = give_back(T[n].dkv).reshape(R[n], 640)
+        mine = (T[n].dkvown if near else give_back(T[n].dkv)).reshape(R[n], 640)
         late = dict(q16=p.q16, kvall=p.kvall, cos=p.cos, sin=p.sin, choice=p.choice) if r else {}
         more = dict(lse=f.lse) if r else {}
         rest = dict(wou=wou, routes=rt[r]) if r else dict(wou=wou, lens=lens)
@@ -713,14 +751,15 @@
                         f=dict(o=f.o, b=f.b, gp=Far(f.gp), up=Far(f.up), yf=f.yf, sx=f.sx, **more)),
                    dict(b=feed_outs(r), da2=Out((R[n], COLS_A), BF), first=Out((8, dp)), dh2=Out((full, dp)),
                         **(dict(t=turned_outs(r)) if r else out_parts(Out))),
-                   dict(bs=feed_scratch(r), tl=Tiles.scratch(geo), **(dict(ts=turned_scratch(r)) if r else {})))
+                   dict(bs=feed_scratch(r), tl=Tiles.scratch(geo), **(dict(ts=turned_scratch(r)) if r else {}),
+                        **(dict(gv=give_scratch(r)) if r and near else {})), **(remote(6) if r else {}))
         dh, B[r], L[n] = got.dh2, join(got.b), join(da2=got.da2, first=got.first)
         if r:
             T[r] = join(got.t)
     p, f = P[0], F[0]
     saved = [join(P[r], F[r], B[r], L[r] or {}) for r in range(3)]
-    if (geo.n_dp, geo.n_blk) == (G, 4):
-        gu_d = products(geo, saved, GU), products(geo, saved, DOWN)
+    if near:
+        gu_d = gate_up_grads(geo, saved), down_grads(geo, saved)
         grad, shards = tail(geo, join(p, f, B[0], got, wa=wa, dh=dh, lens=lens.value, spread=spread), saved, gu_d,
                             turned_scratch(0, 1))
         return out, grad, shards
@@ -741,25 +780,21 @@
                      spread=spread),
                 dict(da2=Out((R[0], COLS_A), BF), first=Out((8, dp)), grad=Out((full, d))), dict(dh2=V((full, dp), F32)))
     saved[0] = join(saved[0], L[0])
-    slabs = [products(geo, saved, kind, spread) for kind in (QKV, OUT, GU, DOWN)]
+    slabs = [products(geo, saved, QKV), products(geo, saved, OUT, spread), gate_up_grads(geo, saved), down_grads(geo, saved)]
     shards = [lax.psum(lax.psum_scatter(v, "dp", scatter_dimension=0, tiled=True), "blk") for v in slabs]
     return out, L[0].grad, shards
 
 
-QKV, OUT, GU, DOWN = range(4)
+QKV, OUT = range(2)
 
 
 def product_parts(geo, saved, kind, spread=None):
-    dp, ff = geo.dp, geo.ff
+    dp = geo.dp
     if kind == QKV:
         ins = dict(lefts=[v.u for v in saved], rights=[[v.da2 for v in saved]], small=[v.small for v in saved],
                    first=[v.first for v in saved])
         return ins, (dp, COLS_A), 512
-    if kind == OUT:
-        return dict(lefts=[v.o for v in saved], rights=[[v.dy for v in saved]], spread=spread), (dp, dp), 512
-    if kind == GU:
-        return dict(lefts=[v.w for v in saved], rights=[[v.dgp for v in saved], [v.dup for v in saved]]), (dp, 2 * ff), 512
-    return dict(lefts=[v.z for v in saved], rights=[[v.df for v in saved]]), (ff, dp), 256
+    return dict(lefts=[v.o for v in saved], rights=[[v.dy for v in saved]], spread=spread), (dp, dp), 512
 
 
 def product_body(geo, kind, shape, tile, k):
@@ -795,6 +830,52 @@
                 dict(left=pltpu.VMEM((shape[0], total), BF))).res
 
 
+def gate_up_grads(geo, saved):
+    R = [geo.rows(r) for r in range(3)]
+    total, dp, n = sum(R), geo.dp, geo.ff // FT
+
+    def body(w0, w1, w2, g0, g1, g2, u0, u1, u2, out, left):
+        t = pl.program_id(0)
+
+        @pl.when(t == 0)
+        def _():
+            at = 0
+            for i, w in enumerate((w0, w1, w2)):
+                for c in range(0, dp, 256):
+                    left[c:c + 256, at:at + R[i]] = w[:, c:c + 256].T
+                at += R[i]
+
+        def put(parts):
+            out[...] = dot(left[...], jnp.concatenate([v[...] for v in parts], axis=0)).astype(BF)
+        pl.when(t < n)(lambda: put((g0, g1, g2)))
+        pl.when(t >= n)(lambda: put((u0, u1, u2)))
+    held = [pl.BlockSpec((rows, dp), lambda t: (0, 0)) for rows in R]
+    gate = [pl.BlockSpec((rows, FT), lambda t: (0, jnp.minimum(t, n - 1))) for rows in R]
+    up = [pl.BlockSpec((rows, FT), lambda t: (0, jnp.maximum(t - n, 0))) for rows in R]
+    return pl.pallas_call(
+        body, grid=(2 * n,), out_shape=jax.ShapeDtypeStruct((dp, 2 * geo.ff), BF), in_specs=held + gate + up,
+        out_specs=pl.BlockSpec((dp, FT), lambda t: (0, t)), scratch_shapes=[pltpu.VMEM((dp, total), BF)],
+        compiler_params=pltpu.CompilerParams(vmem_limit_bytes=63 << 20), name="gate_up_grads",
+    )(*[v.w for v in saved], *[v.dgp for v in saved], *[v.dup for v in saved])
+
+
+def down_grads(geo, saved, tile=512):
+    R = [geo.rows(r) for r in range(3)]
+    dp = geo.dp
+
+    def body(z0, z1, z2, d0, d1, d2, out):
+        left = jnp.concatenate([v[...] for v in (z0, z1, z2)], axis=0)
+        right = jnp.concatenate([v[...] for v in (d0, d1, d2)], axis=0)
+        out[...] = dot_tn(left, right).astype(BF)
+    return pl.pallas_call(
+        body, grid=(geo.ff // tile,), out_shape=jax.ShapeDtypeStruct((geo.ff, dp), BF),
+        in_specs=[pl.BlockSpec((rows, tile), lambda t: (0, t)) for rows in R]
+        + [pl.BlockSpec((rows, dp), lambda t: (0, 0)) for rows in R],
+        out_specs=pl.BlockSpec((tile, dp), lambda t: (t, 0)),
+        compiler_params=pltpu.CompilerParams(vmem_limit_bytes=63 << 20), name="down_grads",
+    )(*[v.z for v in saved], *[v.df for v in saved])
+
+
 def phase(body, ins, outs, scratch=None):
     leaf = lambda v: not isinstance(v, (dict, list, tuple))
     fi, ti = jax.tree.flatten(ins, is_leaf=leaf)
@@ -1107,14 +1188,14 @@
     def tick(t):
         if t == 6:
             locs[0].wait()
-        if t == nch + len(stages) - 2:
+        for s in reversed(range(len(stages))):
+            for i in range(nch):
+                if AG_STARTS[i] + s == t:
+                    stages[s](i)
+        if t == AG_STARTS[-1] + len(stages) - 1:
             for l in locs[1:]:
                 l.wait()
-        for s in reversed(range(len(stages))):
-            i = t - s
-            if 0 <= i < nch:
-                stages[s](i)
-    return [first] + [functools.partial(tick, t) for t in range(nch + len(stages) - 1)]
+    return [first] + [functools.partial(tick, t) for t in range(AG_STARTS[-1] + len(stages))]
 
 
 def gather_sems(n, nch):
@@ -1354,6 +1435,7 @@
 
 
 A_TICKS = 8
+AG_STARTS = (0, 1, 2, 3, 4)
 AG_CHUNKS = [(0, 0, 1664, 4), (1, 0, 1024, 2), (2, 0, 2560, 4), (2, 2560, 2560, 4), (3, 0, 1024, 2)]
 RS_CHUNKS = [(2, 0, 640, 4), (3, 0, 256, 2), (2, 640, 640, 4), (2, 1280, 640, 4), (3, 256, 256, 2), (2, 1920, 640, 4),
              (2, 2560, 640, 4), (3, 512, 256, 2), (2, 3200, 640, 4), (2, 3840, 640, 4), (3, 768, 256, 2), (2, 4480, 640, 4),
@@ -1426,63 +1508,25 @@
             v.wait_send()
 
 
-def share_kernel(own, out, lsem, ssem, rsem):
+def give(dkv, out, got1, half, got2, ssem, rsem):
     dp, blk, y, c, ym, cm = mates()
-    meet(ym, cm)
-    s = Share(own, out, ssem, rsem)
-    s.start()
-    local = pltpu.make_async_copy(own, out.at[blk], lsem)
-    local.start()
-    s.forward()
-    s.arrive()
-    s.sent()
-    local.wait()
-
-
-def share_rows(geo, ident, kv):
-    if geo.n_blk != 4:
-        return lax.all_gather(kv, "blk", axis=0, tiled=False)
-    dma = pltpu.SemaphoreType.DMA
-    return pl.pallas_call(
-        share_kernel, out_shape=jax.ShapeDtypeStruct((4,) + kv.shape, kv.dtype),
-        in_specs=[pl.BlockSpec(memory_space=pltpu.VMEM)], out_specs=pl.BlockSpec(memory_space=pl.ANY),
-        scratch_shapes=[dma, dma((3,)), dma((3,))],
-        compiler_params=pltpu.CompilerParams(collective_id=ident, has_side_effects=True), name="share_rows")(kv)
-
-
-def give_kernel(dkv, out, got1, half, got2, ssem, rsem):
-    dp, blk, y, c, ym, cm = mates()
-    meet(ym, cm)
 
     def rem(src, dst, k, to):
         return pltpu.make_async_remote_copy(src_ref=src, dst_ref=dst, send_sem=ssem.at[k], recv_sem=rsem.at[k],
                                             device_id=to, device_id_type=MESH)
-    first = [rem(dkv.at[yy, 1 - c], got1.at[yy], yy, cm) for yy in range(2)]
+    first = [rem(dkv.at[2 * yy + 1 - c], got1.at[yy], yy, cm) for yy in range(2)]
     for f in first:
         f.start()
     for f in first:
         f.wait_recv()
-    half[...] = (got1[1 - y].astype(F32) + dkv[1 - y, c].astype(F32)).astype(BF)
+    half[...] = (got1[1 - y].astype(F32) + dkv[2 * (1 - y) + c].astype(F32)).astype(BF)
     second = rem(half, got2, 2, ym)
     second.start()
-    mine = got1[y].astype(F32) + dkv[y, c].astype(F32)
+    mine = got1[y].astype(F32) + dkv[2 * y + c].astype(F32)
     second.wait_recv()
     out[...] = mine + got2[...].astype(F32)
     for f in first + [second]:
         f.wait_send()
-
-
-def give_rows(geo, ident, dkv):
-    if geo.n_blk != 4:
-        return lax.psum_scatter(dkv, "blk", scatter_dimension=0, tiled=False).astype(F32)
-    dma = pltpu.SemaphoreType.DMA
-    piece = dkv.shape[1:]
-    vm = pl.BlockSpec(memory_space=pltpu.VMEM)
-    return pl.pallas_call(
-        give_kernel, out_shape=jax.ShapeDtypeStruct(piece, F32), in_specs=[vm], out_specs=vm,
-        scratch_shapes=[pltpu.VMEM((2,) + piece, BF), pltpu.VMEM(piece, BF), pltpu.VMEM(piece, BF), dma((3,)), dma((3,))],
-        compiler_params=pltpu.CompilerParams(collective_id=ident, has_side_effects=True, vmem_limit_bytes=40 << 20),
-        name="give_rows")(dkv.reshape((2, 2) + piece))
 
 
 def per_device(block_input, cotangent, seq_lengths, routes_two, routes_three, query_weight, key_weight, value_weight, output_weight,
@@ -1493,10 +1537,10 @@
     geo = Geo(count, bl, n_dp, n_blk, d, gate_weight.shape[1], (None, routes_two.shape[2], routes_three.shape[2]))
     slabs = pack(geo, query_weight, key_weight, value_weight, output_weight, gate_weight, up_weight, down_weight, first_gain,
                  second_gain, router_weight)
-    ids = iter(range(10, 30))
     out, grad, shards = block(geo, block_input.reshape(count * bl, d), cotangent.reshape(count * bl, d), seq_lengths.reshape(count),
                 (routes_two.reshape(count, -1), routes_three.reshape(count, -1)), slabs,
-                lambda kv: share_rows(geo, next(ids), kv), lambda dkv: give_rows(geo, next(ids), dkv))
+                lambda kv: lax.all_gather(kv, "blk", axis=0, tiled=False),
+                              lambda dkv: lax.psum_scatter(dkv, "blk", scatter_dimension=0, tiled=False).astype(F32))
     return (out.reshape(block_input.shape), grad.reshape(block_input.shape)) + unpack(geo, shards)
 
 

time: 546 us -> 542 us (level)
    pallas_call x4 -> x2, Pallas kernels: 43.4 us -> 27.4 us  [the longest x1 17.6 us: gate_up_grads(): pl.pallas_call(body, grid=(2 * n,), out_shape=jax.ShapeDtypeStruct((dp, 2...]
    pallas_call x9 -> x7, Pallas kernels: 464 us -> 478 us  [call(): pl.pallas_call(kernel, out_shape=[jax.ShapeDtypeStruct(o.shape, o.dtype)...]
    unnamed x39 -> x31, local copies, waits for them, and re-layouts: 13.3 us -> 10.5 us
where the time goes in v5:
time: 542 us; the launch traced here: 534 us
  Pallas kernels  506 us (93%)
  local copies, waits for them, and re-layouts  19 us (4%)
  other arithmetic  8.21 us (2%)
    pallas_call x7, Pallas kernels, call(): pl.pallas_call(kernel, out_shape=[jax.ShapeDtypeStruct(o.shape, o.dtype)...  478 us
    pallas_call x1, Pallas kernels, gate_up_grads(): pl.pallas_call(body, grid=(2 * n,), out_shape=jax.ShapeDtypeStruct((dp, 2...  17.6 us

profile of v5, /device:TPU:0, one launch (start us, length us, event | category | flops | bytes accessed | tf_op | source)
XLA Modules:
  0.0 534.4 jit_solution(3707790378813542881)
XLA Ops:
  0.7 1.3 copy.71
  2.0 0.7 pad_maximum_fusion.1
  2.8 1.0 pad_maximum_fusion
  4.0 1.1 concatenate.14
  5.1 0.8 pad.25.refs_1_
  5.9 0.3 reshape.107
  6.3 0.7 pad.27.refs_2_
  7.0 1.7 constant_dynamic-slice_fusion
  8.7 0.8 reshape.109
  9.6 1.0 copy.69
  10.6 1.3 copy.55
  11.9 1.3 copy.52
  13.2 1.2 fusion.2.refs_3_
  14.4 123.1 %head.1 = (f32[2,8,768]{2,1,0:T(8,128)}, bf16[512,1024]{1,0:T(8,128)(2,1)}, bf16[4,2,256,640]{3,2,1,0:T(8,128)(2,1)}, bf16[512,1024]{1,0:T(8,128)(2,1)}, f32[512...) custom-call(f32[256,128]{1,0:T(8,128)} %get-tuple-element.235.refs_0, ...), custom_call_target="tpu_custom_call" | custom-call | tf_op jit(solution)/shard_map/head/pallas_call | solution.py:97
  137.5 37.1 %forward.2 = (bf16[512,1024]{1,0:T(8,128)(2,1)}, bf16[512,2560]{1,0:T(8,128)(2,1)}, f32[512,128]{1,0:T(8,128)}, bf16[512,2560]{1,0:T(8,128)(2,1)}, bf16[512,1024...) custom-call(f32[256,128]{1,0:T(8,128)} %get-tuple-element.235.refs_0, ...), custom_call_target="tpu_custom_call" | custom-call | tf_op jit(solution)/shard_map/forward/pallas_call | solution.py:97
  174.6 33.5 %forward.3 = (bf16[256,1024]{1,0:T(8,128)(2,1)}, bf16[256,2560]{1,0:T(8,128)(2,1)}, f32[2,8,384]{2,1,0:T(8,128)}, bf16[256,1024]{1,0:T(8,128)(2,1)}, f32[256,128...) custom-call(f32[256,128]{1,0:T(8,128)} %get-tuple-element.235.refs_0, ...), custom_call_target="tpu_custom_call" | custom-call | tf_op jit(solution)/shard_map/forward/pallas_call | solution.py:97
  208.1 47.5 %turn.1 = (bf16[128,1024]{1,0:T(8,128)(2,1)}, bf16[128,2560]{1,0:T(8,128)(2,1)}, bf16[128,2560]{1,0:T(8,128)(2,1)}, bf16[128,1024]{1,0:T(8,128)(2,1)}, f32[128,1...) custom-call(bf16[512,960]{1,0:T(8,128)(2,1)} %bitcast.40, ...), custom_call_target="tpu_custom_call" | custom-call | tf_op jit(solution)/shard_map/turn/pallas_call | solution.py:97
  255.6 2.4 copy.58
  258.1 43.6 %backward.2 = (bf16[256,1024]{1,0:T(8,128)(2,1)}, bf16[256,2560]{1,0:T(8,128)(2,1)}, bf16[256,2560]{1,0:T(8,128)(2,1)}, bf16[256,1024]{1,0:T(8,128)(2,1)}, f32[2...) custom-call(f32[512,1024]{1,0:T(8,128)} %get-tuple-element.123.refs_, ...), custom_call_target="tpu_custom_call" | custom-call | tf_op jit(solution)/shard_map/backward/pallas_call | solution.py:97
  301.7 27.7 %backward.3 = (bf16[512,1024]{1,0:T(8,128)(2,1)}, bf16[512,2560]{1,0:T(8,128)(2,1)}, bf16[512,2560]{1,0:T(8,128)(2,1)}, bf16[512,1024]{1,0:T(8,128)(2,1)}, f32[8...) custom-call(f32[512,1024]{1,0:T(8,128)} %get-tuple-element.138.refs_, ...), custom_call_target="tpu_custom_call" | custom-call | tf_op jit(solution)/shard_map/backward/pallas_call | solution.py:97
  329.4 9.8 %down_grads.1.refs_10_ = bf16[2560,1024]{1,0:T(8,128)(2,1)} custom-call(bf16[512,2560]{1,0:T(8,128)(2,1)} %get-tuple-element.157.z0, bf16[256,2560]{1,0:T(8,128)(2,1)} %get-tuple-element.158.z1, bf16[128,2560]{1,0:T(8,128)(2,1)} %get-tuple-element.159.z2, bf16[512,1024]{1,0:T(8,128)(2,1)} %get-tuple-element.160.d0, bf16[256,1024]{1,0:T(8,128)(2,1)} %get-tuple-element.161.d1, ...), custom_call_target="tpu_custom_call" | custom-call | tf_op jit(solution)/shard_map/down_grads/pallas_call | solution.py:870
  339.2 17.6 %gate_up_grads.1.refs_11_ = bf16[1024,5120]{1,0:T(8,128)(2,1)} custom-call(bf16[512,1024]{1,0:T(8,128)(2,1)} %get-tuple-element.163.w0, bf16[256,1024]{1,0:T(8,128)(2,1)} %get-tuple-element.164.w1, bf16[128,1024]{1,0:T(8,128)(2,1)} %get-tuple-element.165.w2, bf16[512,2560]{1,0:T(8,128)(2,1)} %get-tuple-element.166.g0, ...), custom_call_target="tpu_custom_call" | custom-call | tf_op jit(solution)/shard_map/gate_up_grads/pallas_call | solution.py:855
  356.8 165.9 %tail.1 = (bf16[512,1024]{1,0:T(8,128)(2,1)}, bf16[512,1664]{1,0:T(8,128)(2,1)}, bf16[4,2,256,640]{3,2,1,0:T(8,128)(2,1)}, bf16[1024,1664]{1,0:T(8,128)(2,1)}, b...) custom-call(bf16[512,1024]{1,0:T(8,128)(2,1)} %get-tuple-element.103, ...), custom_call_target="tpu_custom_call" | custom-call | tf_op jit(solution)/shard_map/tail/pallas_call | solution.py:97
  522.7 2.9 copy.59
  525.6 0.7 convert_reduce_fusion
  526.5 0.6 convert_element_type.75
  527.3 0.8 slice_convert_fusion.4
  528.1 0.7 bitcast_convert_fusion
  528.8 0.7 bitcast_convert_fusion.1
  529.6 1.0 reshape.126
  530.8 1.4 reshape.127
  532.2 1.7 slice_convert_fusion.1
  (36 shorter events, 1.2 us)
Async XLA Ops:
  0.6 5.2 copy-start.8
  3.9 4.7 copy-start.3
  8.7 1.9 copy-start.1
  9.5 2.4 copy-start.2
  10.6 2.6 copy-start.5
  10.6 2.6 copy-start.6
  522.7 2.9 copy-start.7
  525.6 3.9 copy-start.9
  527.2 3.3 copy-start.4
  530.7 1.5 copy-start

commit v6 on v5

--- a/solution.py
+++ b/solution.py
@@ -1439,7 +1439,7 @@
 AG_CHUNKS = [(0, 0, 1664, 4), (1, 0, 1024, 2), (2, 0, 2560, 4), (2, 2560, 2560, 4), (3, 0, 1024, 2)]
 RS_CHUNKS = [(2, 0, 640, 4), (3, 0, 256, 2), (2, 640, 640, 4), (2, 1280, 640, 4), (3, 256, 256, 2), (2, 1920, 640, 4),
              (2, 2560, 640, 4), (3, 512, 256, 2), (2, 3200, 640, 4), (2, 3840, 640, 4), (3, 768, 256, 2), (2, 4480, 640, 4),
-             (0, 0, 896, 4), (1, 0, 512, 2), (0, 896, 768, 4), (1, 512, 512, 2)]
+             (1, 0, 512, 2), (0, 0, 896, 4), (1, 512, 512, 2), (0, 896, 768, 4)]
 RS_CHUNKS_READY = 12 - AHEAD + 1
 
 

time: 542 us -> 539 us (level)
  no operation moved by 1% of the time
where the time goes in v6:
time: 539 us; the launch traced here: 531 us
  Pallas kernels  503 us (93%)
  local copies, waits for them, and re-layouts  19 us (4%)
  other arithmetic  8.21 us (2%)
    pallas_call x7, Pallas kernels, call(): pl.pallas_call(kernel, out_shape=[jax.ShapeDtypeStruct(o.shape, o.dtype)...  475 us
    pallas_call x1, Pallas kernels, gate_up_grads(): pl.pallas_call(body, grid=(2 * n,), out_shape=jax.ShapeDtypeStruct((dp, 2...  17.6 us

profile of v6, /device:TPU:0, one launch (start us, length us, event | category | flops | bytes accessed | tf_op | source)
XLA Modules:
  0.0 531.1 jit_solution(13395014424242813577)
XLA Ops:
  0.7 1.3 copy.71
  2.0 0.7 pad_maximum_fusion.1
  2.8 1.0 pad_maximum_fusion
  4.0 1.1 concatenate.14
  5.1 0.8 pad.25.refs_1_
  5.9 0.3 reshape.107
  6.3 0.7 pad.27.refs_2_
  7.0 1.7 constant_dynamic-slice_fusion
  8.7 0.8 reshape.109
  9.6 1.0 copy.69
  10.6 1.3 copy.55
  11.9 1.3 copy.52
  13.2 1.2 fusion.2.refs_3_
  14.4 123.1 %head.1 = (f32[2,8,768]{2,1,0:T(8,128)}, bf16[512,1024]{1,0:T(8,128)(2,1)}, bf16[4,2,256,640]{3,2,1,0:T(8,128)(2,1)}, bf16[512,1024]{1,0:T(8,128)(2,1)}, f32[512...) custom-call(f32[256,128]{1,0:T(8,128)} %get-tuple-element.235.refs_0, ...), custom_call_target="tpu_custom_call" | custom-call | tf_op jit(solution)/shard_map/head/pallas_call | solution.py:97
  137.5 37.1 %forward.2 = (bf16[512,1024]{1,0:T(8,128)(2,1)}, bf16[512,2560]{1,0:T(8,128)(2,1)}, f32[512,128]{1,0:T(8,128)}, bf16[512,2560]{1,0:T(8,128)(2,1)}, bf16[512,1024...) custom-call(f32[256,128]{1,0:T(8,128)} %get-tuple-element.235.refs_0, ...), custom_call_target="tpu_custom_call" | custom-call | tf_op jit(solution)/shard_map/forward/pallas_call | solution.py:97
  174.6 33.5 %forward.3 = (bf16[256,1024]{1,0:T(8,128)(2,1)}, bf16[256,2560]{1,0:T(8,128)(2,1)}, f32[2,8,384]{2,1,0:T(8,128)}, bf16[256,1024]{1,0:T(8,128)(2,1)}, f32[256,128...) custom-call(f32[256,128]{1,0:T(8,128)} %get-tuple-element.235.refs_0, ...), custom_call_target="tpu_custom_call" | custom-call | tf_op jit(solution)/shard_map/forward/pallas_call | solution.py:97
  208.1 47.5 %turn.1 = (bf16[128,1024]{1,0:T(8,128)(2,1)}, bf16[128,2560]{1,0:T(8,128)(2,1)}, bf16[128,2560]{1,0:T(8,128)(2,1)}, bf16[128,1024]{1,0:T(8,128)(2,1)}, f32[128,1...) custom-call(bf16[512,960]{1,0:T(8,128)(2,1)} %bitcast.40, ...), custom_call_target="tpu_custom_call" | custom-call | tf_op jit(solution)/shard_map/turn/pallas_call | solution.py:97
  255.6 2.4 copy.58
  258.1 43.6 %backward.2 = (bf16[256,1024]{1,0:T(8,128)(2,1)}, bf16[256,2560]{1,0:T(8,128)(2,1)}, bf16[256,2560]{1,0:T(8,128)(2,1)}, bf16[256,1024]{1,0:T(8,128)(2,1)}, f32[2...) custom-call(f32[512,1024]{1,0:T(8,128)} %get-tuple-element.123.refs_, ...), custom_call_target="tpu_custom_call" | custom-call | tf_op jit(solution)/shard_map/backward/pallas_call | solution.py:97
  301.7 27.7 %backward.3 = (bf16[512,1024]{1,0:T(8,128)(2,1)}, bf16[512,2560]{1,0:T(8,128)(2,1)}, bf16[512,2560]{1,0:T(8,128)(2,1)}, bf16[512,1024]{1,0:T(8,128)(2,1)}, f32[8...) custom-call(f32[512,1024]{1,0:T(8,128)} %get-tuple-element.138.refs_, ...), custom_call_target="tpu_custom_call" | custom-call | tf_op jit(solution)/shard_map/backward/pallas_call | solution.py:97
  329.4 9.8 %down_grads.1.refs_10_ = bf16[2560,1024]{1,0:T(8,128)(2,1)} custom-call(bf16[512,2560]{1,0:T(8,128)(2,1)} %get-tuple-element.157.z0, bf16[256,2560]{1,0:T(8,128)(2,1)} %get-tuple-element.158.z1, bf16[128,2560]{1,0:T(8,128)(2,1)} %get-tuple-element.159.z2, bf16[512,1024]{1,0:T(8,128)(2,1)} %get-tuple-element.160.d0, bf16[256,1024]{1,0:T(8,128)(2,1)} %get-tuple-element.161.d1, ...), custom_call_target="tpu_custom_call" | custom-call | tf_op jit(solution)/shard_map/down_grads/pallas_call | solution.py:870
  339.2 17.6 %gate_up_grads.1.refs_11_ = bf16[1024,5120]{1,0:T(8,128)(2,1)} custom-call(bf16[512,1024]{1,0:T(8,128)(2,1)} %get-tuple-element.163.w0, bf16[256,1024]{1,0:T(8,128)(2,1)} %get-tuple-element.164.w1, bf16[128,1024]{1,0:T(8,128)(2,1)} %get-tuple-element.165.w2, bf16[512,2560]{1,0:T(8,128)(2,1)} %get-tuple-element.166.g0, ...), custom_call_target="tpu_custom_call" | custom-call | tf_op jit(solution)/shard_map/gate_up_grads/pallas_call | solution.py:855
  356.8 162.6 %tail.1 = (bf16[512,1024]{1,0:T(8,128)(2,1)}, bf16[512,1664]{1,0:T(8,128)(2,1)}, bf16[4,2,256,640]{3,2,1,0:T(8,128)(2,1)}, bf16[1024,1664]{1,0:T(8,128)(2,1)}, b...) custom-call(bf16[512,1024]{1,0:T(8,128)(2,1)} %get-tuple-element.103, ...), custom_call_target="tpu_custom_call" | custom-call | tf_op jit(solution)/shard_map/tail/pallas_call | solution.py:97
  519.5 2.9 copy.59
  522.3 0.7 convert_reduce_fusion
  523.2 0.6 convert_element_type.75
  524.0 0.8 slice_convert_fusion.4
  524.8 0.7 bitcast_convert_fusion
  525.5 0.7 bitcast_convert_fusion.1
  526.3 1.0 reshape.126
  527.5 1.4 reshape.127
  528.9 1.7 slice_convert_fusion.1
  (36 shorter events, 1.2 us)
Async XLA Ops:
  0.6 5.2 copy-start.8
  3.9 4.7 copy-start.3
  8.7 1.9 copy-start.1
  9.5 2.4 copy-start.2
  10.6 2.6 copy-start.5
  10.6 2.6 copy-start.6
  519.4 2.9 copy-start.7
  522.3 3.9 copy-start.9
  524.0 3.3 copy-start.4
  527.4 1.5 copy-start
